TPU v7x, 32 devices: a whole 2x2x4 slice. The times are simulated.
32 devices in a mesh: gx: 8 (over y, x, core), yz: 4 (over z).
Axes of the slice: x: 2, y: 2, z: 4, core: 2. Of those that a mesh axis runs over, the one named last changes fastest.
Arguments:
- volume: bfloat16 [64, 16, 32, 128], P('gx', None, 'yz'), may hold values from -6 to 6
- weight_one: bfloat16 [32, 432], replicated, may hold values from -0.875 to 0.875
- weight_two: bfloat16 [64, 864], replicated, may hold values from -0.625 to 0.625
- weight_three: bfloat16 [128, 1728], replicated, may hold values from -0.21875 to 0.21875
Outputs:
- features: bfloat16 [128, 16, 256], P('yz', 'gx')
All inputs are finite; a program needn't handle non-finite values.
Results may differ from a plain program's by a relative error of at most 0.0053.
Values may be sent and summed in bfloat16 or wider, within the bound.
No kernel may reach another device: no remote copies, remote signals or barrier semaphores. Data moves between devices by JAX's collectives and lax.ppermute only.
A program may use at most 64 MiB of HBM per device.

v0:
```python
import jax
import jax.numpy as jnp
from jax import lax
from jax.sharding import PartitionSpec as P


def with_halo(block, sides, width):
    for axis, dim in sides:
        count = lax.axis_size(axis)
        forward = [(i, i + 1) for i in range(count - 1)]
        backward = [(target, source) for source, target in forward]
        low = lax.ppermute(
            lax.slice_in_dim(block, block.shape[dim] - width, None, axis=dim), axis, forward
        )
        high = lax.ppermute(lax.slice_in_dim(block, 0, width, axis=dim), axis, backward)
        block = jnp.concatenate([low, block, high], axis=dim)
    return block


def block_conv(padded, weight):
    in_rows = weight.shape[1] // 27
    kernel = weight.reshape(weight.shape[0], 3, 3, 3, in_rows)
    result = lax.conv_general_dilated(
        padded[None],
        kernel,
        (1, 1, 1),
        "VALID",
        dimension_numbers=("NDCHW", "ODHWI", "NDCHW"),
        preferred_element_type=jnp.float32,
    )
    return result[0]


def conv_pool(padded, weight):
    activated = jax.nn.relu(block_conv(padded, weight))
    planes, rows, height, breadth = activated.shape
    grouped = activated.reshape(planes // 2, 2, rows, height // 2, 2, breadth // 2, 2)
    return (jnp.sum(grouped, axis=(1, 4, 6)) * 0.125).astype(jnp.bfloat16)


def conv_planes(padded, weight):
    result = block_conv(padded, weight)
    planes, rows, height, breadth = result.shape
    return result.reshape(planes, rows, height * breadth)


def face_cells(block):
    grown = with_halo(block, (("gx", 0), ("yz", 2)), 1)
    return jnp.pad(grown, ((0, 0), (0, 0), (0, 0), (1, 1)))


def per_device(volume, weight_one, weight_two, weight_three):
    pooled_one = conv_pool(face_cells(volume), weight_one)
    pooled_two = conv_pool(face_cells(pooled_one), weight_two)
    shards = lax.axis_size("yz")
    out_rows = weight_three.shape[0] // shards
    grown = with_halo(pooled_two, (("gx", 0),), 1)
    whole = lax.all_gather(grown, "yz", axis=2, tiled=True)
    whole = jnp.pad(whole, ((0, 0), (0, 0), (1, 1), (1, 1)))
    picked = lax.dynamic_slice_in_dim(weight_three, lax.axis_index("yz") * out_rows, out_rows, 0)
    summed = jnp.moveaxis(conv_planes(whole, picked), 0, 1)
    return jax.nn.relu(summed).astype(jnp.bfloat16)


def solution(mesh):
    placed = (P("gx", None, "yz", None), P(), P(), P())
    return jax.shard_map(
        per_device, mesh=mesh, in_specs=placed, out_specs=P("yz", "gx", None), check_vma=False
    )
```

profile of v0, /device:TPU:4, one launch (start us, length us, event | category | flops | bytes accessed | tf_op | source)
XLA Modules:
  0.0 97.5 jit_solution(7059281720104508196)
XLA Ops:
  0.8 1.9 %collective-permute-start = (bf16[1,16,8,128]{3,2,1,0:T(8,128)(2,1)S(1)}, bf16[1,16,8,128]{3,2,1,0:T(8,128)(2,1)S(1)}, u32[]{:S(2)}, u32[]{:S(2)}) collective-permute-start(bf16[1,16,8,128]{3,2,1,0:T(8,128)(2,1)S(1)} %get-tuple-element.12), channel_id=1, source_target_pairs={{0,4},{4,8},{8,12},{12,16},{16,20},{20,24},{24,28},{1,5},{5,9},{9,... | collective-permute-start | bytes 98312 | tf_op jit(solution)/shard_map/ppermute | solution.py:12
  2.8 4.5 %collective-permute-start.1 = (bf16[1,16,8,128]{3,2,1,0:T(8,128)(2,1)S(1)}, bf16[1,16,8,128]{3,2,1,0:T(8,128)(2,1)S(1)}, u32[]{:S(2)}, u32[]{:S(2)}) collective-permute-start(bf16[1,16,8,128]{3,2,1,0:T(8,128)(2,1)S(1)} %get-tuple-element.11), channel_id=1, source_target_pairs={{4,0},{8,4},{12,8},{16,12},{20,16},{24,20},{28,24},{5,1},{9,5},{13... | collective-permute-start | bytes 98312 | tf_op jit(solution)/shard_map/ppermute | solution.py:15
  9.0 3.5 %collective-permute-start.2 = (bf16[10,16,1,128]{3,2,1,0:T(2,128)(2,1)S(1)}, bf16[10,16,1,128]{3,2,1,0:T(2,128)(2,1)S(1)}, u32[]{:S(2)}, u32[]{:S(2)}) collective-permute-start(bf16[10,16,1,128]{3,2,1,0:T(2,128)(2,1)S(1)} %get-tuple-element.7), channel_id=1, source_target_pairs={{0,1},{1,2},{2,3},{4,5},{5,6},{6,7},{8,9},{9,10},{10,11},{12,13},{... | collective-permute-start | bytes 122888 | tf_op jit(solution)/shard_map/ppermute | solution.py:12
  12.5 1.3 %collective-permute-start.3 = (bf16[10,16,1,128]{3,2,1,0:T(2,128)(2,1)S(1)}, bf16[10,16,1,128]{3,2,1,0:T(2,128)(2,1)S(1)}, u32[]{:S(2)}, u32[]{:S(2)}) collective-permute-start(bf16[10,16,1,128]{3,2,1,0:T(2,128)(2,1)S(1)} %get-tuple-element.8), channel_id=1, source_target_pairs={{1,0},{2,1},{3,2},{5,4},{6,5},{7,6},{9,8},{10,9},{11,10},{13,12},{... | collective-permute-start | bytes 122888 | tf_op jit(solution)/shard_map/ppermute | solution.py:15
  15.0 4.1 %collective-permute-done.3 = bf16[10,16,1,128]{3,2,1,0:T(2,128)(2,1)S(1)} collective-permute-done((bf16[10,16,1,128]{3,2,1,0:T(2,128)(2,1)S(1)}, bf16[10,16,1,128]{3,2,1,0:T(2,128)(2,1)S(1)}, u32[]{:S(2)}, u32[]{:S(2)}) %collective-permute-start.3) | collective-permute-done | bytes 40992 | tf_op jit(solution)/shard_map/ppermute | solution.py:15
  19.2 1.2 %fusion.18 = bf16[10,16,10,1,130]{4,2,1,0,3:T(8,128)(2,1)S(1)} fusion(bf16[10,16,1,128]{3,2,1,0:T(2,128)(2,1)S(1)} %collective-permute-done.3, bf16[10,16,8,128]{3,2,1,0:T(8,128)(2,1)S(1)} %constant_dynamic-update-slice_fusion, bf16[10,16,1,128]{3,2,1,0:T(2,128)(2,1)S(1)} %collective-permute-done.2), kind=kLoop, calls=%fused_computation.20 | loop fusion | flops 2496000 | bytes 825600 | tf_op jit(solution)/shard_map/broadcast_in_dim | solution.py:24
  20.7 3.7 %reshape.59 = bf16[10,16,10,1,8,17]{5,4,2,1,0,3:T(8,128)(2,1)} reshape(bf16[10,16,10,1,136]{4,2,1,0,3:T(8,128)(2,1)S(1)} %pad.15) | data formatting | bytes 870400 | tf_op jit(solution)/shard_map/conv_general_dilated | solution.py:23
  24.4 7.9 %copy.58 = bf16[10,16,10,1,8,17]{1,4,5,2,0,3:T(8,128)(2,1)} copy(bf16[10,16,10,1,8,17]{5,4,2,1,0,3:T(8,128)(2,1)} %reshape.59) | data formatting | bytes 870400 | tf_op jit(solution)/shard_map/conv_general_dilated | solution.py:23
  32.3 1.1 %slice.48 = bf16[10,16,10,1,7,2]{1,4,5,2,0,3:T(8,128)(2,1)S(1)} slice(bf16[10,16,10,1,8,17]{1,4,5,2,0,3:T(8,128)(2,1)} %copy.58), slice={[0:10], [0:16], [0:10], [0:1], [1:8], [0:2]} | slice | bytes 89600 | tf_op jit(solution)/shard_map/conv_general_dilated | solution.py:23
  33.5 7.3 %select_maximum_fusion = f32[8,8,8,17,32]{4,2,3,1,0:T(8,128)S(1)} fusion(pred[8,17]{0,1:T(8,128)(4,1)S(1)} %copy-done.2, bf16[32,3,3,3,16]{0,4,3,2,1:T(8,128)(2,1)S(1)} %bitcast.51, bf16[10,16,10,1,7,2]{1,4,5,2,0,3:T(8,128)(2,1)S(1)} %slice.48, bf16[10,16,10,1,8,17]{1,4,5,2,0,3:T(8,128)(2,1)} %copy.58), kind=kOutput, calls=%fused_computation.2 | convolution fusion | flops 242664448 | bytes 1621896 | tf_op jit(solution)/shard_map/conv_general_dilated | solution.py:23
  41.5 2.2 %slice.49 = f32[8,8,1,128,32]{4,1,3,0,2:T(8,128)} slice(f32[8,8,1,136,32]{4,1,3,0,2:T(8,128)S(1)} %bitcast.41), slice={[0:8], [0:8], [0:1], [0:128], [0:32]} | slice | bytes 2097152 | tf_op jit(solution)/shard_map/jit(relu)/max | solution.py:35
  43.8 5.0 %reduce_sum.18 = f32[4,32,4,64]{1,2,3,0:T(4,128)S(1)} reduce(f32[4,2,32,4,2,64,2]{2,4,3,6,5,1,0:T(2,128)} %bitcast.42, f32[]{:T(128)} %constant.8.clone.1), dimensions={1,4,6}, to_apply=%region_0.1 | reduce | flops 229376 | bytes 1179652 | tf_op jit(solution)/shard_map/reduce_sum | solution.py:38
  49.0 1.9 %collective-permute-start.4 = (bf16[1,32,4,64]{1,2,3,0:T(4,128)(2,1)S(1)}, bf16[1,32,4,64]{1,2,3,0:T(4,128)(2,1)S(1)}, u32[]{:S(2)}, u32[]{:S(2)}) collective-permute-start(bf16[1,32,4,64]{1,2,3,0:T(4,128)(2,1)S(1)} %get-tuple-element.9), channel_id=1, source_target_pairs={{0,4},{4,8},{8,12},{12,16},{16,20},{20,24},{24,28},{1,5},{5,9},{9,... | collective-permute-start | bytes 49160 | tf_op jit(solution)/shard_map/ppermute | solution.py:12
  50.9 4.5 %collective-permute-start.5 = (bf16[1,32,4,64]{1,2,3,0:T(4,128)(2,1)S(1)}, bf16[1,32,4,64]{1,2,3,0:T(4,128)(2,1)S(1)}, u32[]{:S(2)}, u32[]{:S(2)}) collective-permute-start(bf16[1,32,4,64]{1,2,3,0:T(4,128)(2,1)S(1)} %get-tuple-element.10), channel_id=1, source_target_pairs={{4,0},{8,4},{12,8},{16,12},{20,16},{24,20},{28,24},{5,1},{9,5},{13... | collective-permute-start | bytes 49160 | tf_op jit(solution)/shard_map/ppermute | solution.py:15
  55.5 1.9 %collective-permute-done.5 = bf16[1,32,4,64]{1,2,3,0:T(4,128)(2,1)S(1)} collective-permute-done((bf16[1,32,4,64]{1,2,3,0:T(4,128)(2,1)S(1)}, bf16[1,32,4,64]{1,2,3,0:T(4,128)(2,1)S(1)}, u32[]{:S(2)}, u32[]{:S(2)}) %collective-permute-start.5) | collective-permute-done | bytes 16416 | tf_op jit(solution)/shard_map/ppermute | solution.py:15
  58.0 3.7 %collective-permute-start.6 = (bf16[6,32,1,64]{1,2,3,0:T(2,128)(2,1)S(1)}, bf16[6,32,1,64]{1,2,3,0:T(2,128)(2,1)S(1)}, u32[]{:S(2)}, u32[]{:S(2)}) collective-permute-start(bf16[6,32,1,64]{1,2,3,0:T(2,128)(2,1)S(1)} %get-tuple-element.5), channel_id=1, source_target_pairs={{0,1},{1,2},{2,3},{4,5},{5,6},{6,7},{8,9},{9,10},{10,11},{12,13},{... | collective-permute-start | bytes 73736 | tf_op jit(solution)/shard_map/ppermute | solution.py:12
  61.7 1.3 %collective-permute-start.7 = (bf16[6,32,1,64]{1,2,3,0:T(2,128)(2,1)S(1)}, bf16[6,32,1,64]{1,2,3,0:T(2,128)(2,1)S(1)}, u32[]{:S(2)}, u32[]{:S(2)}) collective-permute-start(bf16[6,32,1,64]{1,2,3,0:T(2,128)(2,1)S(1)} %get-tuple-element.6), channel_id=1, source_target_pairs={{1,0},{2,1},{3,2},{5,4},{6,5},{7,6},{9,8},{10,9},{11,10},{13,12},{... | collective-permute-start | bytes 73736 | tf_op jit(solution)/shard_map/ppermute | solution.py:15
  63.4 2.1 %collective-permute-done.6 = bf16[6,32,1,64]{1,2,3,0:T(2,128)(2,1)S(1)} collective-permute-done((bf16[6,32,1,64]{1,2,3,0:T(2,128)(2,1)S(1)}, bf16[6,32,1,64]{1,2,3,0:T(2,128)(2,1)S(1)}, u32[]{:S(2)}, u32[]{:S(2)}) %collective-permute-start.6) | collective-permute-done | bytes 24608 | tf_op jit(solution)/shard_map/ppermute | solution.py:12
  65.6 4.0 %collective-permute-done.7 = bf16[6,32,1,64]{1,2,3,0:T(2,128)(2,1)S(1)} collective-permute-done((bf16[6,32,1,64]{1,2,3,0:T(2,128)(2,1)S(1)}, bf16[6,32,1,64]{1,2,3,0:T(2,128)(2,1)S(1)}, u32[]{:S(2)}, u32[]{:S(2)}) %collective-permute-start.7) | collective-permute-done | bytes 24608 | tf_op jit(solution)/shard_map/ppermute | solution.py:15
  70.8 1.4 %fusion.19 = f32[4,4,8,9,64]{4,2,3,1,0:T(8,128)S(1)} fusion(bf16[64,3,3,3,32]{0,4,3,2,1:T(8,128)(2,1)S(1)} %bitcast.49, bf16[6,32,6,1,7,2]{1,4,5,2,0,3:T(8,128)(2,1)S(1)} %slice.54, bf16[6,32,6,1,8,9]{1,4,5,2,0,3:T(8,128)(2,1)S(1)} %copy.66, pred[8,9]{0,1:T(8,128)(4,1)S(1)} %copy-done.3), kind=kOutput, calls=%fused_computation.22 | convolution fusion | flops 128157696 | bytes 603720 | tf_op jit(solution)/shard_map/conv_general_dilated | solution.py:23
  73.0 1.9 %collective-permute-start.8 = (bf16[1,64,2,32]{1,2,3,0:T(2,128)(2,1)S(1)}, bf16[1,64,2,32]{1,2,3,0:T(2,128)(2,1)S(1)}, u32[]{:S(2)}, u32[]{:S(2)}) collective-permute-start(bf16[1,64,2,32]{1,2,3,0:T(2,128)(2,1)S(1)} %get-tuple-element.13), channel_id=1, source_target_pairs={{0,4},{4,8},{8,12},{12,16},{16,20},{20,24},{24,28},{1,5},{5,9},{9,... | collective-permute-start | bytes 24584 | tf_op jit(solution)/shard_map/ppermute | solution.py:12
  74.9 4.5 %collective-permute-start.9 = (bf16[1,64,2,32]{1,2,3,0:T(2,128)(2,1)S(1)}, bf16[1,64,2,32]{1,2,3,0:T(2,128)(2,1)S(1)}, u32[]{:S(2)}, u32[]{:S(2)}) collective-permute-start(bf16[1,64,2,32]{1,2,3,0:T(2,128)(2,1)S(1)} %get-tuple-element.14), channel_id=1, source_target_pairs={{4,0},{8,4},{12,8},{16,12},{20,16},{24,20},{28,24},{5,1},{9,5},{13... | collective-permute-start | bytes 24584 | tf_op jit(solution)/shard_map/ppermute | solution.py:15
  79.6 1.2 %collective-permute-done.9 = bf16[1,64,2,32]{1,2,3,0:T(2,128)(2,1)S(1)} collective-permute-done((bf16[1,64,2,32]{1,2,3,0:T(2,128)(2,1)S(1)}, bf16[1,64,2,32]{1,2,3,0:T(2,128)(2,1)S(1)}, u32[]{:S(2)}, u32[]{:S(2)}) %collective-permute-start.9) | collective-permute-done | bytes 8224 | tf_op jit(solution)/shard_map/ppermute | solution.py:15
  81.0 14.1 %all_gather.3 = bf16[4,64,8,32]{1,3,0,2:T(8,128)(2,1)S(1)} all-gather(bf16[4,64,2,32]{1,3,0,2:T(8,128)(2,1)S(1)} %copy.69), channel_id=1, replica_groups=mesh['gx'=8,'yz'=4] {'yz'}, dimensions={2}, use_global_device_ids=true | all-gather | bytes 163840 | tf_op jit(solution)/shard_map/all_gather | solution.py:58
  (55 shorter events, 10.7 us)
Async XLA Ops:
  0.0 79.4 %copy-start = (bf16[128,1728]{0,1:T(8,128)(2,1)S(1)}, bf16[128,1728]{0,1:T(8,128)(2,1)}, u32[]{:S(2)}) copy-start(bf16[128,1728]{0,1:T(8,128)(2,1)} %param.7) | copy-start | bytes 1327108
  0.8 6.5 %collective-permute-start = (bf16[1,16,8,128]{3,2,1,0:T(8,128)(2,1)S(1)}, bf16[1,16,8,128]{3,2,1,0:T(8,128)(2,1)S(1)}, u32[]{:S(2)}, u32[]{:S(2)}) collective-permute-start(bf16[1,16,8,128]{3,2,1,0:T(8,128)(2,1)S(1)} %get-tuple-element.12), channel_id=1, source_target_pairs={{0,4},{4,8},{8,12},{12,16},{16,20},{20,24},{24,28},{1,5},{5,9},{9,... | collective-permute-start | bytes 98312 | tf_op jit(solution)/shard_map/ppermute | solution.py:12
  2.8 6.1 %collective-permute-start.1 = (bf16[1,16,8,128]{3,2,1,0:T(8,128)(2,1)S(1)}, bf16[1,16,8,128]{3,2,1,0:T(8,128)(2,1)S(1)}, u32[]{:S(2)}, u32[]{:S(2)}) collective-permute-start(bf16[1,16,8,128]{3,2,1,0:T(8,128)(2,1)S(1)} %get-tuple-element.11), channel_id=1, source_target_pairs={{4,0},{8,4},{12,8},{16,12},{20,16},{24,20},{28,24},{5,1},{9,5},{13... | collective-permute-start | bytes 98312 | tf_op jit(solution)/shard_map/ppermute | solution.py:15
  9.0 6.0 %collective-permute-start.2 = (bf16[10,16,1,128]{3,2,1,0:T(2,128)(2,1)S(1)}, bf16[10,16,1,128]{3,2,1,0:T(2,128)(2,1)S(1)}, u32[]{:S(2)}, u32[]{:S(2)}) collective-permute-start(bf16[10,16,1,128]{3,2,1,0:T(2,128)(2,1)S(1)} %get-tuple-element.7), channel_id=1, source_target_pairs={{0,1},{1,2},{2,3},{4,5},{5,6},{6,7},{8,9},{9,10},{10,11},{12,13},{... | collective-permute-start | bytes 122888 | tf_op jit(solution)/shard_map/ppermute | solution.py:12
  12.5 6.7 %collective-permute-start.3 = (bf16[10,16,1,128]{3,2,1,0:T(2,128)(2,1)S(1)}, bf16[10,16,1,128]{3,2,1,0:T(2,128)(2,1)S(1)}, u32[]{:S(2)}, u32[]{:S(2)}) collective-permute-start(bf16[10,16,1,128]{3,2,1,0:T(2,128)(2,1)S(1)} %get-tuple-element.8), channel_id=1, source_target_pairs={{1,0},{2,1},{3,2},{5,4},{6,5},{7,6},{9,8},{10,9},{11,10},{13,12},{... | collective-permute-start | bytes 122888 | tf_op jit(solution)/shard_map/ppermute | solution.py:15
  24.4 9.0 %copy-start.2 = (pred[8,17]{0,1:T(8,128)(4,1)S(1)}, pred[8,17]{0,1:T(8,128)(4,1)}, u32[]{:S(2)}) copy-start(pred[8,17]{0,1:T(8,128)(4,1)} %constant.43) | copy-start | bytes 412
  43.8 19.2 %copy-start.1 = (bf16[64,864]{1,0:T(8,128)(2,1)S(1)}, bf16[64,864]{1,0:T(8,128)(2,1)}, u32[]{:S(2)}) copy-start(bf16[64,864]{1,0:T(8,128)(2,1)} %param.6) | copy-start | bytes 331780
  49.0 6.5 %collective-permute-start.4 = (bf16[1,32,4,64]{1,2,3,0:T(4,128)(2,1)S(1)}, bf16[1,32,4,64]{1,2,3,0:T(4,128)(2,1)S(1)}, u32[]{:S(2)}, u32[]{:S(2)}) collective-permute-start(bf16[1,32,4,64]{1,2,3,0:T(4,128)(2,1)S(1)} %get-tuple-element.9), channel_id=1, source_target_pairs={{0,4},{4,8},{8,12},{12,16},{16,20},{20,24},{24,28},{1,5},{5,9},{9,... | collective-permute-start | bytes 49160 | tf_op jit(solution)/shard_map/ppermute | solution.py:12
  50.9 6.4 %collective-permute-start.5 = (bf16[1,32,4,64]{1,2,3,0:T(4,128)(2,1)S(1)}, bf16[1,32,4,64]{1,2,3,0:T(4,128)(2,1)S(1)}, u32[]{:S(2)}, u32[]{:S(2)}) collective-permute-start(bf16[1,32,4,64]{1,2,3,0:T(4,128)(2,1)S(1)} %get-tuple-element.10), channel_id=1, source_target_pairs={{4,0},{8,4},{12,8},{16,12},{20,16},{24,20},{28,24},{5,1},{9,5},{13... | collective-permute-start | bytes 49160 | tf_op jit(solution)/shard_map/ppermute | solution.py:15
  58.0 7.5 %collective-permute-start.6 = (bf16[6,32,1,64]{1,2,3,0:T(2,128)(2,1)S(1)}, bf16[6,32,1,64]{1,2,3,0:T(2,128)(2,1)S(1)}, u32[]{:S(2)}, u32[]{:S(2)}) collective-permute-start(bf16[6,32,1,64]{1,2,3,0:T(2,128)(2,1)S(1)} %get-tuple-element.5), channel_id=1, source_target_pairs={{0,1},{1,2},{2,3},{4,5},{5,6},{6,7},{8,9},{9,10},{10,11},{12,13},{... | collective-permute-start | bytes 73736 | tf_op jit(solution)/shard_map/ppermute | solution.py:12
  61.7 7.9 %collective-permute-start.7 = (bf16[6,32,1,64]{1,2,3,0:T(2,128)(2,1)S(1)}, bf16[6,32,1,64]{1,2,3,0:T(2,128)(2,1)S(1)}, u32[]{:S(2)}, u32[]{:S(2)}) collective-permute-start(bf16[6,32,1,64]{1,2,3,0:T(2,128)(2,1)S(1)} %get-tuple-element.6), channel_id=1, source_target_pairs={{1,0},{2,1},{3,2},{5,4},{6,5},{7,6},{9,8},{10,9},{11,10},{13,12},{... | collective-permute-start | bytes 73736 | tf_op jit(solution)/shard_map/ppermute | solution.py:15
  69.7 1.1 %copy-start.3 = (pred[8,9]{0,1:T(8,128)(4,1)S(1)}, pred[8,9]{0,1:T(8,128)(4,1)}, u32[]{:S(2)}) copy-start(pred[8,9]{0,1:T(8,128)(4,1)} %constant.42) | copy-start | bytes 220
  72.9 22.8 %copy-start.4 = (pred[8,5]{0,1:T(8,128)(4,1)S(1)}, pred[8,5]{0,1:T(8,128)(4,1)}, u32[]{:S(2)}) copy-start(pred[8,5]{0,1:T(8,128)(4,1)} %constant.41) | copy-start | bytes 124
  73.0 6.7 %collective-permute-start.8 = (bf16[1,64,2,32]{1,2,3,0:T(2,128)(2,1)S(1)}, bf16[1,64,2,32]{1,2,3,0:T(2,128)(2,1)S(1)}, u32[]{:S(2)}, u32[]{:S(2)}) collective-permute-start(bf16[1,64,2,32]{1,2,3,0:T(2,128)(2,1)S(1)} %get-tuple-element.13), channel_id=1, source_target_pairs={{0,4},{4,8},{8,12},{12,16},{16,20},{20,24},{24,28},{1,5},{5,9},{9,... | collective-permute-start | bytes 24584 | tf_op jit(solution)/shard_map/ppermute | solution.py:12
  74.9 6.0 %collective-permute-start.9 = (bf16[1,64,2,32]{1,2,3,0:T(2,128)(2,1)S(1)}, bf16[1,64,2,32]{1,2,3,0:T(2,128)(2,1)S(1)}, u32[]{:S(2)}, u32[]{:S(2)}) collective-permute-start(bf16[1,64,2,32]{1,2,3,0:T(2,128)(2,1)S(1)} %get-tuple-element.14), channel_id=1, source_target_pairs={{4,0},{8,4},{12,8},{16,12},{20,16},{24,20},{28,24},{5,1},{9,5},{13... | collective-permute-start | bytes 24584 | tf_op jit(solution)/shard_map/ppermute | solution.py:15
where the time goes:
time: 98.2 us; the launch traced here: 97.5 us
  starting transfers between devices  29.1 us (30%)
  local copies, waits for them, and re-layouts  22.7 us (23%)
  waiting for transfers between devices  14.2 us (14%)
  blocking collectives  14.1 us (14%)
  matrix products  9.47 us (10%)
  other arithmetic  7.46 us (8%)
    ppermute x5, starting transfers between devices, with_halo(): lax.ppermute(lax.slice_in_dim(block, 0, width, axis=dim), axis, backward)  16.2 us
    all_gather x1, blocking collectives, per_device(): whole = lax.all_gather(grown, 'yz', axis=2, tiled=True)  14.1 us
    conv_general_dilated x7, local copies, waits for them, and re-layouts, block_conv(): lax.conv_general_dilated(padded[None], kernel, (1, 1, 1), 'VALID', dimens...  13 us
    ppermute x5, starting transfers between devices, with_halo(): lax.ppermute(lax.slice_in_dim(block, block.shape[dim] - width, None, axis...  12.9 us
    ppermute x5, waiting for transfers between devices, with_halo(): lax.ppermute(lax.slice_in_dim(block, 0, width, axis=dim), axis, backward)  11.8 us
    conv_general_dilated x3, matrix products, block_conv(): lax.conv_general_dilated(padded[None], kernel, (1, 1, 1), 'VALID', dimens...  9.47 us
    reduce_sum x2, other arithmetic, conv_pool(): return (jnp.sum(grouped, axis=(1, 4, 6)) * 0.125).astype(jnp.bfloat16)  5.47 us
    max x4, local copies, waits for them, and re-layouts, conv_pool(): activated = jax.nn.relu(block_conv(padded, weight))  3.2 us
  transfers between devices with their start and end apart: 10, of which 7 were waited for; matrix products, arithmetic and copies ran while one was open for 3% of the time, Pallas kernels for 0%

commit v1 on v0

v1 whole, which is shorter than its diff:
```python
import functools

import jax
import jax.numpy as jnp
import numpy as np
from jax import lax
from jax.experimental import pallas as pl
from jax.experimental.pallas import tpu as pltpu
from jax.sharding import PartitionSpec as P

BF = jnp.bfloat16
F32 = jnp.float32
WHOLE = pl.BlockSpec(memory_space=pltpu.VMEM)
HALO = 3


def mat(a, b):
    return jnp.dot(a, b, preferred_element_type=F32)


def relu(a):
    return jnp.maximum(a, 0.0)


def iota(shape, dim):
    return lax.broadcasted_iota(jnp.int32, shape, dim)


def call(body, outs, *args, scratch=(), flops=0, name=None):
    moved = sum(a.size * a.dtype.itemsize for a in args)
    return pl.pallas_call(
        body,
        out_shape=[jax.ShapeDtypeStruct(s, d) for s, d in outs],
        in_specs=[WHOLE] * len(args),
        out_specs=[WHOLE] * len(outs),
        scratch_shapes=list(scratch),
        compiler_params=pltpu.CompilerParams(vmem_limit_bytes=40 * 1024 * 1024),
        cost_estimate=pl.CostEstimate(flops=flops, bytes_accessed=moved, transcendentals=0),
        name=name,
    )(*args)


def turn_kernel(vol, turned, send_a, send_b):
    planes, chans, height, breadth = vol.shape
    rows = chans * height
    dest = iota((rows, rows), 0)
    source = (dest & (chans - 1)) * height + dest // chans
    swap = (iota((rows, rows), 1) == source).astype(F32).astype(BF)
    even = lax.rem(lax.axis_index("yz"), 2) == 0
    edge = HALO * chans
    for x in range(planes):
        t = mat(swap, vol[x].reshape(rows, breadth)).astype(BF)
        turned[x] = t
        low, high = t[:edge], t[rows - edge :]
        send_a[x] = jnp.where(even, high, low)
        send_b[x] = jnp.where(even, low, high)


def yz_pairs(gx, yz, second):
    pairs = []
    for g in range(gx):
        for k in range(yz):
            if not second:
                pairs.append((g * yz + k, g * yz + (k ^ 1)))
            elif k in (0, yz - 1):
                pairs.append((g * yz + k, (g ^ 1) * yz + k))
            else:
                pairs.append((g * yz + k, g * yz + (k + 1 if k % 2 else k - 1)))
    return pairs


def ring(x, step):
    count = lax.axis_size("gx")
    return lax.ppermute(x, "gx", [(i, (i + step) % count) for i in range(count)])


def y_sides(got_a, got_b, x):
    k = lax.axis_index("yz")
    last = lax.axis_size("yz") - 1
    even = lax.rem(k, 2) == 0
    a, b = got_a[x], got_b[x]
    zero = jnp.zeros_like(a)
    low = jnp.where(k == 0, zero, jnp.where(even, b, a))
    high = jnp.where(k == last, zero, jnp.where(even, a, b))
    return low, high


def extend_kernel(turned, got_a, got_b, send_low, send_high):
    planes, rows, _ = turned.shape
    edge = got_a.shape[1]
    for out, first in ((send_low, 0), (send_high, planes - HALO)):
        for x in range(HALO):
            low, high = y_sides(got_a, got_b, first + x)
            out[x, :edge] = low
            out[x, edge : edge + rows] = turned[first + x]
            out[x, edge + rows :] = high


def weights_kernel(w1, w2, src1, src2, band1, band2, z_sel, p_sel):
    def spread(w, src, chans):
        sel = (iota((w.shape[1], src.shape[1]), 0) == src[...]).astype(F32).astype(BF)
        return mat(w[...], sel)

    for w, src, band, chans in ((w1, src1, band1, 16), (w2, src2, band2, 32)):
        base = spread(w, src, chans)
        out_rows, columns = base.shape
        wide = -(-columns // 128) * 128
        base = jnp.pad(base, ((0, 0), (0, wide - columns)))
        for y in range(4):
            moved = base if y == 0 else pltpu.roll(base, y * chans, 1)
            band[out_rows * y : out_rows * (y + 1)] = moved[:, :columns].astype(BF)

    rows, columns = z_sel.shape
    breadth = rows // 2
    r, c = iota(z_sel.shape, 0), iota(z_sel.shape, 1)
    tap = c // breadth
    within = c - tap * breadth
    same = (r // breadth) == (within // (breadth // 2))
    cell = (r & (breadth - 1)) // 2 == (within & (breadth // 2 - 1)) + tap - 1
    z_sel[...] = jnp.where(same & cell, 0.125, 0.0).astype(BF)

    rows, columns = p_sel.shape
    z = rows // 8
    r, c = iota(p_sel.shape, 0), iota(p_sel.shape, 1)
    hit = (r // (4 * z) == (c // (z // 2)) % 2) & ((r // (2 * z)) % 2 == c // z)
    hit = hit & ((r & (z - 1)) // 2 == (c & (z // 2 - 1)))
    p_sel[...] = jnp.where(hit, 0.125, 0.0).astype(BF)


def band_sources(chans):
    out = []
    for a in range(3):
        for c in range(3):
            for y in range(6):
                for i in range(chans):
                    out.append(((3 * a + y) * 3 + c) * chans + i if y < 3 else -1)
    return np.asarray(out, np.int32)[None]


def convs_kernel(turned, got_a, got_b, got_low, got_high, band1, band2, z_sel, p_sel, out, taps, pooled, taps2):
    planes, rows, breadth = turned.shape
    edge = got_a.shape[1]
    chans = edge // HALO
    window = 6 * chans
    lane = iota((1, breadth), 1)
    g, k = lax.axis_index("gx"), lax.axis_index("yz")
    g_last, k_last = lax.axis_size("gx") - 1, lax.axis_size("yz") - 1

    def put(e, t):
        wide = t.astype(F32)
        before = jnp.where(lane == 0, 0.0, pltpu.roll(wide, 1, 1)).astype(BF)
        after = jnp.where(lane == breadth - 1, 0.0, pltpu.roll(wide, breadth - 1, 1)).astype(BF)
        for tap, value in enumerate((before, t, after)):
            for part in range(3):
                first = part * 4 * chans
                taps[part, e, tap * window : (tap + 1) * window] = value[first : first + window]

    for x in range(HALO):
        t = got_low[x]
        put(x, jnp.where(g == 0, jnp.zeros_like(t), t))
        t = got_high[x]
        put(HALO + planes + x, jnp.where(g == g_last, jnp.zeros_like(t), t))
    for x in range(planes):
        low, high = y_sides(got_a, got_b, x)
        put(HALO + x, jnp.concatenate([low, turned[x], high], 0))

    pairs = pooled.shape[0]
    w1 = band1[...]
    width = w1.shape[0] // 4
    for j in range(pairs):
        for part in range(3):
            left = taps[part, 2 * j : 2 * j + 3].reshape(-1, breadth)
            right = taps[part, 2 * j + 1 : 2 * j + 4].reshape(-1, breadth)
            r = relu(mat(w1, jnp.concatenate([left, right], 1)))
            s = r[:, :breadth] + r[:, breadth:]
            lower = s[:width] + s[width : 2 * width]
            upper = s[2 * width : 3 * width] + s[3 * width :]
            if part == 0:
                lower = jnp.where(k == 0, 0.0, lower)
            if part == 2:
                upper = jnp.where(k == k_last, 0.0, upper)
            if j == 0:
                lower, upper = jnp.where(g == 0, 0.0, lower), jnp.where(g == 0, 0.0, upper)
            if j == pairs - 1:
                lower, upper = jnp.where(g == g_last, 0.0, lower), jnp.where(g == g_last, 0.0, upper)
            first = 2 * part * width
            pooled[j, first : first + width] = lower.astype(BF)
            pooled[j, first + width : first + 2 * width] = upper.astype(BF)

    window2 = pooled.shape[1]
    for j in range(pairs - 1):
        q = mat(jnp.concatenate([pooled[j], pooled[j + 1]], 1), z_sel[...]).astype(BF)
        for tap in range(3):
            taps2[j, tap * window2 : (tap + 1) * window2] = q[:, tap * breadth : (tap + 1) * breadth]
    left = taps2[0:3].reshape(-1, breadth)
    right = taps2[2:5].reshape(-1, breadth)
    r = relu(mat(band2[...], jnp.concatenate([left, right], 1)))
    width = r.shape[0] // 4
    lower = (r[:width] + r[width : 2 * width]).astype(BF)
    upper = (r[2 * width : 3 * width] + r[3 * width :]).astype(BF)
    out[...] = mat(jnp.concatenate([lower, upper], 1), p_sel[...]).astype(BF)


def lay_kernel(*refs):
    tiles, (low, high) = refs[:-2], refs[-2:]
    k = lax.axis_index("yz")
    even = lax.rem(k, 2) == 0
    half = tiles[0].shape[1] // 2
    lane = iota((1, 2 * half), 1)
    for m in range(len(tiles) // 2):
        a, b = tiles[2 * m][...].astype(F32), tiles[2 * m + 1][...].astype(F32)
        first, second = jnp.where(even, a, b), jnp.where(even, b, a)
        place = pl.ds(pl.multiple_of((lax.div(k, 2) ^ m) * 2 * half, 2 * half), 2 * half)
        low[:, place] = jnp.where(lane < half, first, pltpu.roll(second, half, 1)).astype(BF)
        high[:, place] = jnp.where(lane < half, pltpu.roll(first, half, 1), second).astype(BF)


def last_kernel(z, low, high, before, after, w3, out, taps):
    chans, cells = low.shape
    g = lax.axis_index("gx")
    g_last = lax.axis_size("gx") - 1
    lane = iota((1, cells), 1)
    depth = lane & (z - 1)
    for x, ref in enumerate((before, low, high, after)):
        t = ref[...].astype(F32)
        if x == 0:
            t = jnp.where(g == 0, 0.0, t)
        if x == 3:
            t = jnp.where(g == g_last, 0.0, t)
        for b in range(3):
            for c in range(3):
                step = (b - 1) * z + c - 1
                moved = t if step == 0 else pltpu.roll(t, (-step) % cells, 1)
                inside = (lane + step >= 0) & (lane + step < cells)
                inside = inside & (depth + (c - 1) >= 0) & (depth + (c - 1) < z)
                row = (3 * b + c) * chans
                taps[x, row : row + chans] = jnp.where(inside, moved, 0.0).astype(BF)
    w = w3[...]
    for x in range(2):
        acc = mat(w, taps[x : x + 3].reshape(-1, cells))
        out[:, x * cells : (x + 1) * cells] = relu(acc).astype(BF)


def per_device(volume, weight_one, weight_two, weight_three):
    gx, yz = lax.axis_size("gx"), lax.axis_size("yz")
    planes, chans, height, breadth = volume.shape
    rows = chans * height
    edge = HALO * chans
    c2, c3 = weight_one.shape[0], weight_two.shape[0]

    turned, send_a, send_b = call(
        turn_kernel,
        [((planes, rows, breadth), BF), ((planes, edge, breadth), BF), ((planes, edge, breadth), BF)],
        volume,
    )
    got_a = lax.ppermute(send_a, ("gx", "yz"), yz_pairs(gx, yz, False))
    got_b = lax.ppermute(send_b, ("gx", "yz"), yz_pairs(gx, yz, True))
    k1, k2 = 54 * chans, 54 * c2
    band1, band2, z_sel, p_sel = call(
        weights_kernel,
        [((4 * c2, k1), BF), ((4 * c3, k2), BF), ((2 * breadth, 3 * breadth), BF), ((4 * breadth, breadth), BF)],
        weight_one,
        weight_two,
        jnp.asarray(band_sources(chans)),
        jnp.asarray(band_sources(c2)),
        flops=2 * 64 * 864 * 1728,
    )
    ext = rows + 2 * edge
    send_low, send_high = call(
        extend_kernel, [((HALO, ext, breadth), BF), ((HALO, ext, breadth), BF)], turned, got_a, got_b
    )
    got_high = ring(send_low, -1)
    got_low = ring(send_high, 1)
    pairs = planes // 2 + 2
    (tile,) = call(
        convs_kernel,
        [((c3, breadth), BF)],
        turned,
        got_a,
        got_b,
        got_low,
        got_high,
        band1,
        band2,
        z_sel,
        p_sel,
        scratch=[
            pltpu.VMEM((3, planes + 2 * HALO, 18 * chans, breadth), BF),
            pltpu.VMEM((pairs, 6 * c2, breadth), BF),
            pltpu.VMEM((pairs - 1, 18 * c2, breadth), BF),
        ],
        flops=2 * 600_000_000,
    )
    tiles = [tile] + [lax.ppermute(tile, "yz", [(i, i ^ d) for i in range(yz)]) for d in range(1, yz)]
    cells = yz * (height // 4) * (breadth // 4)
    low, high = call(lay_kernel, [((c3, cells), BF), ((c3, cells), BF)], *tiles)
    after = ring(low, -1)
    before = ring(high, 1)
    out_rows = weight_three.shape[0] // yz
    picked = lax.dynamic_slice_in_dim(weight_three, lax.axis_index("yz") * out_rows, out_rows, 0)
    (out,) = call(
        functools.partial(last_kernel, breadth // 4),
        [((out_rows, 2 * cells), BF)],
        low,
        high,
        before,
        after,
        picked,
        scratch=[pltpu.VMEM((4, 9 * c3, cells), BF)],
        flops=2 * 32 * 1728 * 512,
    )
    return out.reshape(out_rows, 2, cells)


def solution(mesh):
    placed = (P("gx", None, "yz", None), P(), P(), P())
    return jax.shard_map(
        per_device, mesh=mesh, in_specs=placed, out_specs=P("yz", "gx", None), check_vma=False
    )
```

time: 98.2 us -> 32.5 us (0.33)
  the two profiles are of different devices: /device:TPU:4 before, /device:TPU:3 now
where the time goes in v1:
time: 32.5 us; the launch traced here: 32.3 us
  starting transfers between devices  12.8 us (39%)
  waiting for transfers between devices  12.8 us (39%)
  Pallas kernels  4.59 us (14%)
  local copies, waits for them, and re-layouts  2.04 us (6%)
    ppermute x4, waiting for transfers between devices, ring(): lax.ppermute(x, 'gx', [(i, (i + step) % count) for i in range(count)])  8.3 us
    ppermute x4, starting transfers between devices, ring(): lax.ppermute(x, 'gx', [(i, (i + step) % count) for i in range(count)])  5.39 us
    ppermute x3, starting transfers between devices, per_device(): lax.ppermute(tile, 'yz', [(i, i ^ d) for i in range(yz)])  5.12 us
    pallas_call x6, Pallas kernels, call(): pl.pallas_call(body, out_shape=[jax.ShapeDtypeStruct(s, d) for s, d in ou...  4.59 us
    ppermute x3, waiting for transfers between devices, per_device(): lax.ppermute(tile, 'yz', [(i, i ^ d) for i in range(yz)])  3.28 us
    ppermute x1, starting transfers between devices, per_device(): got_a = lax.ppermute(send_a, ('gx', 'yz'), yz_pairs(gx, yz, False))  1.36 us
    ppermute x1, waiting for transfers between devices, per_device(): got_a = lax.ppermute(send_a, ('gx', 'yz'), yz_pairs(gx, yz, False))  1.21 us
    unnamed x13, local copies, waits for them, and re-layouts  1.21 us
  transfers between devices with their start and end apart: 9, of which 7 were waited for; matrix products, arithmetic and copies ran while one was open for 1% of the time, Pallas kernels for 4%

profile of v1, /device:TPU:3, one launch (start us, length us, event | category | flops | bytes accessed | tf_op | source)
XLA Modules:
  0.0 32.3 jit_solution(462943182530843756)
XLA Ops:
  0.0 1.0 %copy-done.1 = bf16[8,16,8,128]{3,2,1,0:T(8,128)(2,1)S(1)} copy-done((bf16[8,16,8,128]{3,2,1,0:T(8,128)(2,1)S(1)}, bf16[8,16,8,128]{3,2,1,0:T(8,128)(2,1)}, u32[]{:S(2)}) %copy-start.1) | copy-done | bytes 262168
  1.0 0.2 shard_map.64
  1.2 1.4 %collective-permute-start = (bf16[8,48,128]{2,1,0:T(8,128)(2,1)S(1)}, bf16[8,48,128]{2,1,0:T(8,128)(2,1)S(1)}, u32[]{:S(2)}, u32[]{:S(2)}) collective-permute-start(bf16[8,48,128]{2,1,0:T(8,128)(2,1)S(1)} %get-tuple-element.17), channel_id=1, source_target_pairs={{0,1},{1,0},{2,3},{3,2},{4,5},{5,4},{6,7},{7,6},{8,9},{9,8},{10,11... | collective-permute-start | bytes 294920 | tf_op jit(solution)/shard_map/ppermute | solution.py:256
  2.6 1.0 %collective-permute-start.1 = (bf16[8,48,128]{2,1,0:T(8,128)(2,1)S(1)}, bf16[8,48,128]{2,1,0:T(8,128)(2,1)S(1)}, u32[]{:S(2)}, u32[]{:S(2)}) collective-permute-start(bf16[8,48,128]{2,1,0:T(8,128)(2,1)S(1)} %get-tuple-element.18), channel_id=1, source_target_pairs={{0,4},{1,2},{2,1},{3,7},{4,0},{5,6},{6,5},{7,3},{8,12},{9,10},{10,... | collective-permute-start | bytes 294920 | tf_op jit(solution)/shard_map/ppermute | solution.py:257
  3.6 1.2 %collective-permute-done.got_a = bf16[8,48,128]{2,1,0:T(8,128)(2,1)S(1)} collective-permute-done((bf16[8,48,128]{2,1,0:T(8,128)(2,1)S(1)}, bf16[8,48,128]{2,1,0:T(8,128)(2,1)S(1)}, u32[]{:S(2)}, u32[]{:S(2)}) %collective-permute-start) | collective-permute-done | bytes 98336 | tf_op jit(solution)/shard_map/ppermute | solution.py:256
  4.8 0.0 copy-start.5
  4.9 3.0 %collective-permute-start.2 = (bf16[3,224,128]{2,1,0:T(8,128)(2,1)S(1)}, bf16[3,224,128]{2,1,0:T(8,128)(2,1)S(1)}, u32[]{:S(2)}, u32[]{:S(2)}) collective-permute-start(bf16[3,224,128]{2,1,0:T(8,128)(2,1)S(1)} %get-tuple-element.19), channel_id=1, source_target_pairs={{0,4},{4,8},{8,12},{12,16},{16,20},{20,24},{24,28},{28,0},{1,5},{5... | collective-permute-start | bytes 516104 | tf_op jit(solution)/shard_map/ppermute | solution.py:74
  7.9 1.4 %shard_map.66 = (bf16[128,864]{1,0:T(8,128)(2,1)S(1)}, bf16[256,1728]{1,0:T(8,128)(2,1)S(1)}, bf16[256,384]{1,0:T(8,128)(2,1)S(1)}, bf16[512,128]{1,0:T(8,128)(2,1)S(1)}) custom-call(bf16[32,432]{1,0:T(8,128)(2,1)S(1)} %copy-done.3, bf16[64,864]{1,0:T(8,128)(2,1)S(1)} %copy-done.2, s32[1,864]{1,0:T(1,128)S(1)} %copy-done.5, s32[1,1728]{1,0:T(1,128)S(1)} %copy-done.4), custom_call_target="tpu_custom_call" | custom-call | flops 191102976 | bytes 148608 | tf_op jit(solution)/shard_map/pallas_call | solution.py:31
  9.2 2.0 %collective-permute-done.2.got_low = bf16[3,224,128]{2,1,0:T(8,128)(2,1)S(1)} collective-permute-done((bf16[3,224,128]{2,1,0:T(8,128)(2,1)S(1)}, bf16[3,224,128]{2,1,0:T(8,128)(2,1)S(1)}, u32[]{:S(2)}, u32[]{:S(2)}) %collective-permute-start.2) | collective-permute-done | bytes 172064 | tf_op jit(solution)/shard_map/ppermute | solution.py:74
  11.2 2.5 %collective-permute-done.3.got_high = bf16[3,224,128]{2,1,0:T(8,128)(2,1)S(1)} collective-permute-done((bf16[3,224,128]{2,1,0:T(8,128)(2,1)S(1)}, bf16[3,224,128]{2,1,0:T(8,128)(2,1)S(1)}, u32[]{:S(2)}, u32[]{:S(2)}) %collective-permute-start.3) | collective-permute-done | bytes 172064 | tf_op jit(solution)/shard_map/ppermute | solution.py:74
  13.7 2.3 %shard_map.67.refs_0_ = bf16[64,128]{1,0:T(8,128)(2,1)S(1)} custom-call(bf16[8,128,128]{2,1,0:T(8,128)(2,1)S(1)} %get-tuple-element.16.turned, bf16[8,48,128]{2,1,0:T(8,128)(2,1)S(1)} %collective-permute-done.got_a, bf16[8,48,128]{2,1,0:T(8,128)(2,1)S(1)} %collective-permute-done.1.got_b, bf16[3,224,128]{2,1,0:T(8,128)(2,1)S(1)} %collective-permute-done.2.got_low, ...), custom_call_target="tpu_custom_call" | custom-call | flops 1200000000 | bytes 2236416 | tf_op jit(solution)/shard_map/pallas_call | solution.py:31
  16.0 2.5 %collective-permute-start.4 = (bf16[64,128]{1,0:T(8,128)(2,1)S(1)}, bf16[64,128]{1,0:T(8,128)(2,1)S(1)}, u32[]{:S(2)}, u32[]{:S(2)}) collective-permute-start(bf16[64,128]{1,0:T(8,128)(2,1)S(1)} %shard_map.67.refs_0_), channel_id=1, source_target_pairs={{0,1},{1,0},{2,3},{3,2},{4,5},{5,4},{6,7},{7,6},{8,9},{9,8},{10,11... | collective-permute-start | bytes 49160 | tf_op jit(solution)/shard_map/ppermute | solution.py:294
  18.5 1.5 %collective-permute-start.5 = (bf16[64,128]{1,0:T(8,128)(2,1)S(1)}, bf16[64,128]{1,0:T(8,128)(2,1)S(1)}, u32[]{:S(2)}, u32[]{:S(2)}) collective-permute-start(bf16[64,128]{1,0:T(8,128)(2,1)S(1)} %shard_map.67.refs_0_), channel_id=1, source_target_pairs={{0,2},{1,3},{2,0},{3,1},{4,6},{5,7},{6,4},{7,5},{8,10},{9,11},{10,... | collective-permute-start | bytes 49160 | tf_op jit(solution)/shard_map/ppermute | solution.py:294
  20.0 1.1 %collective-permute-start.6 = (bf16[64,128]{1,0:T(8,128)(2,1)S(1)}, bf16[64,128]{1,0:T(8,128)(2,1)S(1)}, u32[]{:S(2)}, u32[]{:S(2)}) collective-permute-start(bf16[64,128]{1,0:T(8,128)(2,1)S(1)} %shard_map.67.refs_0_), channel_id=1, source_target_pairs={{0,3},{1,2},{2,1},{3,0},{4,7},{5,6},{6,5},{7,4},{8,11},{9,10},{10,... | collective-permute-start | bytes 49160 | tf_op jit(solution)/shard_map/ppermute | solution.py:294
  21.1 0.8 %collective-permute-done.5.refs_2_ = bf16[64,128]{1,0:T(8,128)(2,1)S(1)} collective-permute-done((bf16[64,128]{1,0:T(8,128)(2,1)S(1)}, bf16[64,128]{1,0:T(8,128)(2,1)S(1)}, u32[]{:S(2)}, u32[]{:S(2)}) %collective-permute-start.5) | collective-permute-done | bytes 16416 | tf_op jit(solution)/shard_map/ppermute | solution.py:294
  22.0 2.4 %collective-permute-done.6.refs_3_ = bf16[64,128]{1,0:T(8,128)(2,1)S(1)} collective-permute-done((bf16[64,128]{1,0:T(8,128)(2,1)S(1)}, bf16[64,128]{1,0:T(8,128)(2,1)S(1)}, u32[]{:S(2)}, u32[]{:S(2)}) %collective-permute-start.6) | collective-permute-done | bytes 16416 | tf_op jit(solution)/shard_map/ppermute | solution.py:294
  24.4 0.1 shard_map.68
  24.5 2.4 %collective-permute-start.7 = (bf16[64,256]{1,0:T(8,128)(2,1)S(1)}, bf16[64,256]{1,0:T(8,128)(2,1)S(1)}, u32[]{:S(2)}, u32[]{:S(2)}) collective-permute-start(bf16[64,256]{1,0:T(8,128)(2,1)S(1)} %get-tuple-element.26.high), channel_id=1, source_target_pairs={{0,4},{4,8},{8,12},{12,16},{16,20},{20,24},{24,28},{28,0},{1,5},{5... | collective-permute-start | bytes 98312 | tf_op jit(solution)/shard_map/ppermute | solution.py:74
  26.9 0.2 constant_dynamic-slice_fusion
  27.1 0.2 copy.8.w3
  27.3 0.6 %collective-permute-done.7.before = bf16[64,256]{1,0:T(8,128)(2,1)S(1)} collective-permute-done((bf16[64,256]{1,0:T(8,128)(2,1)S(1)}, bf16[64,256]{1,0:T(8,128)(2,1)S(1)}, u32[]{:S(2)}, u32[]{:S(2)}) %collective-permute-start.7) | collective-permute-done | bytes 32800 | tf_op jit(solution)/shard_map/ppermute | solution.py:74
  27.9 3.2 %collective-permute-done.8.after = bf16[64,256]{1,0:T(8,128)(2,1)S(1)} collective-permute-done((bf16[64,256]{1,0:T(8,128)(2,1)S(1)}, bf16[64,256]{1,0:T(8,128)(2,1)S(1)}, u32[]{:S(2)}, u32[]{:S(2)}) %collective-permute-start.8) | collective-permute-done | bytes 32800 | tf_op jit(solution)/shard_map/ppermute | solution.py:74
  31.2 0.5 %shard_map.69 = bf16[32,512]{1,0:T(8,128)(2,1)S(1)} custom-call(bf16[64,256]{1,0:T(8,128)(2,1)S(1)} %get-tuple-element.25.low, bf16[64,256]{1,0:T(8,128)(2,1)S(1)} %get-tuple-element.26.high, bf16[64,256]{1,0:T(8,128)(2,1)S(1)} %collective-permute-done.7.before, bf16[64,256]{1,0:T(8,128)(2,1)S(1)} %collective-permute-done.8.after, bf16[32,1728]{1,0:T(8,128)(2,1)S(1)} %copy.8.w3), custom_call_target="tpu_custom_call" | custom-call | flops 56623104 | bytes 241664 | tf_op jit(solution)/shard_map/pallas_call | solution.py:31
  31.7 0.6 %reshape.3 = bf16[32,2,256]{2,1,0:T(2,128)(2,1)} reshape(bf16[32,512]{1,0:T(8,128)(2,1)S(1)} %shard_map.69) | data formatting | bytes 65536 | tf_op jit(solution)/shard_map/reshape | solution.py:312
  (15 shorter events, 0.1 us)
Async XLA Ops:
  0.0 26.9 %copy-start = (bf16[128,1728]{0,1:T(8,128)(2,1)S(1)}, bf16[128,1728]{0,1:T(8,128)(2,1)}, u32[]{:S(2)}) copy-start(bf16[128,1728]{0,1:T(8,128)(2,1)} %param.9) | copy-start | bytes 1327108
  0.0 1.0 %copy-start.1 = (bf16[8,16,8,128]{3,2,1,0:T(8,128)(2,1)S(1)}, bf16[8,16,8,128]{3,2,1,0:T(8,128)(2,1)}, u32[]{:S(2)}) copy-start(bf16[8,16,8,128]{3,2,1,0:T(8,128)(2,1)} %vol.1) | copy-start | bytes 786436
  1.2 3.5 %collective-permute-start = (bf16[8,48,128]{2,1,0:T(8,128)(2,1)S(1)}, bf16[8,48,128]{2,1,0:T(8,128)(2,1)S(1)}, u32[]{:S(2)}, u32[]{:S(2)}) collective-permute-start(bf16[8,48,128]{2,1,0:T(8,128)(2,1)S(1)} %get-tuple-element.17), channel_id=1, source_target_pairs={{0,1},{1,0},{2,3},{3,2},{4,5},{5,4},{6,7},{7,6},{8,9},{9,8},{10,11... | collective-permute-start | bytes 294920 | tf_op jit(solution)/shard_map/ppermute | solution.py:256
  2.6 2.2 %collective-permute-start.1 = (bf16[8,48,128]{2,1,0:T(8,128)(2,1)S(1)}, bf16[8,48,128]{2,1,0:T(8,128)(2,1)S(1)}, u32[]{:S(2)}, u32[]{:S(2)}) collective-permute-start(bf16[8,48,128]{2,1,0:T(8,128)(2,1)S(1)} %get-tuple-element.18), channel_id=1, source_target_pairs={{0,4},{1,2},{2,1},{3,7},{4,0},{5,6},{6,5},{7,3},{8,12},{9,10},{10,... | collective-permute-start | bytes 294920 | tf_op jit(solution)/shard_map/ppermute | solution.py:257
  4.8 3.1 %copy-start.2 = (bf16[64,864]{1,0:T(8,128)(2,1)S(1)}, bf16[64,864]{1,0:T(8,128)(2,1)}, u32[]{:S(2)}) copy-start(bf16[64,864]{1,0:T(8,128)(2,1)} %w2.1) | copy-start | bytes 331780
  4.8 3.1 %copy-start.3 = (bf16[32,432]{1,0:T(8,128)(2,1)S(1)}, bf16[32,432]{1,0:T(8,128)(2,1)}, u32[]{:S(2)}) copy-start(bf16[32,432]{1,0:T(8,128)(2,1)} %w1.1) | copy-start | bytes 82948
  4.8 3.1 %copy-start.4 = (s32[1,1728]{1,0:T(1,128)S(1)}, s32[1,1728]{1,0:T(1,128)}, u32[]{:S(2)}) copy-start(s32[1,1728]{1,0:T(1,128)} %constant.15.clone.src2) | copy-start | bytes 20740
  4.8 3.0 %copy-start.5 = (s32[1,864]{1,0:T(1,128)S(1)}, s32[1,864]{1,0:T(1,128)}, u32[]{:S(2)}) copy-start(s32[1,864]{1,0:T(1,128)} %constant.14.clone.src1) | copy-start | bytes 10372
  4.9 6.4 %collective-permute-start.2 = (bf16[3,224,128]{2,1,0:T(8,128)(2,1)S(1)}, bf16[3,224,128]{2,1,0:T(8,128)(2,1)S(1)}, u32[]{:S(2)}, u32[]{:S(2)}) collective-permute-start(bf16[3,224,128]{2,1,0:T(8,128)(2,1)S(1)} %get-tuple-element.19), channel_id=1, source_target_pairs={{0,4},{4,8},{8,12},{12,16},{16,20},{20,24},{24,28},{28,0},{1,5},{5... | collective-permute-start | bytes 516104 | tf_op jit(solution)/shard_map/ppermute | solution.py:74
  7.8 5.8 %collective-permute-start.3 = (bf16[3,224,128]{2,1,0:T(8,128)(2,1)S(1)}, bf16[3,224,128]{2,1,0:T(8,128)(2,1)S(1)}, u32[]{:S(2)}, u32[]{:S(2)}) collective-permute-start(bf16[3,224,128]{2,1,0:T(8,128)(2,1)S(1)} %get-tuple-element.20), channel_id=1, source_target_pairs={{0,28},{4,0},{8,4},{12,8},{16,12},{20,16},{24,20},{28,24},{1,29},{... | collective-permute-start | bytes 516104 | tf_op jit(solution)/shard_map/ppermute | solution.py:74
  16.0 5.1 %collective-permute-start.4 = (bf16[64,128]{1,0:T(8,128)(2,1)S(1)}, bf16[64,128]{1,0:T(8,128)(2,1)S(1)}, u32[]{:S(2)}, u32[]{:S(2)}) collective-permute-start(bf16[64,128]{1,0:T(8,128)(2,1)S(1)} %shard_map.67.refs_0_), channel_id=1, source_target_pairs={{0,1},{1,0},{2,3},{3,2},{4,5},{5,4},{6,7},{7,6},{8,9},{9,8},{10,11... | collective-permute-start | bytes 49160 | tf_op jit(solution)/shard_map/ppermute | solution.py:294
  18.5 3.5 %collective-permute-start.5 = (bf16[64,128]{1,0:T(8,128)(2,1)S(1)}, bf16[64,128]{1,0:T(8,128)(2,1)S(1)}, u32[]{:S(2)}, u32[]{:S(2)}) collective-permute-start(bf16[64,128]{1,0:T(8,128)(2,1)S(1)} %shard_map.67.refs_0_), channel_id=1, source_target_pairs={{0,2},{1,3},{2,0},{3,1},{4,6},{5,7},{6,4},{7,5},{8,10},{9,11},{10,... | collective-permute-start | bytes 49160 | tf_op jit(solution)/shard_map/ppermute | solution.py:294
  20.0 4.4 %collective-permute-start.6 = (bf16[64,128]{1,0:T(8,128)(2,1)S(1)}, bf16[64,128]{1,0:T(8,128)(2,1)S(1)}, u32[]{:S(2)}, u32[]{:S(2)}) collective-permute-start(bf16[64,128]{1,0:T(8,128)(2,1)S(1)} %shard_map.67.refs_0_), channel_id=1, source_target_pairs={{0,3},{1,2},{2,1},{3,0},{4,7},{5,6},{6,5},{7,4},{8,11},{9,10},{10,... | collective-permute-start | bytes 49160 | tf_op jit(solution)/shard_map/ppermute | solution.py:294
  24.5 3.4 %collective-permute-start.7 = (bf16[64,256]{1,0:T(8,128)(2,1)S(1)}, bf16[64,256]{1,0:T(8,128)(2,1)S(1)}, u32[]{:S(2)}, u32[]{:S(2)}) collective-permute-start(bf16[64,256]{1,0:T(8,128)(2,1)S(1)} %get-tuple-element.26.high), channel_id=1, source_target_pairs={{0,4},{4,8},{8,12},{12,16},{16,20},{20,24},{24,28},{28,0},{1,5},{5... | collective-permute-start | bytes 98312 | tf_op jit(solution)/shard_map/ppermute | solution.py:74
  26.9 4.2 %collective-permute-start.8 = (bf16[64,256]{1,0:T(8,128)(2,1)S(1)}, bf16[64,256]{1,0:T(8,128)(2,1)S(1)}, u32[]{:S(2)}, u32[]{:S(2)}) collective-permute-start(bf16[64,256]{1,0:T(8,128)(2,1)S(1)} %get-tuple-element.25.low), channel_id=1, source_target_pairs={{0,28},{4,0},{8,4},{12,8},{16,12},{20,16},{24,20},{28,24},{1,29},{... | collective-permute-start | bytes 98312 | tf_op jit(solution)/shard_map/ppermute | solution.py:74

commit v2 on v1

v2 whole, which is shorter than its diff:
```python
import functools

import jax
import jax.numpy as jnp
from jax import lax
from jax.experimental import pallas as pl
from jax.experimental.pallas import tpu as pltpu
from jax.sharding import PartitionSpec as P

BF = jnp.bfloat16
F32 = jnp.float32
WHOLE = pl.BlockSpec(memory_space=pltpu.VMEM)
HALO = 3


def mat(a, b):
    return jnp.dot(a, b, preferred_element_type=F32)


def relu(a):
    return jnp.maximum(a, 0.0)


def iota(shape, dim):
    return lax.broadcasted_iota(jnp.int32, shape, dim)


def call(body, outs, *args, scratch=(), flops=0, space=pltpu.VMEM):
    moved = sum(a.size * a.dtype.itemsize for a in args)
    return pl.pallas_call(
        body,
        out_shape=[jax.ShapeDtypeStruct(s, d) for s, d in outs],
        in_specs=[pl.BlockSpec(memory_space=space)] * len(args),
        out_specs=[WHOLE] * len(outs),
        scratch_shapes=list(scratch),
        compiler_params=pltpu.CompilerParams(vmem_limit_bytes=40 * 1024 * 1024),
        cost_estimate=pl.CostEstimate(flops=flops, bytes_accessed=moved, transcendentals=0),
    )(*args)


def turn_kernel(vol, turned, send_a, send_b):
    planes, chans, height, breadth = vol.shape
    rows = chans * height
    dest = iota((rows, rows), 0)
    source = (dest & (chans - 1)) * height + dest // chans
    swap = (iota((rows, rows), 1) == source).astype(F32).astype(BF)
    even = lax.rem(lax.axis_index("yz"), 2) == 0
    edge = HALO * chans
    for x in range(planes):
        t = mat(swap, vol[x].reshape(rows, breadth)).astype(BF)
        turned[x] = t
        low, high = t[:edge], t[rows - edge :]
        send_a[x] = jnp.where(even, high, low)
        send_b[x] = jnp.where(even, low, high)


def yz_pairs(gx, yz, second):
    pairs = []
    for g in range(gx):
        for k in range(yz):
            if not second:
                pairs.append((g * yz + k, g * yz + (k ^ 1)))
            elif k in (0, yz - 1):
                pairs.append((g * yz + k, (g ^ 1) * yz + k))
            else:
                pairs.append((g * yz + k, g * yz + (k + 1 if k % 2 else k - 1)))
    return pairs


def gx_pairs(gx, yz, far):
    pairs = []
    for g in range(gx):
        for k in range(yz):
            if not far:
                pairs.append((g * yz + k, (g ^ 1) * yz + k))
            elif g in (0, gx - 1):
                pairs.append((g * yz + k, g * yz + (k ^ 1)))
            else:
                pairs.append((g * yz + k, (g + 1 if g % 2 else g - 1) * yz + k))
    return pairs


def is_even(axis):
    return lax.rem(lax.axis_index(axis), 2) == 0


def y_sides(got_a, got_b, x):
    k = lax.axis_index("yz")
    last = lax.axis_size("yz") - 1
    even = lax.rem(k, 2) == 0
    a, b = got_a[x], got_b[x]
    zero = jnp.zeros_like(a)
    low = jnp.where(k == 0, zero, jnp.where(even, b, a))
    high = jnp.where(k == last, zero, jnp.where(even, a, b))
    return low, high


def extend_kernel(turned, got_a, got_b, _, send_mate, send_far):
    planes, rows, _ = turned.shape
    edge = got_a.shape[1]
    even = is_even("gx")
    for out, first in (
        (send_mate, jnp.where(even, planes - HALO, 0)),
        (send_far, jnp.where(even, 0, planes - HALO)),
    ):
        for x in range(HALO):
            low, high = y_sides(got_a, got_b, first + x)
            out[x, :edge] = low
            out[x, edge : edge + rows] = turned[first + x]
            out[x, edge + rows :] = high


def weights_kernel(w1_hbm, w2_hbm, band1, band1_last, band2, z_sel, p_sel, w1, w2, sems):
    loads = [pltpu.make_async_copy(a, b, sems.at[i]) for i, (a, b) in enumerate(((w1_hbm, w1), (w2_hbm, w2)))]
    for load in loads:
        load.start()

    rows, columns = z_sel.shape
    breadth = rows // 2
    r, c = iota(z_sel.shape, 0), iota(z_sel.shape, 1)
    tap = c // breadth
    within = c - tap * breadth
    same = (r // breadth) == (within // (breadth // 2))
    cell = (r & (breadth - 1)) == 2 * ((within & (breadth // 2 - 1)) + tap - 1)
    z_sel[...] = jnp.where(same & cell, 1.0, 0.0).astype(BF)

    rows, columns = p_sel.shape
    z = rows // 8
    r, c = iota(p_sel.shape, 0), iota(p_sel.shape, 1)
    hit = (r // (4 * z) == (c // (z // 2)) % 2) & ((r // z) % 4 == 2 * (c // z))
    hit = hit & ((r & (z - 1)) == 2 * (c & (z // 2 - 1)))
    p_sel[...] = jnp.where(hit, 1.0, 0.0).astype(BF)

    for load in loads:
        load.wait()
    for w, band, last in ((w1, band1, band1_last), (w2, band2, None)):
        out_rows, columns = w.shape[0], band.shape[1]
        chans = w.shape[1] // 27
        col = iota((1, columns), 1)
        block = col // chans
        row, group = block % 6, block // 6
        source = ((group // 3 * 3 + row) * 3 + group % 3) * chans + col % chans
        source = jnp.where(row < 3, source, -1)
        sel = (iota((w.shape[1], columns), 0) == source).astype(F32).astype(BF)
        base = mat(w[...], sel)
        wide = -(-columns // 128) * 128
        base = jnp.pad(base, ((0, 0), (0, wide - columns)))
        for y in range(4):
            moved = base if y == 0 else pltpu.roll(base, y * chans, 1)
            rows = slice(out_rows * y, out_rows * (y + 1))
            band[rows] = moved[:, :columns].astype(BF)
            if last is not None:
                last[rows] = moved[:, columns // 3 * 2 : columns].astype(BF)


def put_taps(dest, t, chans):
    breadth = t.shape[1]
    window = 6 * chans
    lane = iota((1, breadth), 1)
    wide = t.astype(F32)
    before = jnp.where(lane == 0, 0.0, pltpu.roll(wide, 1, 1)).astype(BF)
    after = jnp.where(lane == breadth - 1, 0.0, pltpu.roll(wide, breadth - 1, 1)).astype(BF)
    for tap, value in enumerate((before, t, after)):
        for part in range(3):
            first = part * 4 * chans
            dest(part)[tap * window : (tap + 1) * window] = value[first : first + window]


def pool_first(acc, part, outside):
    k = lax.axis_index("yz")
    breadth = acc.shape[1] // 2
    width = acc.shape[0] // 4
    r = relu(acc)
    s = r[:, :breadth] + r[:, breadth:]
    halves = []
    for y in range(2):
        t = s[2 * y * width : (2 * y + 1) * width] + s[(2 * y + 1) * width : (2 * y + 2) * width]
        t = (t + pltpu.roll(t, breadth - 1, 1)) * 0.125
        drop = outside
        if part == 0 and y == 0:
            drop = drop | (k == 0)
        if part == 2 and y == 1:
            drop = drop | (k == lax.axis_size("yz") - 1)
        halves.append(jnp.where(drop, 0.0, t))
    return jnp.concatenate(halves, 0).astype(BF)


def inner_kernel(turned, got_a, got_b, band1, taps, pooled, partial):
    planes, rows, breadth = turned.shape
    chans = got_a.shape[1] // HALO
    for x in range(planes):
        low, high = y_sides(got_a, got_b, x)
        put_taps(lambda part: taps.at[part, x], jnp.concatenate([low, turned[x], high], 0), chans)
    w = band1[...]
    zero = jnp.zeros((taps.shape[2], breadth), BF)
    pairs = planes // 2
    for p in range(pairs):
        for part in range(3):
            if p == 0:
                left = jnp.concatenate([zero, taps[part, 0:2].reshape(-1, breadth)], 0)
            else:
                left = taps[part, 2 * p - 1 : 2 * p + 2].reshape(-1, breadth)
            if p == pairs - 1:
                right = jnp.concatenate([taps[part, planes - 2 : planes].reshape(-1, breadth), zero], 0)
            else:
                right = taps[part, 2 * p : 2 * p + 3].reshape(-1, breadth)
            acc = mat(w, jnp.concatenate([left, right], 1))
            if p == 0:
                partial[0, part] = acc
            elif p == pairs - 1:
                partial[1, part] = acc
            else:
                half = pooled.shape[1] // 3
                pooled[p - 1, part * half : (part + 1) * half] = pool_first(acc, part, False)


def outer_kernel(
    taps, pooled_in, partial, got_mate, got_far, band1, band1_last, band2, z_sel, p_sel, out, taps_low, taps_high, pooled, taps2
):
    _, planes, depth, breadth = taps.shape
    chans = depth // 18
    even = is_even("gx")
    g, g_last = lax.axis_index("gx"), lax.axis_size("gx") - 1
    for x in range(HALO):
        mate, far = got_mate[x], got_far[x]
        zero = jnp.zeros_like(mate)
        low = jnp.where(g == 0, zero, jnp.where(even, far, mate))
        high = jnp.where(g == g_last, zero, jnp.where(even, mate, far))
        put_taps(lambda part: taps_low.at[part, x], low, chans)
        put_taps(lambda part: taps_high.at[part, x], high, chans)

    pairs = pooled.shape[0]
    half = pooled.shape[1] // 3
    w = band1[...]
    for part in range(3):
        rows = slice(part * half, (part + 1) * half)
        left = taps_low[part].reshape(-1, breadth)
        right = jnp.concatenate([taps_low[part, 1:3].reshape(-1, breadth), taps[part, 0]], 0)
        pooled[0, rows] = pool_first(mat(w, jnp.concatenate([left, right], 1)), part, g == 0)
        left = jnp.concatenate([taps[part, planes - 1], taps_high[part, 0:2].reshape(-1, breadth)], 0)
        right = taps_high[part].reshape(-1, breadth)
        pooled[pairs - 1, rows] = pool_first(mat(w, jnp.concatenate([left, right], 1)), part, g == g_last)
        acc = partial[0, part]
        left = acc[:, :breadth] + mat(w[:, :depth], taps_low[part, 2])
        pooled[1, rows] = pool_first(jnp.concatenate([left, acc[:, breadth:]], 1), part, False)
        acc = partial[1, part]
        right = acc[:, breadth:] + mat(band1_last[...], taps_high[part, 0])
        pooled[pairs - 2, rows] = pool_first(jnp.concatenate([acc[:, :breadth], right], 1), part, False)
    for j in range(pairs - 4):
        pooled[2 + j] = pooled_in[j]

    window = pooled.shape[1]
    for j in range(pairs - 1):
        q = mat(jnp.concatenate([pooled[j], pooled[j + 1]], 1), z_sel[...]).astype(BF)
        for tap in range(3):
            taps2[j, tap * window : (tap + 1) * window] = q[:, tap * breadth : (tap + 1) * breadth]
    left = taps2[0:3].reshape(-1, breadth)
    right = taps2[2:5].reshape(-1, breadth)
    r = relu(mat(band2[...], jnp.concatenate([left, right], 1)))
    width = r.shape[0] // 4
    halves = []
    for y in range(2):
        t = r[2 * y * width : (2 * y + 1) * width] + r[(2 * y + 1) * width : (2 * y + 2) * width]
        t = t + pltpu.roll(t, 2 * breadth - breadth // 2, 1)
        t = (t + pltpu.roll(t, 2 * breadth - 1, 1)) * 0.125
        halves.append(t.astype(BF))
    out[...] = mat(jnp.concatenate(halves, 1), p_sel[...]).astype(BF)


def lay_kernel(*refs):
    tiles, (mate, far) = refs[:-2], refs[-2:]
    k = lax.axis_index("yz")
    even = is_even("yz")
    half = tiles[0].shape[1] // 2
    lane = iota((1, 2 * half), 1)
    for m in range(len(tiles) // 2):
        a, b = tiles[2 * m][...].astype(F32), tiles[2 * m + 1][...].astype(F32)
        first, second = jnp.where(even, a, b), jnp.where(even, b, a)
        place = pl.ds(pl.multiple_of((lax.div(k, 2) ^ m) * 2 * half, 2 * half), 2 * half)
        low = jnp.where(lane < half, first, pltpu.roll(second, half, 1))
        high = jnp.where(lane < half, pltpu.roll(first, half, 1), second)
        mate[:, place] = jnp.where(is_even("gx"), high, low).astype(BF)
        far[:, place] = jnp.where(is_even("gx"), low, high).astype(BF)


def plane_taps(dest, t, z):
    chans, cells = t.shape
    lane = iota((1, cells), 1)
    depth = lane & (z - 1)
    for b in range(3):
        for c in range(3):
            step = (b - 1) * z + c - 1
            moved = t if step == 0 else pltpu.roll(t, (-step) % cells, 1)
            inside = (lane + step >= 0) & (lane + step < cells)
            inside = inside & (depth + (c - 1) >= 0) & (depth + (c - 1) < z)
            row = (3 * b + c) * chans
            dest[row : row + chans] = jnp.where(inside, moved, 0.0).astype(BF)


def middle_kernel(z, mate, far, w3, partial, taps):
    chans, cells = mate.shape
    even = is_even("gx")
    a, b = mate[...].astype(F32), far[...].astype(F32)
    plane_taps(taps.at[0], jnp.where(even, b, a), z)
    plane_taps(taps.at[1], jnp.where(even, a, b), z)
    w = w3[...]
    depth = 9 * chans
    both = taps[...].reshape(2 * depth, cells)
    partial[0] = mat(w[:, depth:], both)
    partial[1] = mat(w[:, : 2 * depth], both)


def last_kernel(z, partial, got_mate, got_far, w3, out, taps):
    chans, cells = got_mate.shape
    g, g_last = lax.axis_index("gx"), lax.axis_size("gx") - 1
    even = is_even("gx")
    mate, far = got_mate[...].astype(F32), got_far[...].astype(F32)
    plane_taps(taps.at[0], jnp.where(g == 0, 0.0, jnp.where(even, far, mate)), z)
    plane_taps(taps.at[1], jnp.where(g == g_last, 0.0, jnp.where(even, mate, far)), z)
    w = w3[...]
    depth = 9 * chans
    first = relu(partial[0] + mat(w[:, :depth], taps[0]))
    second = relu(partial[1] + mat(w[:, 2 * depth :], taps[1]))
    out[...] = jnp.stack([first, second], 1).astype(BF)


def per_device(volume, weight_one, weight_two, weight_three):
    gx, yz = lax.axis_size("gx"), lax.axis_size("yz")
    planes, chans, height, breadth = volume.shape
    rows = chans * height
    edge = HALO * chans
    c2, c3 = weight_one.shape[0], weight_two.shape[0]

    turned, send_a, send_b = call(
        turn_kernel,
        [((planes, rows, breadth), BF), ((planes, edge, breadth), BF), ((planes, edge, breadth), BF)],
        volume,
    )
    got_b = lax.ppermute(send_b, ("gx", "yz"), yz_pairs(gx, yz, True))
    got_a = lax.ppermute(send_a, ("gx", "yz"), yz_pairs(gx, yz, False))
    k1, k2 = 54 * chans, 54 * c2
    band1, band1_last, band2, z_sel, p_sel = call(
        weights_kernel,
        [
            ((4 * c2, k1), BF),
            ((4 * c2, k1 // 3), BF),
            ((4 * c3, k2), BF),
            ((2 * breadth, 3 * breadth), BF),
            ((4 * breadth, breadth), BF),
        ],
        weight_one,
        weight_two,
        scratch=[
            pltpu.VMEM(weight_one.shape, BF),
            pltpu.VMEM(weight_two.shape, BF),
            pltpu.SemaphoreType.DMA((2,)),
        ],
        flops=2 * 64 * 864 * 1728,
        space=pltpu.HBM,
    )
    ext = rows + 2 * edge
    send_mate, send_far = call(
        extend_kernel,
        [((HALO, ext, breadth), BF), ((HALO, ext, breadth), BF)],
        turned,
        got_a,
        got_b,
        p_sel,
    )
    near, away = gx_pairs(gx, yz, False), gx_pairs(gx, yz, True)
    got_far = lax.ppermute(send_far, ("gx", "yz"), away)
    got_mate = lax.ppermute(send_mate, ("gx", "yz"), near)
    pairs = planes // 2 + 2
    taps, pooled, partial = call(
        inner_kernel,
        [
            ((3, planes, 18 * chans, breadth), BF),
            ((pairs - 4, 6 * c2, breadth), BF),
            ((2, 3, 4 * c2, 2 * breadth), F32),
        ],
        turned,
        got_a,
        got_b,
        band1,
        flops=2 * 300_000_000,
    )
    (tile,) = call(
        outer_kernel,
        [((c3, breadth), BF)],
        taps,
        pooled,
        partial,
        got_mate,
        got_far,
        band1,
        band1_last,
        band2,
        z_sel,
        p_sel,
        scratch=[
            pltpu.VMEM((3, HALO, 18 * chans, breadth), BF),
            pltpu.VMEM((3, HALO, 18 * chans, breadth), BF),
            pltpu.VMEM((pairs, 6 * c2, breadth), BF),
            pltpu.VMEM((pairs - 1, 18 * c2, breadth), BF),
        ],
        flops=2 * 400_000_000,
    )
    tiles = [tile] + [lax.ppermute(tile, "yz", [(i, i ^ d) for i in range(yz)]) for d in range(1, yz)]
    cells = yz * (height // 4) * (breadth // 4)
    z = breadth // 4
    mate, far = call(lay_kernel, [((c3, cells), BF), ((c3, cells), BF)], *tiles)
    got_far = lax.ppermute(far, ("gx", "yz"), away)
    got_mate = lax.ppermute(mate, ("gx", "yz"), near)
    out_rows = weight_three.shape[0] // yz
    picked = lax.dynamic_slice_in_dim(weight_three, lax.axis_index("yz") * out_rows, out_rows, 0)
    (partial,) = call(
        functools.partial(middle_kernel, z),
        [((2, out_rows, cells), F32)],
        mate,
        far,
        picked,
        scratch=[pltpu.VMEM((2, 9 * c3, cells), BF)],
        flops=2 * 32 * 1152 * 512,
    )
    (out,) = call(
        functools.partial(last_kernel, z),
        [((out_rows, 2, cells), BF)],
        partial,
        got_mate,
        got_far,
        picked,
        scratch=[pltpu.VMEM((2, 9 * c3, cells), BF)],
        flops=2 * 32 * 576 * 512,
    )
    return out


def solution(mesh):
    placed = (P("gx", None, "yz", None), P(), P(), P())
    return jax.shard_map(
        per_device, mesh=mesh, in_specs=placed, out_specs=P("yz", "gx", None), check_vma=False
    )
```

time: 32.5 us -> 30.9 us (0.951)
  the two profiles are of different devices: /device:TPU:3 before, /device:TPU:4 now
where the time goes in v2:
time: 30.9 us; the launch traced here: 30.7 us
  waiting for transfers between devices  12 us (39%)
  starting transfers between devices  9.06 us (29%)
  Pallas kernels  6.44 us (21%)
  local copies, waits for them, and re-layouts  3.04 us (10%)
    pallas_call x8, Pallas kernels, call(): pl.pallas_call(body, out_shape=[jax.ShapeDtypeStruct(s, d) for s, d in ou...  6.44 us
    ppermute x3, starting transfers between devices, per_device(): lax.ppermute(tile, 'yz', [(i, i ^ d) for i in range(yz)])  5.58 us
    ppermute x1, waiting for transfers between devices, per_device(): got_far = lax.ppermute(send_far, ('gx', 'yz'), away)  4.66 us
    ppermute x3, waiting for transfers between devices, per_device(): lax.ppermute(tile, 'yz', [(i, i ^ d) for i in range(yz)])  3.88 us
    ppermute x1, waiting for transfers between devices, per_device(): got_far = lax.ppermute(far, ('gx', 'yz'), away)  3.11 us
    unnamed x9, local copies, waits for them, and re-layouts  2.85 us
    ppermute x1, starting transfers between devices, per_device(): got_a = lax.ppermute(send_a, ('gx', 'yz'), yz_pairs(gx, yz, False))  1.64 us
    ppermute x1, starting transfers between devices, per_device(): got_far = lax.ppermute(send_far, ('gx', 'yz'), away)  1.12 us
  transfers between devices with their start and end apart: 9, of which 5 were waited for; matrix products, arithmetic and copies ran while one was open for 1% of the time, Pallas kernels for 10%

profile of v2, /device:TPU:4, one launch (start us, length us, event | category | flops | bytes accessed | tf_op | source)
XLA Modules:
  0.0 30.7 jit_solution(4070408125553781955)
XLA Ops:
  0.0 1.0 %copy-done.1 = bf16[8,16,8,128]{3,2,1,0:T(8,128)(2,1)S(1)} copy-done((bf16[8,16,8,128]{3,2,1,0:T(8,128)(2,1)S(1)}, bf16[8,16,8,128]{3,2,1,0:T(8,128)(2,1)}, u32[]{:S(2)}) %copy-start.1) | copy-done | bytes 262168
  1.0 0.2 shard_map.46
  1.2 1.6 %collective-permute-start = (bf16[8,48,128]{2,1,0:T(8,128)(2,1)S(1)}, bf16[8,48,128]{2,1,0:T(8,128)(2,1)S(1)}, u32[]{:S(2)}, u32[]{:S(2)}) collective-permute-start(bf16[8,48,128]{2,1,0:T(8,128)(2,1)S(1)} %get-tuple-element.21), channel_id=1, source_target_pairs={{0,1},{1,0},{2,3},{3,2},{4,5},{5,4},{6,7},{7,6},{8,9},{9,8},{10,11... | collective-permute-start | bytes 294920 | tf_op jit(solution)/shard_map/ppermute | solution.py:340
  2.9 0.9 %copy-done.2 = bf16[64,864]{1,0:T(8,128)(2,1)S(1)} copy-done((bf16[64,864]{1,0:T(8,128)(2,1)S(1)}, bf16[64,864]{1,0:T(8,128)(2,1)}, u32[]{:S(2)}) %copy-start.2) | copy-done | bytes 110616
  3.8 0.8 %copy-done.3 = bf16[32,432]{1,0:T(8,128)(2,1)S(1)} copy-done((bf16[32,432]{1,0:T(8,128)(2,1)S(1)}, bf16[32,432]{1,0:T(8,128)(2,1)}, u32[]{:S(2)}) %copy-start.3) | copy-done | bytes 27672
  4.5 1.6 %shard_map.47 = (bf16[128,864]{1,0:T(8,128)(2,1)S(1)}, bf16[128,288]{1,0:T(8,128)(2,1)S(1)}, bf16[256,1728]{1,0:T(8,128)(2,1)S(1)}, bf16[256,384]{1,0:T(8,128)(2,1)S(1)}, bf16[512,128]{1,0:T(8,128)(2,1)S(1)}) custom-call(bf16[32,432]{1,0:T(8,128)(2,1)S(1)} %copy-done.3, bf16[64,864]{1,0:T(8,128)(2,1)S(1)} %copy-done.2), custom_call_target="tpu_custom_call" | custom-call | flops 191102976 | bytes 138240 | tf_op jit(solution)/shard_map/pallas_call | solution.py:30
  6.3 0.6 %collective-permute-start.2 = (bf16[3,224,128]{2,1,0:T(8,128)(2,1)S(1)}, bf16[3,224,128]{2,1,0:T(8,128)(2,1)S(1)}, u32[]{:S(2)}, u32[]{:S(2)}) collective-permute-start(bf16[3,224,128]{2,1,0:T(8,128)(2,1)S(1)} %get-tuple-element.28), channel_id=1, source_target_pairs={{0,4},{1,5},{2,6},{3,7},{4,0},{5,1},{6,2},{7,3},{8,12},{9,13},{10,... | collective-permute-start | bytes 516104 | tf_op jit(solution)/shard_map/ppermute | solution.py:372
  6.9 1.1 %collective-permute-start.3 = (bf16[3,224,128]{2,1,0:T(8,128)(2,1)S(1)}, bf16[3,224,128]{2,1,0:T(8,128)(2,1)S(1)}, u32[]{:S(2)}, u32[]{:S(2)}) collective-permute-start(bf16[3,224,128]{2,1,0:T(8,128)(2,1)S(1)} %get-tuple-element.29), channel_id=1, source_target_pairs={{0,1},{1,0},{2,3},{3,2},{4,8},{5,9},{6,10},{7,11},{8,4},{9,5},{10,... | collective-permute-start | bytes 516104 | tf_op jit(solution)/shard_map/ppermute | solution.py:371
  8.0 1.1 %shard_map.48 = (bf16[3,8,288,128]{3,2,1,0:T(8,128)(2,1)S(1)}, bf16[2,192,128]{2,1,0:T(8,128)(2,1)S(1)}, f32[2,3,128,256]{3,2,1,0:T(8,128)S(1)}) custom-call(bf16[8,128,128]{2,1,0:T(8,128)(2,1)S(1)} %get-tuple-element.20.turned, bf16[8,48,128]{2,1,0:T(8,128)(2,1)S(1)} %collective-permute-done.got_a, bf16[8,48,128]{2,1,0:T(8,128)(2,1)S(1)} %collective-permute-done.1.got_b, ...), custom_call_target="tpu_custom_call" | custom-call | flops 600000000 | bytes 679936 | tf_op jit(solution)/shard_map/pallas_call | solution.py:30
  9.1 4.7 %collective-permute-done.3.got_far = bf16[3,224,128]{2,1,0:T(8,128)(2,1)S(1)} collective-permute-done((bf16[3,224,128]{2,1,0:T(8,128)(2,1)S(1)}, bf16[3,224,128]{2,1,0:T(8,128)(2,1)S(1)}, u32[]{:S(2)}, u32[]{:S(2)}) %collective-permute-start.3) | collective-permute-done | bytes 172064 | tf_op jit(solution)/shard_map/ppermute | solution.py:371
  13.7 1.9 %shard_map.50.refs_0_ = bf16[64,128]{1,0:T(8,128)(2,1)S(1)} custom-call(bf16[3,8,288,128]{3,2,1,0:T(8,128)(2,1)S(1)} %get-tuple-element.24.taps, bf16[2,192,128]{2,1,0:T(8,128)(2,1)S(1)} %get-tuple-element.25.pooled_in, f32[2,3,128,256]{3,2,1,0:T(8,128)S(1)} %get-tuple-element.26.partial, bf16[3,224,128]{2,1,0:T(8,128)(2,1)S(1)} %collective-permute-done.2.got_mate, ...), custom_call_target="tpu_custom_call" | custom-call | flops 800000000 | bytes 4505600 | tf_op jit(solution)/shard_map/pallas_call | solution.py:30
  15.7 3.1 %collective-permute-start.4 = (bf16[64,128]{1,0:T(8,128)(2,1)S(1)}, bf16[64,128]{1,0:T(8,128)(2,1)S(1)}, u32[]{:S(2)}, u32[]{:S(2)}) collective-permute-start(bf16[64,128]{1,0:T(8,128)(2,1)S(1)} %shard_map.50.refs_0_), channel_id=1, source_target_pairs={{0,1},{1,0},{2,3},{3,2},{4,5},{5,4},{6,7},{7,6},{8,9},{9,8},{10,11... | collective-permute-start | bytes 49160 | tf_op jit(solution)/shard_map/ppermute | solution.py:408
  18.8 0.8 %collective-permute-start.5 = (bf16[64,128]{1,0:T(8,128)(2,1)S(1)}, bf16[64,128]{1,0:T(8,128)(2,1)S(1)}, u32[]{:S(2)}, u32[]{:S(2)}) collective-permute-start(bf16[64,128]{1,0:T(8,128)(2,1)S(1)} %shard_map.50.refs_0_), channel_id=1, source_target_pairs={{0,2},{1,3},{2,0},{3,1},{4,6},{5,7},{6,4},{7,5},{8,10},{9,11},{10,... | collective-permute-start | bytes 49160 | tf_op jit(solution)/shard_map/ppermute | solution.py:408
  19.6 1.7 %collective-permute-start.6 = (bf16[64,128]{1,0:T(8,128)(2,1)S(1)}, bf16[64,128]{1,0:T(8,128)(2,1)S(1)}, u32[]{:S(2)}, u32[]{:S(2)}) collective-permute-start(bf16[64,128]{1,0:T(8,128)(2,1)S(1)} %shard_map.50.refs_0_), channel_id=1, source_target_pairs={{0,3},{1,2},{2,1},{3,0},{4,7},{5,6},{6,5},{7,4},{8,11},{9,10},{10,... | collective-permute-start | bytes 49160 | tf_op jit(solution)/shard_map/ppermute | solution.py:408
  21.3 2.2 %collective-permute-done.5.refs_2_ = bf16[64,128]{1,0:T(8,128)(2,1)S(1)} collective-permute-done((bf16[64,128]{1,0:T(8,128)(2,1)S(1)}, bf16[64,128]{1,0:T(8,128)(2,1)S(1)}, u32[]{:S(2)}, u32[]{:S(2)}) %collective-permute-start.5) | collective-permute-done | bytes 16416 | tf_op jit(solution)/shard_map/ppermute | solution.py:408
  23.5 1.7 %collective-permute-done.6.refs_3_ = bf16[64,128]{1,0:T(8,128)(2,1)S(1)} collective-permute-done((bf16[64,128]{1,0:T(8,128)(2,1)S(1)}, bf16[64,128]{1,0:T(8,128)(2,1)S(1)}, u32[]{:S(2)}, u32[]{:S(2)}) %collective-permute-start.6) | collective-permute-done | bytes 16416 | tf_op jit(solution)/shard_map/ppermute | solution.py:408
  25.2 0.1 shard_map.51
  25.3 0.1 collective-permute-start.7
  25.4 0.2 constant_dynamic-slice_fusion
  25.6 0.2 copy.6.w3
  25.8 0.4 %shard_map.52.partial = f32[2,32,256]{2,1,0:T(8,128)S(1)} custom-call(bf16[64,256]{1,0:T(8,128)(2,1)S(1)} %get-tuple-element.33.mate, bf16[64,256]{1,0:T(8,128)(2,1)S(1)} %get-tuple-element.34.far, bf16[32,1728]{1,0:T(8,128)(2,1)S(1)} %copy.6.w3), custom_call_target="tpu_custom_call" | custom-call | flops 37748736 | bytes 176128 | tf_op jit(solution)/shard_map/pallas_call | solution.py:30
  26.2 0.4 %collective-permute-done.7.got_mate = bf16[64,256]{1,0:T(8,128)(2,1)S(1)} collective-permute-done((bf16[64,256]{1,0:T(8,128)(2,1)S(1)}, bf16[64,256]{1,0:T(8,128)(2,1)S(1)}, u32[]{:S(2)}, u32[]{:S(2)}) %collective-permute-start.7) | collective-permute-done | bytes 32800 | tf_op jit(solution)/shard_map/ppermute | solution.py:413
  26.5 3.1 %collective-permute-done.8.got_far = bf16[64,256]{1,0:T(8,128)(2,1)S(1)} collective-permute-done((bf16[64,256]{1,0:T(8,128)(2,1)S(1)}, bf16[64,256]{1,0:T(8,128)(2,1)S(1)}, u32[]{:S(2)}, u32[]{:S(2)}) %collective-permute-start.8) | collective-permute-done | bytes 32800 | tf_op jit(solution)/shard_map/ppermute | solution.py:412
  29.6 1.0 %shard_map.53 = bf16[32,2,256]{2,1,0:T(2,128)(2,1)} custom-call(f32[2,32,256]{2,1,0:T(8,128)S(1)} %shard_map.52.partial, bf16[64,256]{1,0:T(8,128)(2,1)S(1)} %collective-permute-done.7.got_mate, bf16[64,256]{1,0:T(8,128)(2,1)S(1)} %collective-permute-done.8.got_far, bf16[32,1728]{1,0:T(8,128)(2,1)S(1)} %copy.6.w3), custom_call_target="tpu_custom_call" | custom-call | flops 18874368 | bytes 241664 | tf_op jit(solution)/shard_map/pallas_call | solution.py:30
  (12 shorter events, 0.2 us)
Async XLA Ops:
  0.0 25.4 %copy-start = (bf16[128,1728]{0,1:T(8,128)(2,1)S(1)}, bf16[128,1728]{0,1:T(8,128)(2,1)}, u32[]{:S(2)}) copy-start(bf16[128,1728]{0,1:T(8,128)(2,1)} %param.7) | copy-start | bytes 1327108
  0.0 1.0 %copy-start.1 = (bf16[8,16,8,128]{3,2,1,0:T(8,128)(2,1)S(1)}, bf16[8,16,8,128]{3,2,1,0:T(8,128)(2,1)}, u32[]{:S(2)}) copy-start(bf16[8,16,8,128]{3,2,1,0:T(8,128)(2,1)} %vol.1) | copy-start | bytes 786436
  1.2 5.0 %collective-permute-start = (bf16[8,48,128]{2,1,0:T(8,128)(2,1)S(1)}, bf16[8,48,128]{2,1,0:T(8,128)(2,1)S(1)}, u32[]{:S(2)}, u32[]{:S(2)}) collective-permute-start(bf16[8,48,128]{2,1,0:T(8,128)(2,1)S(1)} %get-tuple-element.21), channel_id=1, source_target_pairs={{0,1},{1,0},{2,3},{3,2},{4,5},{5,4},{6,7},{7,6},{8,9},{9,8},{10,11... | collective-permute-start | bytes 294920 | tf_op jit(solution)/shard_map/ppermute | solution.py:340
  2.9 3.3 %collective-permute-start.1 = (bf16[8,48,128]{2,1,0:T(8,128)(2,1)S(1)}, bf16[8,48,128]{2,1,0:T(8,128)(2,1)S(1)}, u32[]{:S(2)}, u32[]{:S(2)}) collective-permute-start(bf16[8,48,128]{2,1,0:T(8,128)(2,1)S(1)} %get-tuple-element.22), channel_id=1, source_target_pairs={{0,4},{1,2},{2,1},{3,7},{4,0},{5,6},{6,5},{7,3},{8,12},{9,10},{10,... | collective-permute-start | bytes 294920 | tf_op jit(solution)/shard_map/ppermute | solution.py:339
  2.9 0.9 %copy-start.2 = (bf16[64,864]{1,0:T(8,128)(2,1)S(1)}, bf16[64,864]{1,0:T(8,128)(2,1)}, u32[]{:S(2)}) copy-start(bf16[64,864]{1,0:T(8,128)(2,1)} %w2_hbm.1) | copy-start | bytes 331780
  3.8 0.8 %copy-start.3 = (bf16[32,432]{1,0:T(8,128)(2,1)S(1)}, bf16[32,432]{1,0:T(8,128)(2,1)}, u32[]{:S(2)}) copy-start(bf16[32,432]{1,0:T(8,128)(2,1)} %w1_hbm.1) | copy-start | bytes 82948
  6.3 2.8 %collective-permute-start.2 = (bf16[3,224,128]{2,1,0:T(8,128)(2,1)S(1)}, bf16[3,224,128]{2,1,0:T(8,128)(2,1)S(1)}, u32[]{:S(2)}, u32[]{:S(2)}) collective-permute-start(bf16[3,224,128]{2,1,0:T(8,128)(2,1)S(1)} %get-tuple-element.28), channel_id=1, source_target_pairs={{0,4},{1,5},{2,6},{3,7},{4,0},{5,1},{6,2},{7,3},{8,12},{9,13},{10,... | collective-permute-start | bytes 516104 | tf_op jit(solution)/shard_map/ppermute | solution.py:372
  6.9 6.9 %collective-permute-start.3 = (bf16[3,224,128]{2,1,0:T(8,128)(2,1)S(1)}, bf16[3,224,128]{2,1,0:T(8,128)(2,1)S(1)}, u32[]{:S(2)}, u32[]{:S(2)}) collective-permute-start(bf16[3,224,128]{2,1,0:T(8,128)(2,1)S(1)} %get-tuple-element.29), channel_id=1, source_target_pairs={{0,1},{1,0},{2,3},{3,2},{4,8},{5,9},{6,10},{7,11},{8,4},{9,5},{10,... | collective-permute-start | bytes 516104 | tf_op jit(solution)/shard_map/ppermute | solution.py:371
  15.7 5.6 %collective-permute-start.4 = (bf16[64,128]{1,0:T(8,128)(2,1)S(1)}, bf16[64,128]{1,0:T(8,128)(2,1)S(1)}, u32[]{:S(2)}, u32[]{:S(2)}) collective-permute-start(bf16[64,128]{1,0:T(8,128)(2,1)S(1)} %shard_map.50.refs_0_), channel_id=1, source_target_pairs={{0,1},{1,0},{2,3},{3,2},{4,5},{5,4},{6,7},{7,6},{8,9},{9,8},{10,11... | collective-permute-start | bytes 49160 | tf_op jit(solution)/shard_map/ppermute | solution.py:408
  18.8 4.6 %collective-permute-start.5 = (bf16[64,128]{1,0:T(8,128)(2,1)S(1)}, bf16[64,128]{1,0:T(8,128)(2,1)S(1)}, u32[]{:S(2)}, u32[]{:S(2)}) collective-permute-start(bf16[64,128]{1,0:T(8,128)(2,1)S(1)} %shard_map.50.refs_0_), channel_id=1, source_target_pairs={{0,2},{1,3},{2,0},{3,1},{4,6},{5,7},{6,4},{7,5},{8,10},{9,11},{10,... | collective-permute-start | bytes 49160 | tf_op jit(solution)/shard_map/ppermute | solution.py:408
  19.6 5.5 %collective-permute-start.6 = (bf16[64,128]{1,0:T(8,128)(2,1)S(1)}, bf16[64,128]{1,0:T(8,128)(2,1)S(1)}, u32[]{:S(2)}, u32[]{:S(2)}) collective-permute-start(bf16[64,128]{1,0:T(8,128)(2,1)S(1)} %shard_map.50.refs_0_), channel_id=1, source_target_pairs={{0,3},{1,2},{2,1},{3,0},{4,7},{5,6},{6,5},{7,4},{8,11},{9,10},{10,... | collective-permute-start | bytes 49160 | tf_op jit(solution)/shard_map/ppermute | solution.py:408
  25.3 1.3 %collective-permute-start.7 = (bf16[64,256]{1,0:T(8,128)(2,1)S(1)}, bf16[64,256]{1,0:T(8,128)(2,1)S(1)}, u32[]{:S(2)}, u32[]{:S(2)}) collective-permute-start(bf16[64,256]{1,0:T(8,128)(2,1)S(1)} %get-tuple-element.33.mate), channel_id=1, source_target_pairs={{0,4},{1,5},{2,6},{3,7},{4,0},{5,1},{6,2},{7,3},{8,12},{9,13},{10,... | collective-permute-start | bytes 98312 | tf_op jit(solution)/shard_map/ppermute | solution.py:413
  25.3 4.3 %collective-permute-start.8 = (bf16[64,256]{1,0:T(8,128)(2,1)S(1)}, bf16[64,256]{1,0:T(8,128)(2,1)S(1)}, u32[]{:S(2)}, u32[]{:S(2)}) collective-permute-start(bf16[64,256]{1,0:T(8,128)(2,1)S(1)} %get-tuple-element.34.far), channel_id=1, source_target_pairs={{0,1},{1,0},{2,3},{3,2},{4,8},{5,9},{6,10},{7,11},{8,4},{9,5},{10,... | collective-permute-start | bytes 98312 | tf_op jit(solution)/shard_map/ppermute | solution.py:412

commit v3 on v2

--- a/solution.py
+++ b/solution.py
@@ -25,12 +25,13 @@
     return lax.broadcasted_iota(jnp.int32, shape, dim)
 
 
-def call(body, outs, *args, scratch=(), flops=0, space=pltpu.VMEM):
+def call(body, outs, *args, scratch=(), flops=0, hbm=()):
     moved = sum(a.size * a.dtype.itemsize for a in args)
+    args = [pltpu.with_memory_space_constraint(a, pltpu.HBM) if i in hbm else a for i, a in enumerate(args)]
     return pl.pallas_call(
         body,
         out_shape=[jax.ShapeDtypeStruct(s, d) for s, d in outs],
-        in_specs=[pl.BlockSpec(memory_space=space)] * len(args),
+        in_specs=[pl.BlockSpec(memory_space=pltpu.HBM if i in hbm else pltpu.VMEM) for i in range(len(args))],
         out_specs=[WHOLE] * len(outs),
         scratch_shapes=list(scratch),
         compiler_params=pltpu.CompilerParams(vmem_limit_bytes=40 * 1024 * 1024),
@@ -114,7 +115,6 @@
     loads = [pltpu.make_async_copy(a, b, sems.at[i]) for i, (a, b) in enumerate(((w1_hbm, w1), (w2_hbm, w2)))]
     for load in loads:
         load.start()
-
     rows, columns = z_sel.shape
     breadth = rows // 2
     r, c = iota(z_sel.shape, 0), iota(z_sel.shape, 1)
@@ -136,15 +136,15 @@
     for w, band, last in ((w1, band1, band1_last), (w2, band2, None)):
         out_rows, columns = w.shape[0], band.shape[1]
         chans = w.shape[1] // 27
-        col = iota((1, columns), 1)
+        col = iota((1, columns // 3), 1)
         block = col // chans
-        row, group = block % 6, block // 6
-        source = ((group // 3 * 3 + row) * 3 + group % 3) * chans + col % chans
-        source = jnp.where(row < 3, source, -1)
-        sel = (iota((w.shape[1], columns), 0) == source).astype(F32).astype(BF)
-        base = mat(w[...], sel)
+        row, tap = block % 6, block // 6
+        source = jnp.where(row < 3, (row * 3 + tap) * chans + col % chans, -1)
+        sel = (iota((9 * chans, columns // 3), 0) == source).astype(F32).astype(BF)
+        taps = w[...]
+        base = [mat(taps[:, a * 9 * chans : (a + 1) * 9 * chans], sel) for a in range(3)]
         wide = -(-columns // 128) * 128
-        base = jnp.pad(base, ((0, 0), (0, wide - columns)))
+        base = jnp.concatenate(base + [jnp.zeros((out_rows, wide - columns), F32)], 1)
         for y in range(4):
             moved = base if y == 0 else pltpu.roll(base, y * chans, 1)
             rows = slice(out_rows * y, out_rows * (y + 1))
@@ -185,7 +185,9 @@
     return jnp.concatenate(halves, 0).astype(BF)
 
 
-def inner_kernel(turned, got_a, got_b, band1, taps, pooled, partial):
+def inner_kernel(turned, got_a, got_b, band1, w3_hbm, taps, pooled, partial, picked, w3, sem):
+    load = pltpu.make_async_copy(w3_hbm, w3, sem)
+    load.start()
     planes, rows, breadth = turned.shape
     chans = got_a.shape[1] // HALO
     for x in range(planes):
@@ -212,6 +214,11 @@
             else:
                 half = pooled.shape[1] // 3
                 pooled[p - 1, part * half : (part + 1) * half] = pool_first(acc, part, False)
+    load.wait()
+    own = (picked.shape[0], w3.shape[1])
+    first = lax.axis_index("yz") * own[0]
+    pick = (iota(own, 1) == iota(own, 0) + first).astype(F32).astype(BF)
+    picked[...] = lax.dot_general(pick, w3[...], (((1,), (1,)), ((), ())), preferred_element_type=F32).astype(BF)
 
 
 def outer_kernel(
@@ -355,8 +362,8 @@
             pltpu.VMEM(weight_two.shape, BF),
             pltpu.SemaphoreType.DMA((2,)),
         ],
+        hbm=(0, 1),
         flops=2 * 64 * 864 * 1728,
-        space=pltpu.HBM,
     )
     ext = rows + 2 * edge
     send_mate, send_far = call(
@@ -371,17 +378,22 @@
     got_far = lax.ppermute(send_far, ("gx", "yz"), away)
     got_mate = lax.ppermute(send_mate, ("gx", "yz"), near)
     pairs = planes // 2 + 2
-    taps, pooled, partial = call(
+    out_rows = weight_three.shape[0] // yz
+    taps, pooled, partial, picked = call(
         inner_kernel,
         [
             ((3, planes, 18 * chans, breadth), BF),
             ((pairs - 4, 6 * c2, breadth), BF),
             ((2, 3, 4 * c2, 2 * breadth), F32),
+            ((out_rows, weight_three.shape[1]), BF),
         ],
         turned,
         got_a,
         got_b,
         band1,
+        weight_three.T,
+        scratch=[pltpu.VMEM(weight_three.shape[::-1], BF), pltpu.SemaphoreType.DMA],
+        hbm=(4,),
         flops=2 * 300_000_000,
     )
     (tile,) = call(
@@ -411,8 +423,6 @@
     mate, far = call(lay_kernel, [((c3, cells), BF), ((c3, cells), BF)], *tiles)
     got_far = lax.ppermute(far, ("gx", "yz"), away)
     got_mate = lax.ppermute(mate, ("gx", "yz"), near)
-    out_rows = weight_three.shape[0] // yz
-    picked = lax.dynamic_slice_in_dim(weight_three, lax.axis_index("yz") * out_rows, out_rows, 0)
     (partial,) = call(
         functools.partial(middle_kernel, z),
         [((2, out_rows, cells), F32)],

time: 30.9 us -> 29.2 us (0.945)
  local copies, waits for them, and re-layouts: 3.04 us -> 0.95 us
  waiting for transfers between devices: 12 us -> 12.8 us
  starting transfers between devices: 9.06 us -> 8.44 us
  Pallas kernels: 6.44 us -> 6.79 us
    unnamed x9 -> x2, local copies, waits for them, and re-layouts: 2.85 us -> 0.95 us
    ppermute x1, waiting for transfers between devices: 0.01 us -> 1.33 us  [per_device(): got_a = lax.ppermute(send_a, ('gx', 'yz'), yz_pairs(gx, yz, False))]
    ppermute x1, waiting for transfers between devices: 4.66 us -> 4.09 us  [per_device(): got_far = lax.ppermute(send_far, ('gx', 'yz'), away)]
    ppermute x3, starting transfers between devices: 5.58 us -> 5.05 us  [per_device(): lax.ppermute(tile, 'yz', [(i, i ^ d) for i in range(yz)])]
    ppermute x1, starting transfers between devices: 0.57 us -> 0.07 us  [per_device(): got_mate = lax.ppermute(send_mate, ('gx', 'yz'), near)]
    ppermute x1, starting transfers between devices: 1.12 us -> 1.53 us  [per_device(): got_far = lax.ppermute(send_far, ('gx', 'yz'), away)]
    ppermute x1, waiting for transfers between devices: 0.36 us -> 0.75 us  [per_device(): got_mate = lax.ppermute(mate, ('gx', 'yz'), near)]
    ppermute x3, waiting for transfers between devices: 3.88 us -> 3.5 us  [per_device(): lax.ppermute(tile, 'yz', [(i, i ^ d) for i in range(yz)])]
  transfers between devices with their start and end apart: 9 -> 9, of which waited for: 5 -> 6; matrix products, arithmetic and copies ran while one was open for 1% -> 0% of each run, Pallas kernels for 10% -> 12%
where the time goes in v3:
time: 29.2 us; the launch traced here: 29.1 us
  waiting for transfers between devices  12.8 us (44%)
  starting transfers between devices  8.44 us (29%)
  Pallas kernels  6.79 us (23%)
  local copies, waits for them, and re-layouts  0.95 us (3%)
    pallas_call x8, Pallas kernels, call(): pl.pallas_call(body, out_shape=[jax.ShapeDtypeStruct(s, d) for s, d in ou...  6.79 us
    ppermute x3, starting transfers between devices, per_device(): lax.ppermute(tile, 'yz', [(i, i ^ d) for i in range(yz)])  5.05 us
    ppermute x1, waiting for transfers between devices, per_device(): got_far = lax.ppermute(send_far, ('gx', 'yz'), away)  4.09 us
    ppermute x3, waiting for transfers between devices, per_device(): lax.ppermute(tile, 'yz', [(i, i ^ d) for i in range(yz)])  3.5 us
    ppermute x1, waiting for transfers between devices, per_device(): got_far = lax.ppermute(far, ('gx', 'yz'), away)  3.11 us
    ppermute x1, starting transfers between devices, per_device(): got_a = lax.ppermute(send_a, ('gx', 'yz'), yz_pairs(gx, yz, False))  1.64 us
    ppermute x1, starting transfers between devices, per_device(): got_far = lax.ppermute(send_far, ('gx', 'yz'), away)  1.53 us
    ppermute x1, waiting for transfers between devices, per_device(): got_a = lax.ppermute(send_a, ('gx', 'yz'), yz_pairs(gx, yz, False))  1.33 us
  transfers between devices with their start and end apart: 9, of which 6 were waited for; matrix products, arithmetic and copies ran while one was open for 0% of the time, Pallas kernels for 12%

profile of v3, /device:TPU:4, one launch (start us, length us, event | category | flops | bytes accessed | tf_op | source)
XLA Modules:
  0.0 29.1 jit_solution(8712911076839400939)
XLA Ops:
  0.0 0.9 %copy-done = bf16[8,16,8,128]{3,2,1,0:T(8,128)(2,1)S(1)} copy-done((bf16[8,16,8,128]{3,2,1,0:T(8,128)(2,1)S(1)}, bf16[8,16,8,128]{3,2,1,0:T(8,128)(2,1)}, u32[]{:S(2)}) %copy-start) | copy-done | bytes 262168
  1.0 0.2 shard_map.46
  1.2 1.6 %collective-permute-start = (bf16[8,48,128]{2,1,0:T(8,128)(2,1)S(1)}, bf16[8,48,128]{2,1,0:T(8,128)(2,1)S(1)}, u32[]{:S(2)}, u32[]{:S(2)}) collective-permute-start(bf16[8,48,128]{2,1,0:T(8,128)(2,1)S(1)} %get-tuple-element.22), channel_id=1, source_target_pairs={{0,1},{1,0},{2,3},{3,2},{4,5},{5,4},{6,7},{7,6},{8,9},{9,8},{10,11... | collective-permute-start | bytes 294920 | tf_op jit(solution)/shard_map/ppermute | solution.py:347
  2.8 0.0 collective-permute-start.1
  2.8 1.7 %shard_map.47 = (bf16[128,864]{1,0:T(8,128)(2,1)S(1)}, bf16[128,288]{1,0:T(8,128)(2,1)S(1)}, bf16[256,1728]{1,0:T(8,128)(2,1)S(1)}, bf16[256,384]{1,0:T(8,128)(2,1)S(1)}, bf16[512,128]{1,0:T(8,128)(2,1)S(1)}) custom-call(bf16[32,432]{1,0:T(8,128)(2,1)} %w1_hbm.1, bf16[64,864]{1,0:T(8,128)(2,1)} %w2_hbm.1), custom_call_target="tpu_custom_call" | custom-call | flops 191102976 | bytes 138240 | tf_op jit(solution)/shard_map/pallas_call | solution.py:31
  4.5 1.3 %collective-permute-done.got_a = bf16[8,48,128]{2,1,0:T(8,128)(2,1)S(1)} collective-permute-done((bf16[8,48,128]{2,1,0:T(8,128)(2,1)S(1)}, bf16[8,48,128]{2,1,0:T(8,128)(2,1)S(1)}, u32[]{:S(2)}, u32[]{:S(2)}) %collective-permute-start) | collective-permute-done | bytes 98336 | tf_op jit(solution)/shard_map/ppermute | solution.py:347
  5.9 0.0 collective-permute-done.1.got_b
  5.9 0.1 collective-permute-start.2
  6.0 1.5 %collective-permute-start.3 = (bf16[3,224,128]{2,1,0:T(8,128)(2,1)S(1)}, bf16[3,224,128]{2,1,0:T(8,128)(2,1)S(1)}, u32[]{:S(2)}, u32[]{:S(2)}) collective-permute-start(bf16[3,224,128]{2,1,0:T(8,128)(2,1)S(1)} %get-tuple-element.30), channel_id=1, source_target_pairs={{0,1},{1,0},{2,3},{3,2},{4,8},{5,9},{6,10},{7,11},{8,4},{9,5},{10,... | collective-permute-start | bytes 516104 | tf_op jit(solution)/shard_map/ppermute | solution.py:378
  7.5 1.4 %shard_map.48 = (bf16[3,8,288,128]{3,2,1,0:T(8,128)(2,1)S(1)}, bf16[2,192,128]{2,1,0:T(8,128)(2,1)S(1)}, f32[2,3,128,256]{3,2,1,0:T(8,128)S(1)}, bf16[32,1728]{1,0:T(8,128)(2,1)S(1)}) custom-call(bf16[8,128,128]{2,1,0:T(8,128)(2,1)S(1)} %get-tuple-element.21.turned, bf16[8,48,128]{2,1,0:T(8,128)(2,1)S(1)} %collective-permute-done.got_a, ...), custom_call_target="tpu_custom_call" | custom-call | flops 600000000 | bytes 1122304 | tf_op jit(solution)/shard_map/pallas_call | solution.py:31
  9.0 4.1 %collective-permute-done.3.got_far = bf16[3,224,128]{2,1,0:T(8,128)(2,1)S(1)} collective-permute-done((bf16[3,224,128]{2,1,0:T(8,128)(2,1)S(1)}, bf16[3,224,128]{2,1,0:T(8,128)(2,1)S(1)}, u32[]{:S(2)}, u32[]{:S(2)}) %collective-permute-start.3) | collective-permute-done | bytes 172064 | tf_op jit(solution)/shard_map/ppermute | solution.py:378
  13.0 1.9 %shard_map.50.refs_0_ = bf16[64,128]{1,0:T(8,128)(2,1)S(1)} custom-call(bf16[3,8,288,128]{3,2,1,0:T(8,128)(2,1)S(1)} %get-tuple-element.25.taps, bf16[2,192,128]{2,1,0:T(8,128)(2,1)S(1)} %get-tuple-element.26.pooled_in, f32[2,3,128,256]{3,2,1,0:T(8,128)S(1)} %get-tuple-element.27.partial, bf16[3,224,128]{2,1,0:T(8,128)(2,1)S(1)} %collective-permute-done.2.got_mate, ...), custom_call_target="tpu_custom_call" | custom-call | flops 800000000 | bytes 4505600 | tf_op jit(solution)/shard_map/pallas_call | solution.py:31
  15.0 3.9 %collective-permute-start.6 = (bf16[64,128]{1,0:T(8,128)(2,1)S(1)}, bf16[64,128]{1,0:T(8,128)(2,1)S(1)}, u32[]{:S(2)}, u32[]{:S(2)}) collective-permute-start(bf16[64,128]{1,0:T(8,128)(2,1)S(1)} %shard_map.50.refs_0_), channel_id=1, source_target_pairs={{0,3},{1,2},{2,1},{3,0},{4,7},{5,6},{6,5},{7,4},{8,11},{9,10},{10,... | collective-permute-start | bytes 49160 | tf_op jit(solution)/shard_map/ppermute | solution.py:420
  18.9 0.6 %collective-permute-start.5 = (bf16[64,128]{1,0:T(8,128)(2,1)S(1)}, bf16[64,128]{1,0:T(8,128)(2,1)S(1)}, u32[]{:S(2)}, u32[]{:S(2)}) collective-permute-start(bf16[64,128]{1,0:T(8,128)(2,1)S(1)} %shard_map.50.refs_0_), channel_id=1, source_target_pairs={{0,2},{1,3},{2,0},{3,1},{4,6},{5,7},{6,4},{7,5},{8,10},{9,11},{10,... | collective-permute-start | bytes 49160 | tf_op jit(solution)/shard_map/ppermute | solution.py:420
  19.6 0.5 %collective-permute-start.4 = (bf16[64,128]{1,0:T(8,128)(2,1)S(1)}, bf16[64,128]{1,0:T(8,128)(2,1)S(1)}, u32[]{:S(2)}, u32[]{:S(2)}) collective-permute-start(bf16[64,128]{1,0:T(8,128)(2,1)S(1)} %shard_map.50.refs_0_), channel_id=1, source_target_pairs={{0,1},{1,0},{2,3},{3,2},{4,5},{5,4},{6,7},{7,6},{8,9},{9,8},{10,11... | collective-permute-start | bytes 49160 | tf_op jit(solution)/shard_map/ppermute | solution.py:420
  20.0 0.7 %collective-permute-done.6.refs_3_ = bf16[64,128]{1,0:T(8,128)(2,1)S(1)} collective-permute-done((bf16[64,128]{1,0:T(8,128)(2,1)S(1)}, bf16[64,128]{1,0:T(8,128)(2,1)S(1)}, u32[]{:S(2)}, u32[]{:S(2)}) %collective-permute-start.6) | collective-permute-done | bytes 16416 | tf_op jit(solution)/shard_map/ppermute | solution.py:420
  20.7 2.8 %collective-permute-done.5.refs_2_ = bf16[64,128]{1,0:T(8,128)(2,1)S(1)} collective-permute-done((bf16[64,128]{1,0:T(8,128)(2,1)S(1)}, bf16[64,128]{1,0:T(8,128)(2,1)S(1)}, u32[]{:S(2)}, u32[]{:S(2)}) %collective-permute-start.5) | collective-permute-done | bytes 16416 | tf_op jit(solution)/shard_map/ppermute | solution.py:420
  23.5 0.1 shard_map.51
  23.6 0.1 collective-permute-start.7
  23.7 0.1 collective-permute-start.8
  23.8 0.4 %shard_map.52.partial = f32[2,32,256]{2,1,0:T(8,128)S(1)} custom-call(bf16[64,256]{1,0:T(8,128)(2,1)S(1)} %get-tuple-element.34.mate, bf16[64,256]{1,0:T(8,128)(2,1)S(1)} %get-tuple-element.35.far, bf16[32,1728]{1,0:T(8,128)(2,1)S(1)} %get-tuple-element.36.w3), custom_call_target="tpu_custom_call" | custom-call | flops 37748736 | bytes 176128 | tf_op jit(solution)/shard_map/pallas_call | solution.py:31
  24.2 0.8 %collective-permute-done.7.got_mate = bf16[64,256]{1,0:T(8,128)(2,1)S(1)} collective-permute-done((bf16[64,256]{1,0:T(8,128)(2,1)S(1)}, bf16[64,256]{1,0:T(8,128)(2,1)S(1)}, u32[]{:S(2)}, u32[]{:S(2)}) %collective-permute-start.7) | collective-permute-done | bytes 32800 | tf_op jit(solution)/shard_map/ppermute | solution.py:425
  24.9 3.1 %collective-permute-done.8.got_far = bf16[64,256]{1,0:T(8,128)(2,1)S(1)} collective-permute-done((bf16[64,256]{1,0:T(8,128)(2,1)S(1)}, bf16[64,256]{1,0:T(8,128)(2,1)S(1)}, u32[]{:S(2)}, u32[]{:S(2)}) %collective-permute-start.8) | collective-permute-done | bytes 32800 | tf_op jit(solution)/shard_map/ppermute | solution.py:424
  28.0 1.0 %shard_map.53 = bf16[32,2,256]{2,1,0:T(2,128)(2,1)} custom-call(f32[2,32,256]{2,1,0:T(8,128)S(1)} %shard_map.52.partial, bf16[64,256]{1,0:T(8,128)(2,1)S(1)} %collective-permute-done.7.got_mate, bf16[64,256]{1,0:T(8,128)(2,1)S(1)} %collective-permute-done.8.got_far, bf16[32,1728]{1,0:T(8,128)(2,1)S(1)} %get-tuple-element.36.w3), custom_call_target="tpu_custom_call" | custom-call | flops 18874368 | bytes 241664 | tf_op jit(solution)/shard_map/pallas_call | solution.py:31
  (4 shorter events, 0.1 us)
Async XLA Ops:
  0.0 0.9 %copy-start = (bf16[8,16,8,128]{3,2,1,0:T(8,128)(2,1)S(1)}, bf16[8,16,8,128]{3,2,1,0:T(8,128)(2,1)}, u32[]{:S(2)}) copy-start(bf16[8,16,8,128]{3,2,1,0:T(8,128)(2,1)} %vol.1) | copy-start | bytes 786436
  1.2 4.7 %collective-permute-start = (bf16[8,48,128]{2,1,0:T(8,128)(2,1)S(1)}, bf16[8,48,128]{2,1,0:T(8,128)(2,1)S(1)}, u32[]{:S(2)}, u32[]{:S(2)}) collective-permute-start(bf16[8,48,128]{2,1,0:T(8,128)(2,1)S(1)} %get-tuple-element.22), channel_id=1, source_target_pairs={{0,1},{1,0},{2,3},{3,2},{4,5},{5,4},{6,7},{7,6},{8,9},{9,8},{10,11... | collective-permute-start | bytes 294920 | tf_op jit(solution)/shard_map/ppermute | solution.py:347
  2.8 3.0 %collective-permute-start.1 = (bf16[8,48,128]{2,1,0:T(8,128)(2,1)S(1)}, bf16[8,48,128]{2,1,0:T(8,128)(2,1)S(1)}, u32[]{:S(2)}, u32[]{:S(2)}) collective-permute-start(bf16[8,48,128]{2,1,0:T(8,128)(2,1)S(1)} %get-tuple-element.23), channel_id=1, source_target_pairs={{0,4},{1,2},{2,1},{3,7},{4,0},{5,6},{6,5},{7,3},{8,12},{9,10},{10,... | collective-permute-start | bytes 294920 | tf_op jit(solution)/shard_map/ppermute | solution.py:346
  5.9 3.0 %collective-permute-start.2 = (bf16[3,224,128]{2,1,0:T(8,128)(2,1)S(1)}, bf16[3,224,128]{2,1,0:T(8,128)(2,1)S(1)}, u32[]{:S(2)}, u32[]{:S(2)}) collective-permute-start(bf16[3,224,128]{2,1,0:T(8,128)(2,1)S(1)} %get-tuple-element.29), channel_id=1, source_target_pairs={{0,4},{1,5},{2,6},{3,7},{4,0},{5,1},{6,2},{7,3},{8,12},{9,13},{10,... | collective-permute-start | bytes 516104 | tf_op jit(solution)/shard_map/ppermute | solution.py:379
  6.0 7.0 %collective-permute-start.3 = (bf16[3,224,128]{2,1,0:T(8,128)(2,1)S(1)}, bf16[3,224,128]{2,1,0:T(8,128)(2,1)S(1)}, u32[]{:S(2)}, u32[]{:S(2)}) collective-permute-start(bf16[3,224,128]{2,1,0:T(8,128)(2,1)S(1)} %get-tuple-element.30), channel_id=1, source_target_pairs={{0,1},{1,0},{2,3},{3,2},{4,8},{5,9},{6,10},{7,11},{8,4},{9,5},{10,... | collective-permute-start | bytes 516104 | tf_op jit(solution)/shard_map/ppermute | solution.py:378
  15.0 5.7 %collective-permute-start.6 = (bf16[64,128]{1,0:T(8,128)(2,1)S(1)}, bf16[64,128]{1,0:T(8,128)(2,1)S(1)}, u32[]{:S(2)}, u32[]{:S(2)}) collective-permute-start(bf16[64,128]{1,0:T(8,128)(2,1)S(1)} %shard_map.50.refs_0_), channel_id=1, source_target_pairs={{0,3},{1,2},{2,1},{3,0},{4,7},{5,6},{6,5},{7,4},{8,11},{9,10},{10,... | collective-permute-start | bytes 49160 | tf_op jit(solution)/shard_map/ppermute | solution.py:420
  18.9 4.6 %collective-permute-start.5 = (bf16[64,128]{1,0:T(8,128)(2,1)S(1)}, bf16[64,128]{1,0:T(8,128)(2,1)S(1)}, u32[]{:S(2)}, u32[]{:S(2)}) collective-permute-start(bf16[64,128]{1,0:T(8,128)(2,1)S(1)} %shard_map.50.refs_0_), channel_id=1, source_target_pairs={{0,2},{1,3},{2,0},{3,1},{4,6},{5,7},{6,4},{7,5},{8,10},{9,11},{10,... | collective-permute-start | bytes 49160 | tf_op jit(solution)/shard_map/ppermute | solution.py:420
  19.6 4.0 %collective-permute-start.4 = (bf16[64,128]{1,0:T(8,128)(2,1)S(1)}, bf16[64,128]{1,0:T(8,128)(2,1)S(1)}, u32[]{:S(2)}, u32[]{:S(2)}) collective-permute-start(bf16[64,128]{1,0:T(8,128)(2,1)S(1)} %shard_map.50.refs_0_), channel_id=1, source_target_pairs={{0,1},{1,0},{2,3},{3,2},{4,5},{5,4},{6,7},{7,6},{8,9},{9,8},{10,11... | collective-permute-start | bytes 49160 | tf_op jit(solution)/shard_map/ppermute | solution.py:420
  23.6 1.3 %collective-permute-start.7 = (bf16[64,256]{1,0:T(8,128)(2,1)S(1)}, bf16[64,256]{1,0:T(8,128)(2,1)S(1)}, u32[]{:S(2)}, u32[]{:S(2)}) collective-permute-start(bf16[64,256]{1,0:T(8,128)(2,1)S(1)} %get-tuple-element.34.mate), channel_id=1, source_target_pairs={{0,4},{1,5},{2,6},{3,7},{4,0},{5,1},{6,2},{7,3},{8,12},{9,13},{10,... | collective-permute-start | bytes 98312 | tf_op jit(solution)/shard_map/ppermute | solution.py:425
  23.7 4.3 %collective-permute-start.8 = (bf16[64,256]{1,0:T(8,128)(2,1)S(1)}, bf16[64,256]{1,0:T(8,128)(2,1)S(1)}, u32[]{:S(2)}, u32[]{:S(2)}) collective-permute-start(bf16[64,256]{1,0:T(8,128)(2,1)S(1)} %get-tuple-element.35.far), channel_id=1, source_target_pairs={{0,1},{1,0},{2,3},{3,2},{4,8},{5,9},{6,10},{7,11},{8,4},{9,5},{10,... | collective-permute-start | bytes 98312 | tf_op jit(solution)/shard_map/ppermute | solution.py:424

commit v4 on v0

v4 whole, which is shorter than its diff:
```python
import functools

import jax
import jax.numpy as jnp
from jax import lax
from jax.experimental import pallas as pl
from jax.experimental.pallas import tpu as pltpu
from jax.sharding import PartitionSpec as P

BF = jnp.bfloat16
F32 = jnp.float32
WHOLE = pl.BlockSpec(memory_space=pltpu.VMEM)
PLANES = 2
HALO = 2 * PLANES - 1
EDGE = 3


def mat(a, b):
    return jnp.dot(a, b, preferred_element_type=F32)


def relu(a):
    return jnp.maximum(a, 0.0)


def iota(shape, dim):
    return lax.broadcasted_iota(jnp.int32, shape, dim)


def call(body, outs, *args, scratch=(), flops=0, hbm=()):
    moved = sum(a.size * a.dtype.itemsize for a in args)
    args = [pltpu.with_memory_space_constraint(a, pltpu.HBM) if i in hbm else a for i, a in enumerate(args)]
    return pl.pallas_call(
        body,
        out_shape=[jax.ShapeDtypeStruct(s, d) for s, d in outs],
        in_specs=[pl.BlockSpec(memory_space=pltpu.HBM if i in hbm else pltpu.VMEM) for i in range(len(args))],
        out_specs=[WHOLE] * len(outs),
        scratch_shapes=list(scratch),
        compiler_params=pltpu.CompilerParams(vmem_limit_bytes=40 * 1024 * 1024),
        cost_estimate=pl.CostEstimate(flops=flops, bytes_accessed=moved, transcendentals=0),
    )(*args)


def turn_kernel(vol, turned, send_mate, send_far):
    planes, chans, height, breadth = vol.shape
    rows = chans * height
    dest = iota((rows, rows), 0)
    source = (dest & (chans - 1)) * height + dest // chans
    swap = (iota((rows, rows), 1) == source).astype(F32).astype(BF)
    for x in range(planes):
        turned[x] = mat(swap, vol[x].reshape(rows, breadth)).astype(BF)
    even = is_even("gx")
    for out, first in (
        (send_mate, jnp.where(even, planes - HALO, 0)),
        (send_far, jnp.where(even, 0, planes - HALO)),
    ):
        for x in range(HALO):
            out[x] = turned[first + x]


def yz_pairs(gx, yz, second):
    pairs = []
    for g in range(gx):
        for k in range(yz):
            if not second:
                pairs.append((g * yz + k, g * yz + (k ^ 1)))
            elif k in (0, yz - 1):
                pairs.append((g * yz + k, (g ^ 1) * yz + k))
            else:
                pairs.append((g * yz + k, g * yz + (k + 1 if k % 2 else k - 1)))
    return pairs


def gx_pairs(gx, yz, far):
    pairs = []
    for g in range(gx):
        for k in range(yz):
            if not far:
                pairs.append((g * yz + k, (g ^ 1) * yz + k))
            elif g in (0, gx - 1):
                pairs.append((g * yz + k, g * yz + (k ^ 1)))
            else:
                pairs.append((g * yz + k, (g + 1 if g % 2 else g - 1) * yz + k))
    return pairs


def is_even(axis):
    return lax.rem(lax.axis_index(axis), 2) == 0


def from_sides(mate, far, even, no_low, no_high):
    zero = jnp.zeros_like(mate)
    low = jnp.where(no_low, zero, jnp.where(even, far, mate))
    high = jnp.where(no_high, zero, jnp.where(even, mate, far))
    return low, high


def all_planes(turned, got_mate, got_far):
    g = lax.axis_index("gx")
    even, first, last = is_even("gx"), g == 0, g == lax.axis_size("gx") - 1
    sides = [from_sides(got_mate[x], got_far[x], even, first, last) for x in range(HALO)]
    return [low for low, _ in sides] + [turned[x] for x in range(turned.shape[0])] + [high for _, high in sides]


def edge_kernel(turned, got_far, got_mate, _, send_a, send_b):
    edge = send_a.shape[1]
    even = is_even("yz")
    for x, t in enumerate(all_planes(turned, got_mate, got_far)):
        low, high = t[:edge], t[t.shape[0] - edge :]
        send_a[x] = jnp.where(even, high, low)
        send_b[x] = jnp.where(even, low, high)


def weights_kernel(w1_hbm, w2_hbm, lower1, upper1, middle2, outer2, z_sel, p_sel, w1, w2, sems):
    loads = [pltpu.make_async_copy(a, b, sems.at[i]) for i, (a, b) in enumerate(((w1_hbm, w1), (w2_hbm, w2)))]
    for load in loads:
        load.start()

    rows, columns = z_sel.shape
    breadth = rows // 2
    r, c = iota(z_sel.shape, 0), iota(z_sel.shape, 1)
    tap = c // breadth
    within = c - tap * breadth
    same = (r // breadth) == (within // (breadth // 2))
    cell = (r & (breadth - 1)) == 2 * ((within & (breadth // 2 - 1)) + tap - 1)
    z_sel[...] = jnp.where(same & cell, 1.0, 0.0).astype(BF)

    rows, columns = p_sel.shape
    z = rows // 8
    r, c = iota(p_sel.shape, 0), iota(p_sel.shape, 1)
    hit = (r // (4 * z) == (c // (z // 2)) % 2) & ((r // z) % 4 == 2 * (c // z))
    hit = hit & ((r & (z - 1)) == 2 * (c & (z // 2 - 1)))
    p_sel[...] = jnp.where(hit, 1.0, 0.0).astype(BF)

    for load in loads:
        load.wait()
    for w, bands in (
        (w1, ((lower1, lambda y: (0, 1, 2)), (upper1, lambda y: (3, 4, 5)))),
        (w2, ((middle2, lambda y: (2, 3)), (outer2, lambda y: (0, 1) if y < 2 else (4, 5)))),
    ):
        out_rows, width = w.shape[0], w.shape[1] // 9
        taps = w[...].astype(F32)
        zero = jnp.zeros((out_rows, width), F32)
        for band, window in bands:
            for y in range(4):
                pieces = []
                for a in range(3):
                    for row in window(y):
                        first = (3 * a + row - y) * width
                        pieces.append(taps[:, first : first + width] if 0 <= row - y < 3 else zero)
                band[out_rows * y : out_rows * (y + 1)] = jnp.concatenate(pieces, 1).astype(BF)


def put_taps(dest, t, chans):
    breadth = t.shape[1]
    lane = iota((1, breadth), 1)
    wide = t.astype(F32)
    before = jnp.where(lane == 0, 0.0, pltpu.roll(wide, 1, 1)).astype(BF)
    after = jnp.where(lane == breadth - 1, 0.0, pltpu.roll(wide, breadth - 1, 1)).astype(BF)
    for y in range(t.shape[0] // chans):
        for tap, value in enumerate((before, t, after)):
            row = (3 * y + tap) * chans
            dest[row : row + chans] = value[y * chans : (y + 1) * chans]


def three(taps, e, first, rows):
    return jnp.concatenate([taps[e + a, first : first + rows] for a in range(3)], 0)


def two_cells(taps, j, first, rows):
    return jnp.concatenate([three(taps, 2 * j, first, rows), three(taps, 2 * j + 1, first, rows)], 1)


def pool_first(acc, j, pairs, no_low, no_high):
    g = lax.axis_index("gx")
    breadth = acc.shape[1] // 2
    width = acc.shape[0] // 4
    r = relu(acc)
    s = r[:, :breadth] + r[:, breadth:]
    halves = []
    for y, drop in enumerate((no_low, no_high)):
        t = s[2 * y * width : (2 * y + 1) * width] + s[(2 * y + 1) * width : (2 * y + 2) * width]
        t = (t + pltpu.roll(t, breadth - 1, 1)) * 0.125
        if j < PLANES - 1:
            drop = drop | (g == 0)
        if j > pairs - PLANES:
            drop = drop | (g == lax.axis_size("gx") - 1)
        halves.append(t if drop is False else jnp.where(drop, 0.0, t))
    return jnp.concatenate(halves, 0).astype(BF)


def second_taps(pooled, z_sel):
    beside = [jnp.concatenate([a, b], 1) for a, b in zip(pooled[:-1], pooled[1:])]
    q = mat(jnp.concatenate(beside, 0), z_sel)
    breadth = q.shape[1] // 2
    before, here = q[:, :breadth], q[:, breadth:]
    lane = iota((1, breadth), 1)
    last = (lane & (breadth // 2 - 1)) == breadth // 2 - 1
    after = jnp.where(last, 0.0, pltpu.roll(here, breadth - 1, 1))
    taps = [t.astype(BF) for t in (before, here, after)]
    chans = pooled[0].shape[0] // 2
    planes = []
    for j in range(len(beside)):
        rows = [slice((2 * j + y) * chans, (2 * j + y + 1) * chans) for y in range(2)]
        planes.append([t[r] for r in rows for t in taps])
    columns = [jnp.concatenate(planes[j] + planes[j + 1] + planes[j + 2], 0) for j in range(0, len(planes) - 2, 2)]
    return jnp.concatenate(columns, 1)


def inner_kernel(
    turned, got_mate, got_far, lower1, upper1, middle2, z_sel, w3_hbm, partial1, partial2, picked, taps, w3, sem
):
    load = pltpu.make_async_copy(w3_hbm, w3, sem)
    load.start()
    chans = lower1.shape[1] // 27
    for e, t in enumerate(all_planes(turned, got_mate, got_far)):
        put_taps(taps.at[e], t, chans)
    pairs = partial1.shape[1]
    width = lower1.shape[0] // 4
    lower, upper = lower1[: 3 * width], upper1[width:]
    step = 3 * chans
    pooled = []
    zero = jnp.zeros((width, partial1.shape[3]), F32)
    for j in range(pairs):
        partial1[0, j, :width] = zero
        partial1[0, j, width:] = mat(upper, two_cells(taps, j, 0, 3 * step))
        partial1[1, j, : 3 * width] = mat(lower, two_cells(taps, j, 5 * step, 3 * step))
        partial1[1, j, 3 * width :] = zero
        a = mat(lower, two_cells(taps, j, step, 3 * step))
        b = mat(upper, two_cells(taps, j, 4 * step, 3 * step))
        acc = jnp.concatenate([a[:width], a[width:] + b[: 2 * width], b[2 * width :]], 0)
        pooled.append(pool_first(acc, j, pairs, False, False))
    partial2[...] = mat(middle2[...], second_taps(pooled, z_sel[...]))
    load.wait()
    out_rows = picked.shape[0] // 9
    own = (out_rows, w3.shape[1])
    first = lax.axis_index("yz") * out_rows
    pick = (iota(own, 1) == iota(own, 0) + first).astype(F32).astype(BF)
    own3 = lax.dot_general(pick, w3[...], (((1,), (1,)), ((), ())), preferred_element_type=F32)
    depth = picked.shape[1] // 3
    for tap in range(9):
        pieces = [own3[:, (9 * a + tap) * depth : (9 * a + tap + 1) * depth] for a in range(3)]
        picked[tap * out_rows : (tap + 1) * out_rows] = jnp.concatenate(pieces, 1)


def outer_kernel(got_a, got_b, partial1, partial2, lower1, upper1, outer2, z_sel, p_sel, out, low_taps, high_taps):
    planes, edge, breadth = got_a.shape
    chans = edge // EDGE
    k = lax.axis_index("yz")
    even, first, last = is_even("yz"), k == 0, k == lax.axis_size("yz") - 1
    for e in range(planes):
        low, high = from_sides(got_a[e], got_b[e], even, first, last)
        put_taps(low_taps.at[e], low, chans)
        put_taps(high_taps.at[e], high, chans)
    pairs = partial1.shape[1]
    width = lower1.shape[0] // 4
    lower, upper = lower1[: 3 * width], upper1[width:]
    rows = 3 * edge
    below, above = [], []
    for j in range(pairs):
        p = partial1[0, j]
        a = p[: 3 * width] + mat(lower, two_cells(low_taps, j, 0, rows))
        below.append(pool_first(jnp.concatenate([a, p[3 * width :]], 0), j, pairs, first, False))
        p = partial1[1, j]
        b = p[width:] + mat(upper, two_cells(high_taps, j, 0, rows))
        above.append(pool_first(jnp.concatenate([p[:width], b], 0), j, pairs, False, last))
    width = outer2.shape[0] // 4
    halves = []
    for y, pooled in enumerate((below, above)):
        part = slice(2 * y * width, 2 * (y + 1) * width)
        r = relu(partial2[part] + mat(outer2[part], second_taps(pooled, z_sel[...])))
        t = r[:width] + r[width:]
        cells = t.shape[1]
        t = t + pltpu.roll(t, cells - breadth // 2, 1)
        t = (t + pltpu.roll(t, cells - 1, 1)) * 0.125
        halves.append(t.astype(BF))
    for x in range(0, PLANES, 2):
        both = [t[:, x * breadth : (x + 2) * breadth] for t in halves]
        out[x // 2 * width : (x // 2 + 1) * width] = mat(jnp.concatenate(both, 1), p_sel[...]).astype(BF)


def lay(tiles, rows):
    even = is_even("yz")
    half = tiles[0].shape[1] // 2
    lane = iota((1, 2 * half), 1)
    tiles = [tiles[i] for i in [0, 3, 2, 1]]
    low, high = [], []
    for m in range(len(tiles) // 2):
        a, b = tiles[2 * m][rows].astype(F32), tiles[2 * m + 1][rows].astype(F32)
        first, second = jnp.where(even, a, b), jnp.where(even, b, a)
        low.append(jnp.where(lane < half, first, pltpu.roll(second, half, 1)))
        high.append(jnp.where(lane < half, pltpu.roll(first, half, 1), second))
    return low, high


def put_plane(dest, blocks):
    wide = blocks[0].shape[1]
    k = lax.axis_index("yz")
    for m, block in enumerate(blocks):
        dest[:, pl.ds(pl.multiple_of((lax.div(k, 2) ^ m) * wide, wide), wide)] = block.astype(BF)


def lay_kernel(*refs):
    tiles, (mate, far) = refs[:-2], refs[-2:]
    low, high = lay(tiles, slice(None))
    even = is_even("gx")
    put_plane(mate, [jnp.where(even, b, a) for a, b in zip(low, high)])
    put_plane(far, [jnp.where(even, a, b) for a, b in zip(low, high)])


def shift_taps(products, z):
    rows, cells = products.shape[0] // 9, products.shape[1]
    lane = iota((1, cells), 1)
    depth = lane & (z - 1)
    total = None
    for b in range(3):
        one = [products[(3 * b + c) * rows : (3 * b + c + 1) * rows] for c in range(3)]
        t = one[1] + jnp.where(depth == 0, 0.0, pltpu.roll(one[0], 1, 1))
        t = t + jnp.where(depth == z - 1, 0.0, pltpu.roll(one[2], cells - 1, 1))
        if b == 0:
            t = jnp.where(lane < z, 0.0, pltpu.roll(t, z, 1))
        if b == 2:
            t = jnp.where(lane >= cells - z, 0.0, pltpu.roll(t, cells - z, 1))
        total = t if total is None else total + t
    return total


def middle_kernel(z, mate, far, w3, partial):
    depth = mate.shape[0]
    even = is_even("gx")
    a, b = mate[...], far[...]
    both = jnp.concatenate([jnp.where(even, b, a), jnp.where(even, a, b)], 0)
    w = w3[...].astype(BF)
    partial[0] = shift_taps(mat(w[:, depth:], both), z)
    partial[1] = shift_taps(mat(w[:, : 2 * depth], both), z)


def last_kernel(z, partial, got_far, got_mate, w3, out):
    depth = got_mate.shape[0]
    g, g_last = lax.axis_index("gx"), lax.axis_size("gx") - 1
    low, high = from_sides(got_mate[...], got_far[...], is_even("gx"), g == 0, g == g_last)
    w = w3[...].astype(BF)
    first = relu(partial[0] + shift_taps(mat(w[:, :depth], low), z))
    second = relu(partial[1] + shift_taps(mat(w[:, 2 * depth :], high), z))
    out[...] = jnp.stack([first, second], 1).astype(BF)


def all_kernel(z, *refs):
    tiles, (w3, out, planes) = refs[:-3], refs[-3:]
    depth = planes.shape[1]
    for x in range(2):
        low, high = lay(tiles, slice(x * depth, (x + 1) * depth))
        put_plane(planes.at[2 * x], low)
        put_plane(planes.at[2 * x + 1], high)
    g, g_last = lax.axis_index("gx"), lax.axis_size("gx") - 1
    t = [planes[x] for x in range(4)]
    t[0] = jnp.where(g == 0, jnp.zeros_like(t[0]), t[0])
    t[3] = jnp.where(g == g_last, jnp.zeros_like(t[3]), t[3])
    w = w3[...].astype(BF)
    results = [relu(shift_taps(mat(w, jnp.concatenate(t[x : x + 3], 0)), z)) for x in range(2)]
    out[...] = jnp.stack(results, 1).astype(BF)


def per_device(volume, weight_one, weight_two, weight_three):
    gx, yz = lax.axis_size("gx"), lax.axis_size("yz")
    planes, chans, height, breadth = volume.shape
    rows = chans * height
    edge = EDGE * chans
    c2, c3 = weight_one.shape[0], weight_two.shape[0]

    turned, send_mate, send_far = call(
        turn_kernel,
        [((planes, rows, breadth), BF), ((HALO, rows, breadth), BF), ((HALO, rows, breadth), BF)],
        volume,
    )
    near, away = gx_pairs(gx, yz, False), gx_pairs(gx, yz, True)
    got_mate = lax.ppermute(send_mate, ("gx", "yz"), near)
    got_far = lax.ppermute(send_far, ("gx", "yz"), away)
    k1, k2 = 27 * chans, 27 * c2
    lower1, upper1, middle2, outer2, z_sel, p_sel = call(
        weights_kernel,
        [
            ((4 * c2, k1), BF),
            ((4 * c2, k1), BF),
            ((4 * c3, 2 * k2 // 3), BF),
            ((4 * c3, 2 * k2 // 3), BF),
            ((2 * breadth, 2 * breadth), BF),
            ((4 * breadth, breadth), BF),
        ],
        weight_one,
        weight_two,
        scratch=[
            pltpu.VMEM(weight_one.shape, BF),
            pltpu.VMEM(weight_two.shape, BF),
            pltpu.SemaphoreType.DMA((2,)),
        ],
        hbm=(0, 1),
        flops=2 * 64 * 864 * 1728,
    )
    wide = planes + 2 * HALO
    send_a, send_b = call(
        edge_kernel,
        [((wide, edge, breadth), BF), ((wide, edge, breadth), BF)],
        turned,
        got_far,
        got_mate,
        p_sel,
    )
    got_b = lax.ppermute(send_b, ("gx", "yz"), yz_pairs(gx, yz, True))
    got_a = lax.ppermute(send_a, ("gx", "yz"), yz_pairs(gx, yz, False))
    pairs = 2 * PLANES + 2
    out_rows = weight_three.shape[0] // yz
    partial1, partial2, picked = call(
        inner_kernel,
        [
            ((2, pairs, 4 * c2, 2 * breadth), F32),
            ((4 * c3, PLANES * breadth), F32),
            ((9 * out_rows, 3 * c3), F32),
        ],
        turned,
        got_mate,
        got_far,
        lower1,
        upper1,
        middle2,
        z_sel,
        weight_three.T,
        scratch=[
            pltpu.VMEM((wide, 3 * rows, breadth), BF),
            pltpu.VMEM(weight_three.shape[::-1], BF),
            pltpu.SemaphoreType.DMA,
        ],
        hbm=(7,),
        flops=2 * 300_000_000,
    )
    (tile,) = call(
        outer_kernel,
        [((PLANES // 2 * c3, breadth), BF)],
        got_a,
        got_b,
        partial1,
        partial2,
        lower1,
        upper1,
        outer2,
        z_sel,
        p_sel,
        scratch=[pltpu.VMEM((wide, 3 * edge, breadth), BF), pltpu.VMEM((wide, 3 * edge, breadth), BF)],
        flops=2 * 400_000_000,
    )
    tiles = [tile] + [lax.ppermute(tile, "yz", [(i, i ^ d) for i in range(yz)]) for d in range(1, yz)]
    cells = yz * (height // 4) * (breadth // 4)
    z = breadth // 4
    if PLANES == 4:
        (out,) = call(
            functools.partial(all_kernel, z),
            [((out_rows, 2, cells), BF)],
            *tiles[::-1],
            picked,
            scratch=[pltpu.VMEM((4, c3, cells), BF)],
            flops=2 * 32 * 1728 * 512,
        )
        return out
    mate, far = call(lay_kernel, [((c3, cells), BF), ((c3, cells), BF)], tiles[0], *[tiles[d] for d in [3, 2, 1]])
    got_far = lax.ppermute(far, ("gx", "yz"), away)
    got_mate = lax.ppermute(mate, ("gx", "yz"), near)
    (partial,) = call(
        functools.partial(middle_kernel, z),
        [((2, out_rows, cells), F32)],
        mate,
        far,
        picked,
        flops=2 * 32 * 1152 * 512,
    )
    (out,) = call(
        functools.partial(last_kernel, z),
        [((out_rows, 2, cells), BF)],
        partial,
        got_far,
        got_mate,
        picked,
        flops=2 * 32 * 576 * 512,
    )
    return out


def solution(mesh):
    placed = (P("gx", None, "yz", None), P(), P(), P())
    return jax.shard_map(
        per_device, mesh=mesh, in_specs=placed, out_specs=P("yz", "gx", None), check_vma=False
    )
```

time: 98.2 us -> 28.6 us (0.29)
  the two profiles are of different devices: /device:TPU:4 before, /device:TPU:0 now
where the time goes in v4:
time: 28.6 us; the launch traced here: 28.4 us
  starting transfers between devices  11.6 us (41%)
  waiting for transfers between devices  9.42 us (33%)
  Pallas kernels  6.38 us (22%)
  local copies, waits for them, and re-layouts  0.95 us (3%)
    pallas_call x8, Pallas kernels, call(): pl.pallas_call(body, out_shape=[jax.ShapeDtypeStruct(s, d) for s, d in ou...  6.38 us
    ppermute x3, starting transfers between devices, per_device(): lax.ppermute(tile, 'yz', [(i, i ^ d) for i in range(yz)])  4.59 us
    ppermute x3, waiting for transfers between devices, per_device(): lax.ppermute(tile, 'yz', [(i, i ^ d) for i in range(yz)])  3.8 us
    ppermute x1, starting transfers between devices, per_device(): got_far = lax.ppermute(send_far, ('gx', 'yz'), away)  3.09 us
    ppermute x1, waiting for transfers between devices, per_device(): got_a = lax.ppermute(send_a, ('gx', 'yz'), yz_pairs(gx, yz, False))  2.4 us
    ppermute x1, starting transfers between devices, per_device(): got_a = lax.ppermute(send_a, ('gx', 'yz'), yz_pairs(gx, yz, False))  2.09 us
    ppermute x1, waiting for transfers between devices, per_device(): got_far = lax.ppermute(far, ('gx', 'yz'), away)  1.77 us
    ppermute x1, waiting for transfers between devices, per_device(): got_far = lax.ppermute(send_far, ('gx', 'yz'), away)  1.45 us
  transfers between devices with their start and end apart: 9, of which 5 were waited for; matrix products, arithmetic and copies ran while one was open for 0% of the time, Pallas kernels for 12%

profile of v4, /device:TPU:0, one launch (start us, length us, event | category | flops | bytes accessed | tf_op | source)
XLA Modules:
  0.0 28.4 jit_solution(3569020313116815098)
XLA Ops:
  0.0 0.9 %copy-done = bf16[8,16,8,128]{3,2,1,0:T(8,128)(2,1)S(1)} copy-done((bf16[8,16,8,128]{3,2,1,0:T(8,128)(2,1)S(1)}, bf16[8,16,8,128]{3,2,1,0:T(8,128)(2,1)}, u32[]{:S(2)}) %copy-start) | copy-done | bytes 262168
  1.0 0.3 shard_map.46
  1.2 3.1 %collective-permute-start = (bf16[3,128,128]{2,1,0:T(8,128)(2,1)S(1)}, bf16[3,128,128]{2,1,0:T(8,128)(2,1)S(1)}, u32[]{:S(2)}, u32[]{:S(2)}) collective-permute-start(bf16[3,128,128]{2,1,0:T(8,128)(2,1)S(1)} %get-tuple-element.22), channel_id=1, source_target_pairs={{0,1},{1,0},{2,3},{3,2},{4,8},{5,9},{6,10},{7,11},{8,4},{9,5},{10,... | collective-permute-start | bytes 294920 | tf_op jit(solution)/shard_map/ppermute | solution.py:378
  4.3 0.0 collective-permute-start.1
  4.3 1.1 %shard_map.47 = (bf16[128,432]{1,0:T(8,128)(2,1)S(1)}, bf16[128,432]{1,0:T(8,128)(2,1)S(1)}, bf16[256,576]{1,0:T(8,128)(2,1)S(1)}, bf16[256,576]{1,0:T(8,128)(2,...) custom-call(bf16[32,432]{1,0:T(8,128)(2,1)} %w1_hbm.1, bf16[64,864]{1,0:T(8,128)(2,1)} %w2_hbm.1), custom_call_target="tpu_custom_call" | custom-call | flops 191102976 | bytes 138240 | tf_op jit(solution)/shard_map/pallas_call | solution.py:33
  5.4 1.4 %collective-permute-done.got_far = bf16[3,128,128]{2,1,0:T(8,128)(2,1)S(1)} collective-permute-done((bf16[3,128,128]{2,1,0:T(8,128)(2,1)S(1)}, bf16[3,128,128]{2,1,0:T(8,128)(2,1)S(1)}, u32[]{:S(2)}, u32[]{:S(2)}) %collective-permute-start) | collective-permute-done | bytes 98336 | tf_op jit(solution)/shard_map/ppermute | solution.py:378
  6.9 0.0 collective-permute-done.1.got_mate
  6.9 0.1 shard_map.48
  7.0 2.1 %collective-permute-start.2 = (bf16[14,48,128]{2,1,0:T(8,128)(2,1)S(1)}, bf16[14,48,128]{2,1,0:T(8,128)(2,1)S(1)}, u32[]{:S(2)}, u32[]{:S(2)}) collective-permute-start(bf16[14,48,128]{2,1,0:T(8,128)(2,1)S(1)} %get-tuple-element.25), channel_id=1, source_target_pairs={{0,1},{1,0},{2,3},{3,2},{4,5},{5,4},{6,7},{7,6},{8,9},{9,8},{10,11... | collective-permute-start | bytes 516104 | tf_op jit(solution)/shard_map/ppermute | solution.py:410
  9.1 2.0 %shard_map.49 = (f32[2,6,128,256]{3,2,1,0:T(8,128)S(1)}, f32[256,256]{1,0:T(8,128)S(1)}, f32[288,192]{1,0:T(8,128)S(1)}) custom-call(bf16[8,128,128]{2,1,0:T(8,128)(2,1)S(1)} %get-tuple-element.21.turned, bf16[3,128,128]{2,1,0:T(8,128)(2,1)S(1)} %collective-permute-done.1.got_mate, bf16[3,128,128]{2,1,0:T(8,128)(2,1)S(1)} %collective-permute-done.got_far, ...), custom_call_target="tpu_custom_call" | custom-call | flops 600000000 | bytes 1548288 | tf_op jit(solution)/shard_map/pallas_call | solution.py:33
  11.0 2.4 %collective-permute-done.2.got_a = bf16[14,48,128]{2,1,0:T(8,128)(2,1)S(1)} collective-permute-done((bf16[14,48,128]{2,1,0:T(8,128)(2,1)S(1)}, bf16[14,48,128]{2,1,0:T(8,128)(2,1)S(1)}, u32[]{:S(2)}, u32[]{:S(2)}) %collective-permute-start.2) | collective-permute-done | bytes 172064 | tf_op jit(solution)/shard_map/ppermute | solution.py:410
  13.4 0.0 collective-permute-done.3.got_b
  13.4 1.4 %shard_map.50.refs_0_ = bf16[64,128]{1,0:T(8,128)(2,1)S(1)} custom-call(bf16[14,48,128]{2,1,0:T(8,128)(2,1)S(1)} %collective-permute-done.2.got_a, bf16[14,48,128]{2,1,0:T(8,128)(2,1)S(1)} %collective-permute-done.3.got_b, f32[2,6,128,256]{3,2,1,0:T(8,128)S(1)} %get-tuple-element.31.partial1, f32[256,256]{1,0:T(8,128)S(1)} %get-tuple-element.32.partial2, ...), custom_call_target="tpu_custom_call" | custom-call | flops 800000000 | bytes 2957312 | tf_op jit(solution)/shard_map/pallas_call | solution.py:33
  14.9 3.7 %collective-permute-start.4 = (bf16[64,128]{1,0:T(8,128)(2,1)S(1)}, bf16[64,128]{1,0:T(8,128)(2,1)S(1)}, u32[]{:S(2)}, u32[]{:S(2)}) collective-permute-start(bf16[64,128]{1,0:T(8,128)(2,1)S(1)} %shard_map.50.refs_0_), channel_id=1, source_target_pairs={{0,3},{1,2},{2,1},{3,0},{4,7},{5,6},{6,5},{7,4},{8,11},{9,10},{10,... | collective-permute-start | bytes 49160 | tf_op jit(solution)/shard_map/ppermute | solution.py:451
  18.6 0.6 %collective-permute-start.5 = (bf16[64,128]{1,0:T(8,128)(2,1)S(1)}, bf16[64,128]{1,0:T(8,128)(2,1)S(1)}, u32[]{:S(2)}, u32[]{:S(2)}) collective-permute-start(bf16[64,128]{1,0:T(8,128)(2,1)S(1)} %shard_map.50.refs_0_), channel_id=1, source_target_pairs={{0,2},{1,3},{2,0},{3,1},{4,6},{5,7},{6,4},{7,5},{8,10},{9,11},{10,... | collective-permute-start | bytes 49160 | tf_op jit(solution)/shard_map/ppermute | solution.py:451
  19.2 0.3 collective-permute-start.6
  19.5 1.0 %collective-permute-done.4.refs_1_ = bf16[64,128]{1,0:T(8,128)(2,1)S(1)} collective-permute-done((bf16[64,128]{1,0:T(8,128)(2,1)S(1)}, bf16[64,128]{1,0:T(8,128)(2,1)S(1)}, u32[]{:S(2)}, u32[]{:S(2)}) %collective-permute-start.4) | collective-permute-done | bytes 16416 | tf_op jit(solution)/shard_map/ppermute | solution.py:451
  20.5 2.8 %collective-permute-done.5.refs_2_ = bf16[64,128]{1,0:T(8,128)(2,1)S(1)} collective-permute-done((bf16[64,128]{1,0:T(8,128)(2,1)S(1)}, bf16[64,128]{1,0:T(8,128)(2,1)S(1)}, u32[]{:S(2)}, u32[]{:S(2)}) %collective-permute-start.5) | collective-permute-done | bytes 16416 | tf_op jit(solution)/shard_map/ppermute | solution.py:451
  23.3 0.1 shard_map.51
  23.4 0.9 %collective-permute-start.7 = (bf16[64,256]{1,0:T(8,128)(2,1)S(1)}, bf16[64,256]{1,0:T(8,128)(2,1)S(1)}, u32[]{:S(2)}, u32[]{:S(2)}) collective-permute-start(bf16[64,256]{1,0:T(8,128)(2,1)S(1)} %get-tuple-element.35.far), channel_id=1, source_target_pairs={{0,1},{1,0},{2,3},{3,2},{4,8},{5,9},{6,10},{7,11},{8,4},{9,5},{10,... | collective-permute-start | bytes 98312 | tf_op jit(solution)/shard_map/ppermute | solution.py:465
  24.3 0.9 %collective-permute-start.8 = (bf16[64,256]{1,0:T(8,128)(2,1)S(1)}, bf16[64,256]{1,0:T(8,128)(2,1)S(1)}, u32[]{:S(2)}, u32[]{:S(2)}) collective-permute-start(bf16[64,256]{1,0:T(8,128)(2,1)S(1)} %get-tuple-element.34.mate), channel_id=1, source_target_pairs={{0,4},{1,5},{2,6},{3,7},{4,0},{5,1},{6,2},{7,3},{8,12},{9,13},{10,... | collective-permute-start | bytes 98312 | tf_op jit(solution)/shard_map/ppermute | solution.py:466
  25.2 0.4 %shard_map.52.partial = f32[2,32,256]{2,1,0:T(8,128)S(1)} custom-call(bf16[64,256]{1,0:T(8,128)(2,1)S(1)} %get-tuple-element.34.mate, bf16[64,256]{1,0:T(8,128)(2,1)S(1)} %get-tuple-element.35.far, f32[288,192]{1,0:T(8,128)S(1)} %get-tuple-element.36.w3), custom_call_target="tpu_custom_call" | custom-call | flops 37748736 | bytes 286720 | tf_op jit(solution)/shard_map/pallas_call | solution.py:33
  25.6 1.8 %collective-permute-done.7.got_far = bf16[64,256]{1,0:T(8,128)(2,1)S(1)} collective-permute-done((bf16[64,256]{1,0:T(8,128)(2,1)S(1)}, bf16[64,256]{1,0:T(8,128)(2,1)S(1)}, u32[]{:S(2)}, u32[]{:S(2)}) %collective-permute-start.7) | collective-permute-done | bytes 32800 | tf_op jit(solution)/shard_map/ppermute | solution.py:465
  27.4 1.0 %shard_map.53 = bf16[32,2,256]{2,1,0:T(2,128)(2,1)} custom-call(f32[2,32,256]{2,1,0:T(8,128)S(1)} %shard_map.52.partial, bf16[64,256]{1,0:T(8,128)(2,1)S(1)} %collective-permute-done.7.got_far, bf16[64,256]{1,0:T(8,128)(2,1)S(1)} %collective-permute-done.8.got_mate, f32[288,192]{1,0:T(8,128)S(1)} %get-tuple-element.36.w3), custom_call_target="tpu_custom_call" | custom-call | flops 18874368 | bytes 352256 | tf_op jit(solution)/shard_map/pallas_call | solution.py:33
  (4 shorter events, 0.0 us)
Async XLA Ops:
  0.0 0.9 %copy-start = (bf16[8,16,8,128]{3,2,1,0:T(8,128)(2,1)S(1)}, bf16[8,16,8,128]{3,2,1,0:T(8,128)(2,1)}, u32[]{:S(2)}) copy-start(bf16[8,16,8,128]{3,2,1,0:T(8,128)(2,1)} %vol.1) | copy-start | bytes 786436
  1.2 5.7 %collective-permute-start = (bf16[3,128,128]{2,1,0:T(8,128)(2,1)S(1)}, bf16[3,128,128]{2,1,0:T(8,128)(2,1)S(1)}, u32[]{:S(2)}, u32[]{:S(2)}) collective-permute-start(bf16[3,128,128]{2,1,0:T(8,128)(2,1)S(1)} %get-tuple-element.22), channel_id=1, source_target_pairs={{0,1},{1,0},{2,3},{3,2},{4,8},{5,9},{6,10},{7,11},{8,4},{9,5},{10,... | collective-permute-start | bytes 294920 | tf_op jit(solution)/shard_map/ppermute | solution.py:378
  4.3 2.6 %collective-permute-start.1 = (bf16[3,128,128]{2,1,0:T(8,128)(2,1)S(1)}, bf16[3,128,128]{2,1,0:T(8,128)(2,1)S(1)}, u32[]{:S(2)}, u32[]{:S(2)}) collective-permute-start(bf16[3,128,128]{2,1,0:T(8,128)(2,1)S(1)} %get-tuple-element.23), channel_id=1, source_target_pairs={{0,4},{1,5},{2,6},{3,7},{4,0},{5,1},{6,2},{7,3},{8,12},{9,13},{10,... | collective-permute-start | bytes 294920 | tf_op jit(solution)/shard_map/ppermute | solution.py:377
  7.0 6.5 %collective-permute-start.2 = (bf16[14,48,128]{2,1,0:T(8,128)(2,1)S(1)}, bf16[14,48,128]{2,1,0:T(8,128)(2,1)S(1)}, u32[]{:S(2)}, u32[]{:S(2)}) collective-permute-start(bf16[14,48,128]{2,1,0:T(8,128)(2,1)S(1)} %get-tuple-element.25), channel_id=1, source_target_pairs={{0,1},{1,0},{2,3},{3,2},{4,5},{5,4},{6,7},{7,6},{8,9},{9,8},{10,11... | collective-permute-start | bytes 516104 | tf_op jit(solution)/shard_map/ppermute | solution.py:410
  9.1 4.4 %collective-permute-start.3 = (bf16[14,48,128]{2,1,0:T(8,128)(2,1)S(1)}, bf16[14,48,128]{2,1,0:T(8,128)(2,1)S(1)}, u32[]{:S(2)}, u32[]{:S(2)}) collective-permute-start(bf16[14,48,128]{2,1,0:T(8,128)(2,1)S(1)} %get-tuple-element.26), channel_id=1, source_target_pairs={{0,4},{1,2},{2,1},{3,7},{4,0},{5,6},{6,5},{7,3},{8,12},{9,10},{10,... | collective-permute-start | bytes 516104 | tf_op jit(solution)/shard_map/ppermute | solution.py:409
  14.9 5.6 %collective-permute-start.4 = (bf16[64,128]{1,0:T(8,128)(2,1)S(1)}, bf16[64,128]{1,0:T(8,128)(2,1)S(1)}, u32[]{:S(2)}, u32[]{:S(2)}) collective-permute-start(bf16[64,128]{1,0:T(8,128)(2,1)S(1)} %shard_map.50.refs_0_), channel_id=1, source_target_pairs={{0,3},{1,2},{2,1},{3,0},{4,7},{5,6},{6,5},{7,4},{8,11},{9,10},{10,... | collective-permute-start | bytes 49160 | tf_op jit(solution)/shard_map/ppermute | solution.py:451
  18.6 4.6 %collective-permute-start.5 = (bf16[64,128]{1,0:T(8,128)(2,1)S(1)}, bf16[64,128]{1,0:T(8,128)(2,1)S(1)}, u32[]{:S(2)}, u32[]{:S(2)}) collective-permute-start(bf16[64,128]{1,0:T(8,128)(2,1)S(1)} %shard_map.50.refs_0_), channel_id=1, source_target_pairs={{0,2},{1,3},{2,0},{3,1},{4,6},{5,7},{6,4},{7,5},{8,10},{9,11},{10,... | collective-permute-start | bytes 49160 | tf_op jit(solution)/shard_map/ppermute | solution.py:451
  19.2 4.1 %collective-permute-start.6 = (bf16[64,128]{1,0:T(8,128)(2,1)S(1)}, bf16[64,128]{1,0:T(8,128)(2,1)S(1)}, u32[]{:S(2)}, u32[]{:S(2)}) collective-permute-start(bf16[64,128]{1,0:T(8,128)(2,1)S(1)} %shard_map.50.refs_0_), channel_id=1, source_target_pairs={{0,1},{1,0},{2,3},{3,2},{4,5},{5,4},{6,7},{7,6},{8,9},{9,8},{10,11... | collective-permute-start | bytes 49160 | tf_op jit(solution)/shard_map/ppermute | solution.py:451
  23.4 4.0 %collective-permute-start.7 = (bf16[64,256]{1,0:T(8,128)(2,1)S(1)}, bf16[64,256]{1,0:T(8,128)(2,1)S(1)}, u32[]{:S(2)}, u32[]{:S(2)}) collective-permute-start(bf16[64,256]{1,0:T(8,128)(2,1)S(1)} %get-tuple-element.35.far), channel_id=1, source_target_pairs={{0,1},{1,0},{2,3},{3,2},{4,8},{5,9},{6,10},{7,11},{8,4},{9,5},{10,... | collective-permute-start | bytes 98312 | tf_op jit(solution)/shard_map/ppermute | solution.py:465
  24.3 3.1 %collective-permute-start.8 = (bf16[64,256]{1,0:T(8,128)(2,1)S(1)}, bf16[64,256]{1,0:T(8,128)(2,1)S(1)}, u32[]{:S(2)}, u32[]{:S(2)}) collective-permute-start(bf16[64,256]{1,0:T(8,128)(2,1)S(1)} %get-tuple-element.34.mate), channel_id=1, source_target_pairs={{0,4},{1,5},{2,6},{3,7},{4,0},{5,1},{6,2},{7,3},{8,12},{9,13},{10,... | collective-permute-start | bytes 98312 | tf_op jit(solution)/shard_map/ppermute | solution.py:466

commit v5 on v4

--- a/solution.py
+++ b/solution.py
@@ -27,15 +27,16 @@
     return lax.broadcasted_iota(jnp.int32, shape, dim)
 
 
-def call(body, outs, *args, scratch=(), flops=0, hbm=()):
+def call(body, outs, *args, scratch=(), flops=0, hbm=(), hbm_out=False, aliases={}):
     moved = sum(a.size * a.dtype.itemsize for a in args)
     args = [pltpu.with_memory_space_constraint(a, pltpu.HBM) if i in hbm else a for i, a in enumerate(args)]
     return pl.pallas_call(
         body,
         out_shape=[jax.ShapeDtypeStruct(s, d) for s, d in outs],
         in_specs=[pl.BlockSpec(memory_space=pltpu.HBM if i in hbm else pltpu.VMEM) for i in range(len(args))],
-        out_specs=[WHOLE] * len(outs),
+        out_specs=[pl.BlockSpec(memory_space=pltpu.HBM) if hbm_out else WHOLE] * len(outs),
         scratch_shapes=list(scratch),
+        input_output_aliases=aliases,
         compiler_params=pltpu.CompilerParams(vmem_limit_bytes=40 * 1024 * 1024),
         cost_estimate=pl.CostEstimate(flops=flops, bytes_accessed=moved, transcendentals=0),
     )(*args)
@@ -325,40 +326,38 @@
     return total
 
 
-def middle_kernel(z, mate, far, w3, partial):
+def near_kernel(z, mate, far, got_mate, w3, out, ready, pending):
     depth = mate.shape[0]
     even = is_even("gx")
     a, b = mate[...], far[...]
     both = jnp.concatenate([jnp.where(even, b, a), jnp.where(even, a, b)], 0)
     w = w3[...].astype(BF)
-    partial[0] = shift_taps(mat(w[:, depth:], both), z)
-    partial[1] = shift_taps(mat(w[:, : 2 * depth], both), z)
-
-
-def last_kernel(z, partial, got_far, got_mate, w3, out):
-    depth = got_mate.shape[0]
-    g, g_last = lax.axis_index("gx"), lax.axis_size("gx") - 1
-    low, high = from_sides(got_mate[...], got_far[...], is_even("gx"), g == 0, g == g_last)
-    w = w3[...].astype(BF)
-    first = relu(partial[0] + shift_taps(mat(w[:, :depth], low), z))
-    second = relu(partial[1] + shift_taps(mat(w[:, 2 * depth :], high), z))
-    out[...] = jnp.stack([first, second], 1).astype(BF)
-
-
-def all_kernel(z, *refs):
-    tiles, (w3, out, planes) = refs[:-3], refs[-3:]
-    depth = planes.shape[1]
-    for x in range(2):
-        low, high = lay(tiles, slice(x * depth, (x + 1) * depth))
-        put_plane(planes.at[2 * x], low)
-        put_plane(planes.at[2 * x + 1], high)
-    g, g_last = lax.axis_index("gx"), lax.axis_size("gx") - 1
-    t = [planes[x] for x in range(4)]
-    t[0] = jnp.where(g == 0, jnp.zeros_like(t[0]), t[0])
-    t[3] = jnp.where(g == g_last, jnp.zeros_like(t[3]), t[3])
-    w = w3[...].astype(BF)
-    results = [relu(shift_taps(mat(w, jnp.concatenate(t[x : x + 3], 0)), z)) for x in range(2)]
-    out[...] = jnp.stack(results, 1).astype(BF)
+    first, second = w[:, depth:], w[:, : 2 * depth]
+    beside = jnp.where(even, w[:, 2 * depth :], w[:, :depth])
+    t = mat(jnp.where(even, second, first), both) + mat(beside, got_mate[...])
+    done = relu(shift_taps(t, z))
+    part = shift_taps(mat(jnp.where(even, first, second), both), z)
+    ready[...] = done
+    pending[...] = part
+    part = relu(part)
+    out[...] = jnp.stack([jnp.where(even, part, done), jnp.where(even, done, part)], 1).astype(BF)
+
+
+def far_kernel(z, got_far, w3, ready, pending, _, out, block, sem):
+    depth = got_far.shape[0]
+    g = lax.axis_index("gx")
+
+    @pl.when((g > 0) & (g < lax.axis_size("gx") - 1))
+    def _():
+        even = is_even("gx")
+        w = w3[...].astype(BF)
+        beside = jnp.where(even, w[:, :depth], w[:, 2 * depth :])
+        part = relu(pending[...] + shift_taps(mat(beside, got_far[...]), z))
+        done = ready[...]
+        block[...] = jnp.stack([jnp.where(even, part, done), jnp.where(even, done, part)], 1).astype(BF)
+        copy = pltpu.make_async_copy(block, out, sem)
+        copy.start()
+        copy.wait()
 
 
 def per_device(volume, weight_one, weight_two, weight_three):
@@ -451,35 +450,32 @@
     tiles = [tile] + [lax.ppermute(tile, "yz", [(i, i ^ d) for i in range(yz)]) for d in range(1, yz)]
     cells = yz * (height // 4) * (breadth // 4)
     z = breadth // 4
-    if PLANES == 4:
-        (out,) = call(
-            functools.partial(all_kernel, z),
-            [((out_rows, 2, cells), BF)],
-            *tiles[::-1],
-            picked,
-            scratch=[pltpu.VMEM((4, c3, cells), BF)],
-            flops=2 * 32 * 1728 * 512,
-        )
-        return out
     mate, far = call(lay_kernel, [((c3, cells), BF), ((c3, cells), BF)], tiles[0], *[tiles[d] for d in [3, 2, 1]])
     got_far = lax.ppermute(far, ("gx", "yz"), away)
     got_mate = lax.ppermute(mate, ("gx", "yz"), near)
-    (partial,) = call(
-        functools.partial(middle_kernel, z),
-        [((2, out_rows, cells), F32)],
+    shape = (out_rows, 2, cells)
+    out, ready, pending = call(
+        functools.partial(near_kernel, z),
+        [(shape, BF), ((out_rows, cells), F32), ((out_rows, cells), F32)],
         mate,
         far,
-        picked,
-        flops=2 * 32 * 1152 * 512,
-    )
-    (out,) = call(
-        functools.partial(last_kernel, z),
-        [((out_rows, 2, cells), BF)],
-        partial,
-        got_far,
         got_mate,
         picked,
-        flops=2 * 32 * 576 * 512,
+        flops=2 * 32 * 1728 * 512,
+    )
+    (out,) = call(
+        functools.partial(far_kernel, z),
+        [(shape, BF)],
+        got_far,
+        picked,
+        ready,
+        pending,
+        out,
+        scratch=[pltpu.VMEM(shape, BF), pltpu.SemaphoreType.DMA],
+        hbm=(4,),
+        hbm_out=True,
+        aliases={4: 0},
+        flops=2 * 32 * 576 * 256,
     )
     return out
 

time: 28.6 us -> 28.2 us (0.986)
  the two profiles are of different devices: /device:TPU:0 before, /device:TPU:1 now
where the time goes in v5:
time: 28.2 us; the launch traced here: 28.1 us
  starting transfers between devices  13.4 us (48%)
  Pallas kernels  7.16 us (25%)
  waiting for transfers between devices  6.55 us (23%)
  local copies, waits for them, and re-layouts  0.95 us (3%)
    pallas_call x8, Pallas kernels, call(): pl.pallas_call(body, out_shape=[jax.ShapeDtypeStruct(s, d) for s, d in ou...  7.16 us
    ppermute x3, starting transfers between devices, per_device(): lax.ppermute(tile, 'yz', [(i, i ^ d) for i in range(yz)])  3.61 us
    ppermute x3, waiting for transfers between devices, per_device(): lax.ppermute(tile, 'yz', [(i, i ^ d) for i in range(yz)])  3.23 us
    ppermute x1, starting transfers between devices, per_device(): got_mate = lax.ppermute(mate, ('gx', 'yz'), near)  2.83 us
    ppermute x1, starting transfers between devices, per_device(): got_far = lax.ppermute(send_far, ('gx', 'yz'), away)  2.67 us
    ppermute x1, starting transfers between devices, per_device(): got_a = lax.ppermute(send_a, ('gx', 'yz'), yz_pairs(gx, yz, False))  1.44 us
    ppermute x1, starting transfers between devices, per_device(): got_far = lax.ppermute(far, ('gx', 'yz'), away)  1.3 us
    ppermute x1, waiting for transfers between devices, per_device(): got_a = lax.ppermute(send_a, ('gx', 'yz'), yz_pairs(gx, yz, False))  1.18 us
  transfers between devices with their start and end apart: 9, of which 5 were waited for; matrix products, arithmetic and copies ran while one was open for 0% of the time, Pallas kernels for 15%

profile of v5, /device:TPU:1, one launch (start us, length us, event | category | flops | bytes accessed | tf_op | source)
XLA Modules:
  0.0 28.1 jit_solution(11200094095928353769)
XLA Ops:
  0.0 0.9 %copy-done = bf16[8,16,8,128]{3,2,1,0:T(8,128)(2,1)S(1)} copy-done((bf16[8,16,8,128]{3,2,1,0:T(8,128)(2,1)S(1)}, bf16[8,16,8,128]{3,2,1,0:T(8,128)(2,1)}, u32[]{:S(2)}) %copy-start) | copy-done | bytes 262168
  1.0 0.2 shard_map.46
  1.2 2.7 %collective-permute-start = (bf16[3,128,128]{2,1,0:T(8,128)(2,1)S(1)}, bf16[3,128,128]{2,1,0:T(8,128)(2,1)S(1)}, u32[]{:S(2)}, u32[]{:S(2)}) collective-permute-start(bf16[3,128,128]{2,1,0:T(8,128)(2,1)S(1)} %get-tuple-element.25), channel_id=1, source_target_pairs={{0,1},{1,0},{2,3},{3,2},{4,8},{5,9},{6,10},{7,11},{8,4},{9,5},{10,... | collective-permute-start | bytes 294920 | tf_op jit(solution)/shard_map/ppermute | solution.py:377
  3.9 0.5 %collective-permute-start.1 = (bf16[3,128,128]{2,1,0:T(8,128)(2,1)S(1)}, bf16[3,128,128]{2,1,0:T(8,128)(2,1)S(1)}, u32[]{:S(2)}, u32[]{:S(2)}) collective-permute-start(bf16[3,128,128]{2,1,0:T(8,128)(2,1)S(1)} %get-tuple-element.26), channel_id=1, source_target_pairs={{0,4},{1,5},{2,6},{3,7},{4,0},{5,1},{6,2},{7,3},{8,12},{9,13},{10,... | collective-permute-start | bytes 294920 | tf_op jit(solution)/shard_map/ppermute | solution.py:376
  4.4 1.1 %shard_map.47 = (bf16[128,432]{1,0:T(8,128)(2,1)S(1)}, bf16[128,432]{1,0:T(8,128)(2,1)S(1)}, bf16[256,576]{1,0:T(8,128)(2,1)S(1)}, bf16[256,576]{1,0:T(8,128)(2,...) custom-call(bf16[32,432]{1,0:T(8,128)(2,1)} %w1_hbm.1, bf16[64,864]{1,0:T(8,128)(2,1)} %w2_hbm.1), custom_call_target="tpu_custom_call" | custom-call | flops 191102976 | bytes 138240 | tf_op jit(solution)/shard_map/pallas_call | solution.py:33
  5.5 1.1 %collective-permute-done.got_far = bf16[3,128,128]{2,1,0:T(8,128)(2,1)S(1)} collective-permute-done((bf16[3,128,128]{2,1,0:T(8,128)(2,1)S(1)}, bf16[3,128,128]{2,1,0:T(8,128)(2,1)S(1)}, u32[]{:S(2)}, u32[]{:S(2)}) %collective-permute-start) | collective-permute-done | bytes 98336 | tf_op jit(solution)/shard_map/ppermute | solution.py:377
  6.6 0.0 collective-permute-done.1.got_mate
  6.6 0.1 shard_map.48
  6.6 1.4 %collective-permute-start.2 = (bf16[14,48,128]{2,1,0:T(8,128)(2,1)S(1)}, bf16[14,48,128]{2,1,0:T(8,128)(2,1)S(1)}, u32[]{:S(2)}, u32[]{:S(2)}) collective-permute-start(bf16[14,48,128]{2,1,0:T(8,128)(2,1)S(1)} %get-tuple-element.28), channel_id=1, source_target_pairs={{0,1},{1,0},{2,3},{3,2},{4,5},{5,4},{6,7},{7,6},{8,9},{9,8},{10,11... | collective-permute-start | bytes 516104 | tf_op jit(solution)/shard_map/ppermute | solution.py:409
  8.1 1.0 %collective-permute-start.3 = (bf16[14,48,128]{2,1,0:T(8,128)(2,1)S(1)}, bf16[14,48,128]{2,1,0:T(8,128)(2,1)S(1)}, u32[]{:S(2)}, u32[]{:S(2)}) collective-permute-start(bf16[14,48,128]{2,1,0:T(8,128)(2,1)S(1)} %get-tuple-element.29), channel_id=1, source_target_pairs={{0,4},{1,2},{2,1},{3,7},{4,0},{5,6},{6,5},{7,3},{8,12},{9,10},{10,... | collective-permute-start | bytes 516104 | tf_op jit(solution)/shard_map/ppermute | solution.py:408
  9.1 2.0 %shard_map.49 = (f32[2,6,128,256]{3,2,1,0:T(8,128)S(1)}, f32[256,256]{1,0:T(8,128)S(1)}, f32[288,192]{1,0:T(8,128)S(1)}) custom-call(bf16[8,128,128]{2,1,0:T(8,128)(2,1)S(1)} %get-tuple-element.24.turned, bf16[3,128,128]{2,1,0:T(8,128)(2,1)S(1)} %collective-permute-done.1.got_mate, bf16[3,128,128]{2,1,0:T(8,128)(2,1)S(1)} %collective-permute-done.got_far, ...), custom_call_target="tpu_custom_call" | custom-call | flops 600000000 | bytes 1548288 | tf_op jit(solution)/shard_map/pallas_call | solution.py:33
  11.1 1.2 %collective-permute-done.2.got_a = bf16[14,48,128]{2,1,0:T(8,128)(2,1)S(1)} collective-permute-done((bf16[14,48,128]{2,1,0:T(8,128)(2,1)S(1)}, bf16[14,48,128]{2,1,0:T(8,128)(2,1)S(1)}, u32[]{:S(2)}, u32[]{:S(2)}) %collective-permute-start.2) | collective-permute-done | bytes 172064 | tf_op jit(solution)/shard_map/ppermute | solution.py:409
  12.3 1.4 %shard_map.50.refs_0_ = bf16[64,128]{1,0:T(8,128)(2,1)S(1)} custom-call(bf16[14,48,128]{2,1,0:T(8,128)(2,1)S(1)} %collective-permute-done.2.got_a, bf16[14,48,128]{2,1,0:T(8,128)(2,1)S(1)} %collective-permute-done.3.got_b, f32[2,6,128,256]{3,2,1,0:T(8,128)S(1)} %get-tuple-element.34.partial1, f32[256,256]{1,0:T(8,128)S(1)} %get-tuple-element.35.partial2, ...), custom_call_target="tpu_custom_call" | custom-call | flops 800000000 | bytes 2957312 | tf_op jit(solution)/shard_map/pallas_call | solution.py:33
  13.7 3.0 %collective-permute-start.4 = (bf16[64,128]{1,0:T(8,128)(2,1)S(1)}, bf16[64,128]{1,0:T(8,128)(2,1)S(1)}, u32[]{:S(2)}, u32[]{:S(2)}) collective-permute-start(bf16[64,128]{1,0:T(8,128)(2,1)S(1)} %shard_map.50.refs_0_), channel_id=1, source_target_pairs={{0,3},{1,2},{2,1},{3,0},{4,7},{5,6},{6,5},{7,4},{8,11},{9,10},{10,... | collective-permute-start | bytes 49160 | tf_op jit(solution)/shard_map/ppermute | solution.py:450
  16.8 0.3 %collective-permute-start.5 = (bf16[64,128]{1,0:T(8,128)(2,1)S(1)}, bf16[64,128]{1,0:T(8,128)(2,1)S(1)}, u32[]{:S(2)}, u32[]{:S(2)}) collective-permute-start(bf16[64,128]{1,0:T(8,128)(2,1)S(1)} %shard_map.50.refs_0_), channel_id=1, source_target_pairs={{0,2},{1,3},{2,0},{3,1},{4,6},{5,7},{6,4},{7,5},{8,10},{9,11},{10,... | collective-permute-start | bytes 49160 | tf_op jit(solution)/shard_map/ppermute | solution.py:450
  17.0 0.3 %collective-permute-start.6 = (bf16[64,128]{1,0:T(8,128)(2,1)S(1)}, bf16[64,128]{1,0:T(8,128)(2,1)S(1)}, u32[]{:S(2)}, u32[]{:S(2)}) collective-permute-start(bf16[64,128]{1,0:T(8,128)(2,1)S(1)} %shard_map.50.refs_0_), channel_id=1, source_target_pairs={{0,1},{1,0},{2,3},{3,2},{4,5},{5,4},{6,7},{7,6},{8,9},{9,8},{10,11... | collective-permute-start | bytes 49160 | tf_op jit(solution)/shard_map/ppermute | solution.py:450
  17.3 0.9 %collective-permute-done.4.refs_1_ = bf16[64,128]{1,0:T(8,128)(2,1)S(1)} collective-permute-done((bf16[64,128]{1,0:T(8,128)(2,1)S(1)}, bf16[64,128]{1,0:T(8,128)(2,1)S(1)}, u32[]{:S(2)}, u32[]{:S(2)}) %collective-permute-start.4) | collective-permute-done | bytes 16416 | tf_op jit(solution)/shard_map/ppermute | solution.py:450
  18.3 2.3 %collective-permute-done.5.refs_2_ = bf16[64,128]{1,0:T(8,128)(2,1)S(1)} collective-permute-done((bf16[64,128]{1,0:T(8,128)(2,1)S(1)}, bf16[64,128]{1,0:T(8,128)(2,1)S(1)}, u32[]{:S(2)}, u32[]{:S(2)}) %collective-permute-start.5) | collective-permute-done | bytes 16416 | tf_op jit(solution)/shard_map/ppermute | solution.py:450
  20.6 0.1 shard_map.51
  20.7 2.8 %collective-permute-start.8 = (bf16[64,256]{1,0:T(8,128)(2,1)S(1)}, bf16[64,256]{1,0:T(8,128)(2,1)S(1)}, u32[]{:S(2)}, u32[]{:S(2)}) collective-permute-start(bf16[64,256]{1,0:T(8,128)(2,1)S(1)} %get-tuple-element.39.mate), channel_id=1, source_target_pairs={{0,4},{1,5},{2,6},{3,7},{4,0},{5,1},{6,2},{7,3},{8,12},{9,13},{10,... | collective-permute-start | bytes 98312 | tf_op jit(solution)/shard_map/ppermute | solution.py:455
  23.5 1.3 %collective-permute-start.7 = (bf16[64,256]{1,0:T(8,128)(2,1)S(1)}, bf16[64,256]{1,0:T(8,128)(2,1)S(1)}, u32[]{:S(2)}, u32[]{:S(2)}) collective-permute-start(bf16[64,256]{1,0:T(8,128)(2,1)S(1)} %get-tuple-element.37.far), channel_id=1, source_target_pairs={{0,1},{1,0},{2,3},{3,2},{4,8},{5,9},{6,10},{7,11},{8,4},{9,5},{10,... | collective-permute-start | bytes 98312 | tf_op jit(solution)/shard_map/ppermute | solution.py:454
  24.8 1.2 %shard_map.52 = (bf16[32,2,256]{2,1,0:T(2,128)(2,1)}, f32[32,256]{1,0:T(8,128)S(1)}, f32[32,256]{1,0:T(8,128)S(1)}) custom-call(bf16[64,256]{1,0:T(8,128)(2,1)S(1)} %get-tuple-element.39.mate, bf16[64,256]{1,0:T(8,128)(2,1)S(1)} %get-tuple-element.37.far, bf16[64,256]{1,0:T(8,128)(2,1)S(1)} %collective-permute-done.8.got_mate, ...), custom_call_target="tpu_custom_call" | custom-call | flops 56623104 | bytes 319488 | tf_op jit(solution)/shard_map/pallas_call | solution.py:33
  26.0 1.1 %collective-permute-done.7.got_far = bf16[64,256]{1,0:T(8,128)(2,1)S(1)} collective-permute-done((bf16[64,256]{1,0:T(8,128)(2,1)S(1)}, bf16[64,256]{1,0:T(8,128)(2,1)S(1)}, u32[]{:S(2)}, u32[]{:S(2)}) %collective-permute-start.7) | collective-permute-done | bytes 32800 | tf_op jit(solution)/shard_map/ppermute | solution.py:454
  27.1 1.0 %shard_map.53 = bf16[32,2,256]{2,1,0:T(2,128)(2,1)} custom-call(bf16[64,256]{1,0:T(8,128)(2,1)S(1)} %collective-permute-done.7.got_far, f32[288,192]{1,0:T(8,128)S(1)} %get-tuple-element.38.w3, f32[32,256]{1,0:T(8,128)S(1)} %get-tuple-element.40.ready, f32[32,256]{1,0:T(8,128)S(1)} %get-tuple-element.41.pending, ...), custom_call_target="tpu_custom_call", output_to_operand_aliasing={{}: (4, {})} | custom-call | flops 9437184 | bytes 352256 | tf_op jit(solution)/shard_map/pallas_call | solution.py:33
  (4 shorter events, 0.0 us)
Async XLA Ops:
  0.0 0.9 %copy-start = (bf16[8,16,8,128]{3,2,1,0:T(8,128)(2,1)S(1)}, bf16[8,16,8,128]{3,2,1,0:T(8,128)(2,1)}, u32[]{:S(2)}) copy-start(bf16[8,16,8,128]{3,2,1,0:T(8,128)(2,1)} %vol.1) | copy-start | bytes 786436
  1.2 5.4 %collective-permute-start = (bf16[3,128,128]{2,1,0:T(8,128)(2,1)S(1)}, bf16[3,128,128]{2,1,0:T(8,128)(2,1)S(1)}, u32[]{:S(2)}, u32[]{:S(2)}) collective-permute-start(bf16[3,128,128]{2,1,0:T(8,128)(2,1)S(1)} %get-tuple-element.25), channel_id=1, source_target_pairs={{0,1},{1,0},{2,3},{3,2},{4,8},{5,9},{6,10},{7,11},{8,4},{9,5},{10,... | collective-permute-start | bytes 294920 | tf_op jit(solution)/shard_map/ppermute | solution.py:377
  3.9 2.7 %collective-permute-start.1 = (bf16[3,128,128]{2,1,0:T(8,128)(2,1)S(1)}, bf16[3,128,128]{2,1,0:T(8,128)(2,1)S(1)}, u32[]{:S(2)}, u32[]{:S(2)}) collective-permute-start(bf16[3,128,128]{2,1,0:T(8,128)(2,1)S(1)} %get-tuple-element.26), channel_id=1, source_target_pairs={{0,4},{1,5},{2,6},{3,7},{4,0},{5,1},{6,2},{7,3},{8,12},{9,13},{10,... | collective-permute-start | bytes 294920 | tf_op jit(solution)/shard_map/ppermute | solution.py:376
  6.6 5.6 %collective-permute-start.2 = (bf16[14,48,128]{2,1,0:T(8,128)(2,1)S(1)}, bf16[14,48,128]{2,1,0:T(8,128)(2,1)S(1)}, u32[]{:S(2)}, u32[]{:S(2)}) collective-permute-start(bf16[14,48,128]{2,1,0:T(8,128)(2,1)S(1)} %get-tuple-element.28), channel_id=1, source_target_pairs={{0,1},{1,0},{2,3},{3,2},{4,5},{5,4},{6,7},{7,6},{8,9},{9,8},{10,11... | collective-permute-start | bytes 516104 | tf_op jit(solution)/shard_map/ppermute | solution.py:409
  8.1 4.2 %collective-permute-start.3 = (bf16[14,48,128]{2,1,0:T(8,128)(2,1)S(1)}, bf16[14,48,128]{2,1,0:T(8,128)(2,1)S(1)}, u32[]{:S(2)}, u32[]{:S(2)}) collective-permute-start(bf16[14,48,128]{2,1,0:T(8,128)(2,1)S(1)} %get-tuple-element.29), channel_id=1, source_target_pairs={{0,4},{1,2},{2,1},{3,7},{4,0},{5,6},{6,5},{7,3},{8,12},{9,10},{10,... | collective-permute-start | bytes 516104 | tf_op jit(solution)/shard_map/ppermute | solution.py:408
  13.7 4.6 %collective-permute-start.4 = (bf16[64,128]{1,0:T(8,128)(2,1)S(1)}, bf16[64,128]{1,0:T(8,128)(2,1)S(1)}, u32[]{:S(2)}, u32[]{:S(2)}) collective-permute-start(bf16[64,128]{1,0:T(8,128)(2,1)S(1)} %shard_map.50.refs_0_), channel_id=1, source_target_pairs={{0,3},{1,2},{2,1},{3,0},{4,7},{5,6},{6,5},{7,4},{8,11},{9,10},{10,... | collective-permute-start | bytes 49160 | tf_op jit(solution)/shard_map/ppermute | solution.py:450
  16.8 3.8 %collective-permute-start.5 = (bf16[64,128]{1,0:T(8,128)(2,1)S(1)}, bf16[64,128]{1,0:T(8,128)(2,1)S(1)}, u32[]{:S(2)}, u32[]{:S(2)}) collective-permute-start(bf16[64,128]{1,0:T(8,128)(2,1)S(1)} %shard_map.50.refs_0_), channel_id=1, source_target_pairs={{0,2},{1,3},{2,0},{3,1},{4,6},{5,7},{6,4},{7,5},{8,10},{9,11},{10,... | collective-permute-start | bytes 49160 | tf_op jit(solution)/shard_map/ppermute | solution.py:450
  17.0 3.5 %collective-permute-start.6 = (bf16[64,128]{1,0:T(8,128)(2,1)S(1)}, bf16[64,128]{1,0:T(8,128)(2,1)S(1)}, u32[]{:S(2)}, u32[]{:S(2)}) collective-permute-start(bf16[64,128]{1,0:T(8,128)(2,1)S(1)} %shard_map.50.refs_0_), channel_id=1, source_target_pairs={{0,1},{1,0},{2,3},{3,2},{4,5},{5,4},{6,7},{7,6},{8,9},{9,8},{10,11... | collective-permute-start | bytes 49160 | tf_op jit(solution)/shard_map/ppermute | solution.py:450
  20.7 4.1 %collective-permute-start.8 = (bf16[64,256]{1,0:T(8,128)(2,1)S(1)}, bf16[64,256]{1,0:T(8,128)(2,1)S(1)}, u32[]{:S(2)}, u32[]{:S(2)}) collective-permute-start(bf16[64,256]{1,0:T(8,128)(2,1)S(1)} %get-tuple-element.39.mate), channel_id=1, source_target_pairs={{0,4},{1,5},{2,6},{3,7},{4,0},{5,1},{6,2},{7,3},{8,12},{9,13},{10,... | collective-permute-start | bytes 98312 | tf_op jit(solution)/shard_map/ppermute | solution.py:455
  23.5 3.6 %collective-permute-start.7 = (bf16[64,256]{1,0:T(8,128)(2,1)S(1)}, bf16[64,256]{1,0:T(8,128)(2,1)S(1)}, u32[]{:S(2)}, u32[]{:S(2)}) collective-permute-start(bf16[64,256]{1,0:T(8,128)(2,1)S(1)} %get-tuple-element.37.far), channel_id=1, source_target_pairs={{0,1},{1,0},{2,3},{3,2},{4,8},{5,9},{6,10},{7,11},{8,4},{9,5},{10,... | collective-permute-start | bytes 98312 | tf_op jit(solution)/shard_map/ppermute | solution.py:454

commit v6 on v5

--- a/solution.py
+++ b/solution.py
@@ -9,7 +9,6 @@
 
 BF = jnp.bfloat16
 F32 = jnp.float32
-WHOLE = pl.BlockSpec(memory_space=pltpu.VMEM)
 PLANES = 2
 HALO = 2 * PLANES - 1
 EDGE = 3
@@ -27,14 +26,14 @@
     return lax.broadcasted_iota(jnp.int32, shape, dim)
 
 
-def call(body, outs, *args, scratch=(), flops=0, hbm=(), hbm_out=False, aliases={}):
-    moved = sum(a.size * a.dtype.itemsize for a in args)
+def call(body, outs, *args, scratch=(), flops=0, free=False, hbm=(), hbm_out=False, aliases={}):
+    moved = 0 if free else sum(a.size * a.dtype.itemsize for a in args)
     args = [pltpu.with_memory_space_constraint(a, pltpu.HBM) if i in hbm else a for i, a in enumerate(args)]
     return pl.pallas_call(
         body,
         out_shape=[jax.ShapeDtypeStruct(s, d) for s, d in outs],
         in_specs=[pl.BlockSpec(memory_space=pltpu.HBM if i in hbm else pltpu.VMEM) for i in range(len(args))],
-        out_specs=[pl.BlockSpec(memory_space=pltpu.HBM) if hbm_out else WHOLE] * len(outs),
+        out_specs=[pl.BlockSpec(memory_space=pltpu.HBM if hbm_out and i == 0 else pltpu.VMEM) for i in range(len(outs))],
         scratch_shapes=list(scratch),
         input_output_aliases=aliases,
         compiler_params=pltpu.CompilerParams(vmem_limit_bytes=40 * 1024 * 1024),
@@ -112,25 +111,16 @@
         send_b[x] = jnp.where(even, low, high)
 
 
-def weights_kernel(w1_hbm, w2_hbm, lower1, upper1, middle2, outer2, z_sel, p_sel, w1, w2, sems):
+def weights_kernel(w1_hbm, w2_hbm, lower1, upper1, middle2, outer2, p_sel, w1, w2, sems):
     loads = [pltpu.make_async_copy(a, b, sems.at[i]) for i, (a, b) in enumerate(((w1_hbm, w1), (w2_hbm, w2)))]
     for load in loads:
         load.start()
 
-    rows, columns = z_sel.shape
-    breadth = rows // 2
-    r, c = iota(z_sel.shape, 0), iota(z_sel.shape, 1)
-    tap = c // breadth
-    within = c - tap * breadth
-    same = (r // breadth) == (within // (breadth // 2))
-    cell = (r & (breadth - 1)) == 2 * ((within & (breadth // 2 - 1)) + tap - 1)
-    z_sel[...] = jnp.where(same & cell, 1.0, 0.0).astype(BF)
-
     rows, columns = p_sel.shape
-    z = rows // 8
+    z = rows // 4
     r, c = iota(p_sel.shape, 0), iota(p_sel.shape, 1)
-    hit = (r // (4 * z) == (c // (z // 2)) % 2) & ((r // z) % 4 == 2 * (c // z))
-    hit = hit & ((r & (z - 1)) == 2 * (c & (z // 2 - 1)))
+    hit = (r // (2 * z) == (c // (z // 4)) % 2) & ((r // z) % 2 == c // (z // 2))
+    hit = hit & ((r & (z - 1)) == 4 * (c & (z // 4 - 1)))
     p_sel[...] = jnp.where(hit, 1.0, 0.0).astype(BF)
 
     for load in loads:
@@ -187,29 +177,25 @@
         if j > pairs - PLANES:
             drop = drop | (g == lax.axis_size("gx") - 1)
         halves.append(t if drop is False else jnp.where(drop, 0.0, t))
-    return jnp.concatenate(halves, 0).astype(BF)
-
-
-def second_taps(pooled, z_sel):
-    beside = [jnp.concatenate([a, b], 1) for a, b in zip(pooled[:-1], pooled[1:])]
-    q = mat(jnp.concatenate(beside, 0), z_sel)
-    breadth = q.shape[1] // 2
-    before, here = q[:, :breadth], q[:, breadth:]
+    return pooled_taps(jnp.concatenate(halves, 0))
+
+
+def pooled_taps(t):
+    breadth = t.shape[1]
     lane = iota((1, breadth), 1)
-    last = (lane & (breadth // 2 - 1)) == breadth // 2 - 1
-    after = jnp.where(last, 0.0, pltpu.roll(here, breadth - 1, 1))
-    taps = [t.astype(BF) for t in (before, here, after)]
-    chans = pooled[0].shape[0] // 2
-    planes = []
-    for j in range(len(beside)):
-        rows = [slice((2 * j + y) * chans, (2 * j + y + 1) * chans) for y in range(2)]
-        planes.append([t[r] for r in rows for t in taps])
-    columns = [jnp.concatenate(planes[j] + planes[j + 1] + planes[j + 2], 0) for j in range(0, len(planes) - 2, 2)]
-    return jnp.concatenate(columns, 1)
+    before = jnp.where(lane < 2, 0.0, pltpu.roll(t, 2, 1)).astype(BF)
+    after = jnp.where(lane >= breadth - 2, 0.0, pltpu.roll(t, breadth - 2, 1)).astype(BF)
+    chans = t.shape[0] // 2
+    rows = [slice(y * chans, (y + 1) * chans) for y in range(2)]
+    return jnp.concatenate([u[r] for r in rows for u in (before, t.astype(BF), after)], 0)
+
+
+def second_taps(planes):
+    return jnp.concatenate([jnp.concatenate(planes[x : x + 3], 0) for x in range(len(planes) - 2)], 1)
 
 
 def inner_kernel(
-    turned, got_mate, got_far, lower1, upper1, middle2, z_sel, w3_hbm, partial1, partial2, picked, taps, w3, sem
+    turned, got_mate, got_far, lower1, upper1, middle2, w3_hbm, partial1, partial2, picked, taps, w3, sem
 ):
     load = pltpu.make_async_copy(w3_hbm, w3, sem)
     load.start()
@@ -231,7 +217,7 @@
         b = mat(upper, two_cells(taps, j, 4 * step, 3 * step))
         acc = jnp.concatenate([a[:width], a[width:] + b[: 2 * width], b[2 * width :]], 0)
         pooled.append(pool_first(acc, j, pairs, False, False))
-    partial2[...] = mat(middle2[...], second_taps(pooled, z_sel[...]))
+    partial2[...] = mat(middle2[...], second_taps(pooled))
     load.wait()
     out_rows = picked.shape[0] // 9
     own = (out_rows, w3.shape[1])
@@ -244,7 +230,7 @@
         picked[tap * out_rows : (tap + 1) * out_rows] = jnp.concatenate(pieces, 1)
 
 
-def outer_kernel(got_a, got_b, partial1, partial2, lower1, upper1, outer2, z_sel, p_sel, out, low_taps, high_taps):
+def outer_kernel(got_a, got_b, partial1, partial2, lower1, upper1, outer2, p_sel, out, low_taps, high_taps):
     planes, edge, breadth = got_a.shape
     chans = edge // EDGE
     k = lax.axis_index("yz")
@@ -269,15 +255,11 @@
     halves = []
     for y, pooled in enumerate((below, above)):
         part = slice(2 * y * width, 2 * (y + 1) * width)
-        r = relu(partial2[part] + mat(outer2[part], second_taps(pooled, z_sel[...])))
+        r = relu(partial2[part] + mat(outer2[part], second_taps(pooled)))
         t = r[:width] + r[width:]
-        cells = t.shape[1]
-        t = t + pltpu.roll(t, cells - breadth // 2, 1)
-        t = (t + pltpu.roll(t, cells - 1, 1)) * 0.125
-        halves.append(t.astype(BF))
-    for x in range(0, PLANES, 2):
-        both = [t[:, x * breadth : (x + 2) * breadth] for t in halves]
-        out[x // 2 * width : (x // 2 + 1) * width] = mat(jnp.concatenate(both, 1), p_sel[...]).astype(BF)
+        t = [t[:, 2 * x * breadth : (2 * x + 1) * breadth] + t[:, (2 * x + 1) * breadth : 2 * (x + 1) * breadth] for x in range(PLANES)]
+        halves.append([((u + pltpu.roll(u, breadth - 2, 1)) * 0.125).astype(BF) for u in t])
+    out[...] = mat(jnp.concatenate(halves[0] + halves[1], 1), p_sel[...]).astype(BF)
 
 
 def lay(tiles, rows):
@@ -298,7 +280,7 @@
     wide = blocks[0].shape[1]
     k = lax.axis_index("yz")
     for m, block in enumerate(blocks):
-        dest[:, pl.ds(pl.multiple_of((lax.div(k, 2) ^ m) * wide, wide), wide)] = block.astype(BF)
+        dest[: block.shape[0], pl.ds(pl.multiple_of((lax.div(k, 2) ^ m) * wide, wide), wide)] = block.astype(BF)
 
 
 def lay_kernel(*refs):
@@ -307,6 +289,8 @@
     even = is_even("gx")
     put_plane(mate, [jnp.where(even, b, a) for a, b in zip(low, high)])
     put_plane(far, [jnp.where(even, a, b) for a, b in zip(low, high)])
+    depth = mate.shape[0]
+    far[depth:] = jnp.zeros((far.shape[0] - depth, far.shape[1]), BF)
 
 
 def shift_taps(products, z):
@@ -326,38 +310,46 @@
     return total
 
 
-def near_kernel(z, mate, far, got_mate, w3, out, ready, pending):
+def middle_kernel(z, mate, far, w3, beside_mate, beside_far, w_mate, w_far):
     depth = mate.shape[0]
     even = is_even("gx")
-    a, b = mate[...], far[...]
+    a, b = mate[...], far[:depth]
     both = jnp.concatenate([jnp.where(even, b, a), jnp.where(even, a, b)], 0)
     w = w3[...].astype(BF)
     first, second = w[:, depth:], w[:, : 2 * depth]
-    beside = jnp.where(even, w[:, 2 * depth :], w[:, :depth])
-    t = mat(jnp.where(even, second, first), both) + mat(beside, got_mate[...])
-    done = relu(shift_taps(t, z))
-    part = shift_taps(mat(jnp.where(even, first, second), both), z)
-    ready[...] = done
-    pending[...] = part
-    part = relu(part)
-    out[...] = jnp.stack([jnp.where(even, part, done), jnp.where(even, done, part)], 1).astype(BF)
-
-
-def far_kernel(z, got_far, w3, ready, pending, _, out, block, sem):
-    depth = got_far.shape[0]
+    beside_mate[...] = shift_taps(mat(jnp.where(even, second, first), both), z)
+    beside_far[...] = shift_taps(mat(jnp.where(even, first, second), both), z)
+    w_mate[...] = jnp.where(even, w[:, 2 * depth :], w[:, :depth])
+    w_far[...] = jnp.where(even, w[:, :depth], w[:, 2 * depth :])
+
+
+def is_end():
     g = lax.axis_index("gx")
-
-    @pl.when((g > 0) & (g < lax.axis_size("gx") - 1))
+    return (g == 0) | (g == lax.axis_size("gx") - 1)
+
+
+def write_planes(beside_mate, beside_far, out, block, sem):
+    even = is_even("gx")
+    a, b = relu(beside_mate), relu(beside_far)
+    block[...] = jnp.stack([jnp.where(even, b, a), jnp.where(even, a, b)], 1).astype(BF)
+    copy = pltpu.make_async_copy(block, out, sem)
+    copy.start()
+    copy.wait()
+
+
+def near_kernel(z, beside_mate, beside_far, w_mate, got_mate, out, ready, block, sem):
+    ready[...] = beside_mate[...] + shift_taps(mat(w_mate[...], got_mate[...]), z)
+
+    @pl.when(is_end())
     def _():
-        even = is_even("gx")
-        w = w3[...].astype(BF)
-        beside = jnp.where(even, w[:, :depth], w[:, 2 * depth :])
-        part = relu(pending[...] + shift_taps(mat(beside, got_far[...]), z))
-        done = ready[...]
-        block[...] = jnp.stack([jnp.where(even, part, done), jnp.where(even, done, part)], 1).astype(BF)
-        copy = pltpu.make_async_copy(block, out, sem)
-        copy.start()
-        copy.wait()
+        write_planes(ready[...], beside_far[...], out, block, sem)
+
+
+def far_kernel(z, got_far, w_far, ready, beside_far, _, out, block, sem):
+    @pl.when(jnp.logical_not(is_end()))
+    def _():
+        part = beside_far[...] + shift_taps(mat(w_far[...], got_far[: w_far.shape[1]]), z)
+        write_planes(ready[...], part, out, block, sem)
 
 
 def per_device(volume, weight_one, weight_two, weight_three):
@@ -376,14 +368,13 @@
     got_mate = lax.ppermute(send_mate, ("gx", "yz"), near)
     got_far = lax.ppermute(send_far, ("gx", "yz"), away)
     k1, k2 = 27 * chans, 27 * c2
-    lower1, upper1, middle2, outer2, z_sel, p_sel = call(
+    lower1, upper1, middle2, outer2, p_sel = call(
         weights_kernel,
         [
             ((4 * c2, k1), BF),
             ((4 * c2, k1), BF),
             ((4 * c3, 2 * k2 // 3), BF),
             ((4 * c3, 2 * k2 // 3), BF),
-            ((2 * breadth, 2 * breadth), BF),
             ((4 * breadth, breadth), BF),
         ],
         weight_one,
@@ -413,7 +404,7 @@
         inner_kernel,
         [
             ((2, pairs, 4 * c2, 2 * breadth), F32),
-            ((4 * c3, PLANES * breadth), F32),
+            ((4 * c3, 2 * PLANES * breadth), F32),
             ((9 * out_rows, 3 * c3), F32),
         ],
         turned,
@@ -422,19 +413,18 @@
         lower1,
         upper1,
         middle2,
-        z_sel,
         weight_three.T,
         scratch=[
             pltpu.VMEM((wide, 3 * rows, breadth), BF),
             pltpu.VMEM(weight_three.shape[::-1], BF),
             pltpu.SemaphoreType.DMA,
         ],
-        hbm=(7,),
+        hbm=(6,),
         flops=2 * 300_000_000,
     )
     (tile,) = call(
         outer_kernel,
-        [((PLANES // 2 * c3, breadth), BF)],
+        [((c3, breadth), BF)],
         got_a,
         got_b,
         partial1,
@@ -442,7 +432,6 @@
         lower1,
         upper1,
         outer2,
-        z_sel,
         p_sel,
         scratch=[pltpu.VMEM((wide, 3 * edge, breadth), BF), pltpu.VMEM((wide, 3 * edge, breadth), BF)],
         flops=2 * 400_000_000,
@@ -450,28 +439,40 @@
     tiles = [tile] + [lax.ppermute(tile, "yz", [(i, i ^ d) for i in range(yz)]) for d in range(1, yz)]
     cells = yz * (height // 4) * (breadth // 4)
     z = breadth // 4
-    mate, far = call(lay_kernel, [((c3, cells), BF), ((c3, cells), BF)], tiles[0], *[tiles[d] for d in [3, 2, 1]])
+    mate, far = call(lay_kernel, [((c3, cells), BF), ((c3 + 16, cells), BF)], tiles[0], *[tiles[d] for d in [3, 2, 1]])
     got_far = lax.ppermute(far, ("gx", "yz"), away)
     got_mate = lax.ppermute(mate, ("gx", "yz"), near)
     shape = (out_rows, 2, cells)
-    out, ready, pending = call(
-        functools.partial(near_kernel, z),
-        [(shape, BF), ((out_rows, cells), F32), ((out_rows, cells), F32)],
+    plane, weights = ((out_rows, cells), F32), ((9 * out_rows, c3), BF)
+    beside_mate, beside_far, w_mate, w_far = call(
+        functools.partial(middle_kernel, z),
+        [plane, plane, weights, weights],
         mate,
         far,
+        picked,
+        flops=2 * 32 * 1152 * 512,
+    )
+    block = [pltpu.VMEM(shape, BF), pltpu.SemaphoreType.DMA]
+    out, ready = call(
+        functools.partial(near_kernel, z),
+        [(shape, BF), plane],
+        beside_mate,
+        beside_far,
+        w_mate,
         got_mate,
-        picked,
-        flops=2 * 32 * 1728 * 512,
+        scratch=block,
+        hbm_out=True,
+        free=True,
     )
     (out,) = call(
         functools.partial(far_kernel, z),
         [(shape, BF)],
         got_far,
-        picked,
+        w_far,
         ready,
-        pending,
+        beside_far,
         out,
-        scratch=[pltpu.VMEM(shape, BF), pltpu.SemaphoreType.DMA],
+        scratch=block,
         hbm=(4,),
         hbm_out=True,
         aliases={4: 0},

time: 28.2 us -> 27.8 us (0.986)
    ppermute x1, starting transfers between devices: 2.83 us -> 0.01 us  [per_device(): got_mate = lax.ppermute(mate, ('gx', 'yz'), near)]
    ppermute x1, starting transfers between devices: 1.3 us -> 4.05 us  [per_device(): got_far = lax.ppermute(far, ('gx', 'yz'), away)]
    ppermute x1, waiting for transfers between devices: 0.01 us -> 0.62 us  [per_device(): got_mate = lax.ppermute(mate, ('gx', 'yz'), near)]
    ppermute x1, waiting for transfers between devices: 1.05 us -> 0.44 us  [per_device(): got_far = lax.ppermute(far, ('gx', 'yz'), away)]
    pallas_call x8 -> x9, Pallas kernels: 7.16 us -> 6.92 us  [call(): pl.pallas_call(body, out_shape=[jax.ShapeDtypeStruct(s, d) for s, d in ou...]
  transfers between devices with their start and end apart: 9 -> 9, of which waited for: 5 -> 6; matrix products, arithmetic and copies ran while one was open for 0% -> 0% of each run, Pallas kernels for 15% -> 15%
where the time goes in v6:
time: 27.8 us; the launch traced here: 27.6 us
  starting transfers between devices  13.3 us (48%)
  Pallas kernels  6.92 us (25%)
  waiting for transfers between devices  6.37 us (23%)
  local copies, waits for them, and re-layouts  0.95 us (3%)
    pallas_call x9, Pallas kernels, call(): pl.pallas_call(body, out_shape=[jax.ShapeDtypeStruct(s, d) for s, d in ou...  6.92 us
    ppermute x1, starting transfers between devices, per_device(): got_far = lax.ppermute(far, ('gx', 'yz'), away)  4.05 us
    ppermute x3, starting transfers between devices, per_device(): lax.ppermute(tile, 'yz', [(i, i ^ d) for i in range(yz)])  3.61 us
    ppermute x3, waiting for transfers between devices, per_device(): lax.ppermute(tile, 'yz', [(i, i ^ d) for i in range(yz)])  3.23 us
    ppermute x1, starting transfers between devices, per_device(): got_far = lax.ppermute(send_far, ('gx', 'yz'), away)  2.67 us
    ppermute x1, starting transfers between devices, per_device(): got_a = lax.ppermute(send_a, ('gx', 'yz'), yz_pairs(gx, yz, False))  1.44 us
    ppermute x1, waiting for transfers between devices, per_device(): got_far = lax.ppermute(send_far, ('gx', 'yz'), away)  1.09 us
    ppermute x1, starting transfers between devices, per_device(): got_b = lax.ppermute(send_b, ('gx', 'yz'), yz_pairs(gx, yz, True))  1.04 us
  transfers between devices with their start and end apart: 9, of which 6 were waited for; matrix products, arithmetic and copies ran while one was open for 0% of the time, Pallas kernels for 15%

profile of v6, /device:TPU:1, one launch (start us, length us, event | category | flops | bytes accessed | tf_op | source)
XLA Modules:
  0.0 27.6 jit_solution(6126188430959960169)
XLA Ops:
  0.0 0.9 %copy-done = bf16[8,16,8,128]{3,2,1,0:T(8,128)(2,1)S(1)} copy-done((bf16[8,16,8,128]{3,2,1,0:T(8,128)(2,1)S(1)}, bf16[8,16,8,128]{3,2,1,0:T(8,128)(2,1)}, u32[]{:S(2)}) %copy-start) | copy-done | bytes 262168
  1.0 0.2 shard_map.46
  1.2 2.7 %collective-permute-start = (bf16[3,128,128]{2,1,0:T(8,128)(2,1)S(1)}, bf16[3,128,128]{2,1,0:T(8,128)(2,1)S(1)}, u32[]{:S(2)}, u32[]{:S(2)}) collective-permute-start(bf16[3,128,128]{2,1,0:T(8,128)(2,1)S(1)} %get-tuple-element.27), channel_id=1, source_target_pairs={{0,1},{1,0},{2,3},{3,2},{4,8},{5,9},{6,10},{7,11},{8,4},{9,5},{10,... | collective-permute-start | bytes 294920 | tf_op jit(solution)/shard_map/ppermute | solution.py:369
  3.9 0.5 %collective-permute-start.1 = (bf16[3,128,128]{2,1,0:T(8,128)(2,1)S(1)}, bf16[3,128,128]{2,1,0:T(8,128)(2,1)S(1)}, u32[]{:S(2)}, u32[]{:S(2)}) collective-permute-start(bf16[3,128,128]{2,1,0:T(8,128)(2,1)S(1)} %get-tuple-element.28), channel_id=1, source_target_pairs={{0,4},{1,5},{2,6},{3,7},{4,0},{5,1},{6,2},{7,3},{8,12},{9,13},{10,... | collective-permute-start | bytes 294920 | tf_op jit(solution)/shard_map/ppermute | solution.py:368
  4.4 1.1 %shard_map.47 = (bf16[128,432]{1,0:T(8,128)(2,1)S(1)}, bf16[128,432]{1,0:T(8,128)(2,1)S(1)}, bf16[256,576]{1,0:T(8,128)(2,1)S(1)}, bf16[256,576]{1,0:T(8,128)(2,1)S(1)}, bf16[512,128]{1,0:T(8,128)(2,1)S(1)}) custom-call(bf16[32,432]{1,0:T(8,128)(2,1)} %w1_hbm.1, bf16[64,864]{1,0:T(8,128)(2,1)} %w2_hbm.1), custom_call_target="tpu_custom_call" | custom-call | flops 191102976 | bytes 138240 | tf_op jit(solution)/shard_map/pallas_call | solution.py:32
  5.5 1.1 %collective-permute-done.got_far = bf16[3,128,128]{2,1,0:T(8,128)(2,1)S(1)} collective-permute-done((bf16[3,128,128]{2,1,0:T(8,128)(2,1)S(1)}, bf16[3,128,128]{2,1,0:T(8,128)(2,1)S(1)}, u32[]{:S(2)}, u32[]{:S(2)}) %collective-permute-start) | collective-permute-done | bytes 98336 | tf_op jit(solution)/shard_map/ppermute | solution.py:369
  6.6 0.1 shard_map.48
  6.6 1.4 %collective-permute-start.2 = (bf16[14,48,128]{2,1,0:T(8,128)(2,1)S(1)}, bf16[14,48,128]{2,1,0:T(8,128)(2,1)S(1)}, u32[]{:S(2)}, u32[]{:S(2)}) collective-permute-start(bf16[14,48,128]{2,1,0:T(8,128)(2,1)S(1)} %get-tuple-element.30), channel_id=1, source_target_pairs={{0,1},{1,0},{2,3},{3,2},{4,5},{5,4},{6,7},{7,6},{8,9},{9,8},{10,11... | collective-permute-start | bytes 516104 | tf_op jit(solution)/shard_map/ppermute | solution.py:400
  8.1 1.0 %collective-permute-start.3 = (bf16[14,48,128]{2,1,0:T(8,128)(2,1)S(1)}, bf16[14,48,128]{2,1,0:T(8,128)(2,1)S(1)}, u32[]{:S(2)}, u32[]{:S(2)}) collective-permute-start(bf16[14,48,128]{2,1,0:T(8,128)(2,1)S(1)} %get-tuple-element.31), channel_id=1, source_target_pairs={{0,4},{1,2},{2,1},{3,7},{4,0},{5,6},{6,5},{7,3},{8,12},{9,10},{10,... | collective-permute-start | bytes 516104 | tf_op jit(solution)/shard_map/ppermute | solution.py:399
  9.1 2.2 %shard_map.49 = (f32[2,6,128,256]{3,2,1,0:T(8,128)S(1)}, f32[256,512]{1,0:T(8,128)S(1)}, f32[288,192]{1,0:T(8,128)S(1)}) custom-call(bf16[8,128,128]{2,1,0:T(8,128)(2,1)S(1)} %get-tuple-element.26.turned, bf16[3,128,128]{2,1,0:T(8,128)(2,1)S(1)} %collective-permute-done.1.got_mate, bf16[3,128,128]{2,1,0:T(8,128)(2,1)S(1)} %collective-permute-done.got_far, ...), custom_call_target="tpu_custom_call" | custom-call | flops 600000000 | bytes 1417216 | tf_op jit(solution)/shard_map/pallas_call | solution.py:32
  11.3 1.0 %collective-permute-done.2.got_a = bf16[14,48,128]{2,1,0:T(8,128)(2,1)S(1)} collective-permute-done((bf16[14,48,128]{2,1,0:T(8,128)(2,1)S(1)}, bf16[14,48,128]{2,1,0:T(8,128)(2,1)S(1)}, u32[]{:S(2)}, u32[]{:S(2)}) %collective-permute-start.2) | collective-permute-done | bytes 172064 | tf_op jit(solution)/shard_map/ppermute | solution.py:400
  12.3 1.3 %shard_map.50.refs_0_ = bf16[64,128]{1,0:T(8,128)(2,1)S(1)} custom-call(bf16[14,48,128]{2,1,0:T(8,128)(2,1)S(1)} %collective-permute-done.2.got_a, bf16[14,48,128]{2,1,0:T(8,128)(2,1)S(1)} %collective-permute-done.3.got_b, f32[2,6,128,256]{3,2,1,0:T(8,128)S(1)} %get-tuple-element.35.partial1, f32[256,512]{1,0:T(8,128)S(1)} %get-tuple-element.36.partial2, ...), custom_call_target="tpu_custom_call" | custom-call | flops 800000000 | bytes 3088384 | tf_op jit(solution)/shard_map/pallas_call | solution.py:32
  13.6 3.0 %collective-permute-start.4 = (bf16[64,128]{1,0:T(8,128)(2,1)S(1)}, bf16[64,128]{1,0:T(8,128)(2,1)S(1)}, u32[]{:S(2)}, u32[]{:S(2)}) collective-permute-start(bf16[64,128]{1,0:T(8,128)(2,1)S(1)} %shard_map.50.refs_0_), channel_id=1, source_target_pairs={{0,3},{1,2},{2,1},{3,0},{4,7},{5,6},{6,5},{7,4},{8,11},{9,10},{10,... | collective-permute-start | bytes 49160 | tf_op jit(solution)/shard_map/ppermute | solution.py:439
  16.7 0.3 %collective-permute-start.5 = (bf16[64,128]{1,0:T(8,128)(2,1)S(1)}, bf16[64,128]{1,0:T(8,128)(2,1)S(1)}, u32[]{:S(2)}, u32[]{:S(2)}) collective-permute-start(bf16[64,128]{1,0:T(8,128)(2,1)S(1)} %shard_map.50.refs_0_), channel_id=1, source_target_pairs={{0,2},{1,3},{2,0},{3,1},{4,6},{5,7},{6,4},{7,5},{8,10},{9,11},{10,... | collective-permute-start | bytes 49160 | tf_op jit(solution)/shard_map/ppermute | solution.py:439
  16.9 0.3 %collective-permute-start.6 = (bf16[64,128]{1,0:T(8,128)(2,1)S(1)}, bf16[64,128]{1,0:T(8,128)(2,1)S(1)}, u32[]{:S(2)}, u32[]{:S(2)}) collective-permute-start(bf16[64,128]{1,0:T(8,128)(2,1)S(1)} %shard_map.50.refs_0_), channel_id=1, source_target_pairs={{0,1},{1,0},{2,3},{3,2},{4,5},{5,4},{6,7},{7,6},{8,9},{9,8},{10,11... | collective-permute-start | bytes 49160 | tf_op jit(solution)/shard_map/ppermute | solution.py:439
  17.2 0.9 %collective-permute-done.4.refs_1_ = bf16[64,128]{1,0:T(8,128)(2,1)S(1)} collective-permute-done((bf16[64,128]{1,0:T(8,128)(2,1)S(1)}, bf16[64,128]{1,0:T(8,128)(2,1)S(1)}, u32[]{:S(2)}, u32[]{:S(2)}) %collective-permute-start.4) | collective-permute-done | bytes 16416 | tf_op jit(solution)/shard_map/ppermute | solution.py:439
  18.2 2.3 %collective-permute-done.5.refs_2_ = bf16[64,128]{1,0:T(8,128)(2,1)S(1)} collective-permute-done((bf16[64,128]{1,0:T(8,128)(2,1)S(1)}, bf16[64,128]{1,0:T(8,128)(2,1)S(1)}, u32[]{:S(2)}, u32[]{:S(2)}) %collective-permute-start.5) | collective-permute-done | bytes 16416 | tf_op jit(solution)/shard_map/ppermute | solution.py:439
  20.5 0.1 shard_map.51
  20.6 4.0 %collective-permute-start.7 = (bf16[80,256]{1,0:T(8,128)(2,1)S(1)}, bf16[80,256]{1,0:T(8,128)(2,1)S(1)}, u32[]{:S(2)}, u32[]{:S(2)}) collective-permute-start(bf16[80,256]{1,0:T(8,128)(2,1)S(1)} %get-tuple-element.38.far), channel_id=1, source_target_pairs={{0,1},{1,0},{2,3},{3,2},{4,8},{5,9},{6,10},{7,11},{8,4},{9,5},{10,... | collective-permute-start | bytes 122888 | tf_op jit(solution)/shard_map/ppermute | solution.py:443
  24.6 0.6 %shard_map.52 = (f32[32,256]{1,0:T(8,128)S(1)}, f32[32,256]{1,0:T(8,128)S(1)}, bf16[288,64]{1,0:T(8,128)(2,1)S(1)}, bf16[288,64]{1,0:T(8,128)(2,1)S(1)}) custom-call(bf16[64,256]{1,0:T(8,128)(2,1)S(1)} %get-tuple-element.39.mate, bf16[80,256]{1,0:T(8,128)(2,1)S(1)} %get-tuple-element.38.far, f32[288,192]{1,0:T(8,128)S(1)} %get-tuple-element.40.w3), custom_call_target="tpu_custom_call" | custom-call | flops 37748736 | bytes 294912 | tf_op jit(solution)/shard_map/pallas_call | solution.py:32
  25.2 0.6 %collective-permute-done.8.got_mate = bf16[64,256]{1,0:T(8,128)(2,1)S(1)} collective-permute-done((bf16[64,256]{1,0:T(8,128)(2,1)S(1)}, bf16[64,256]{1,0:T(8,128)(2,1)S(1)}, u32[]{:S(2)}, u32[]{:S(2)}) %collective-permute-start.8) | collective-permute-done | bytes 32800 | tf_op jit(solution)/shard_map/ppermute | solution.py:444
  25.8 0.3 %shard_map.53 = (bf16[32,2,256]{2,1,0:T(2,128)(2,1)}, f32[32,256]{1,0:T(8,128)S(1)}) custom-call(f32[32,256]{1,0:T(8,128)S(1)} %get-tuple-element.42.beside_mate, f32[32,256]{1,0:T(8,128)S(1)} %get-tuple-element.43.beside_far, bf16[288,64]{1,0:T(8,128)(2,1)S(1)} %get-tuple-element.44.w_mate, bf16[64,256]{1,0:T(8,128)(2,1)S(1)} %collective-permute-done.8.got_mate), custom_call_target="tpu_custom_call" | custom-call | tf_op jit(solution)/shard_map/pallas_call | solution.py:32
  26.2 0.4 %collective-permute-done.7.got_far = bf16[80,256]{1,0:T(8,128)(2,1)S(1)} collective-permute-done((bf16[80,256]{1,0:T(8,128)(2,1)S(1)}, bf16[80,256]{1,0:T(8,128)(2,1)S(1)}, u32[]{:S(2)}, u32[]{:S(2)}) %collective-permute-start.7) | collective-permute-done | bytes 40992 | tf_op jit(solution)/shard_map/ppermute | solution.py:443
  26.6 1.0 %shard_map.54 = bf16[32,2,256]{2,1,0:T(2,128)(2,1)} custom-call(bf16[80,256]{1,0:T(8,128)(2,1)S(1)} %collective-permute-done.7.got_far, bf16[288,64]{1,0:T(8,128)(2,1)S(1)} %get-tuple-element.41.w_far, f32[32,256]{1,0:T(8,128)S(1)} %get-tuple-element.45.ready, f32[32,256]{1,0:T(8,128)S(1)} %get-tuple-element.43.beside_far, ...), custom_call_target="tpu_custom_call", output_to_operand_aliasing={{}: (4, {})} | custom-call | flops 9437184 | bytes 176128 | tf_op jit(solution)/shard_map/pallas_call | solution.py:32
  (5 shorter events, 0.0 us)
Async XLA Ops:
  0.0 0.9 %copy-start = (bf16[8,16,8,128]{3,2,1,0:T(8,128)(2,1)S(1)}, bf16[8,16,8,128]{3,2,1,0:T(8,128)(2,1)}, u32[]{:S(2)}) copy-start(bf16[8,16,8,128]{3,2,1,0:T(8,128)(2,1)} %vol.1) | copy-start | bytes 786436
  1.2 5.4 %collective-permute-start = (bf16[3,128,128]{2,1,0:T(8,128)(2,1)S(1)}, bf16[3,128,128]{2,1,0:T(8,128)(2,1)S(1)}, u32[]{:S(2)}, u32[]{:S(2)}) collective-permute-start(bf16[3,128,128]{2,1,0:T(8,128)(2,1)S(1)} %get-tuple-element.27), channel_id=1, source_target_pairs={{0,1},{1,0},{2,3},{3,2},{4,8},{5,9},{6,10},{7,11},{8,4},{9,5},{10,... | collective-permute-start | bytes 294920 | tf_op jit(solution)/shard_map/ppermute | solution.py:369
  3.9 2.7 %collective-permute-start.1 = (bf16[3,128,128]{2,1,0:T(8,128)(2,1)S(1)}, bf16[3,128,128]{2,1,0:T(8,128)(2,1)S(1)}, u32[]{:S(2)}, u32[]{:S(2)}) collective-permute-start(bf16[3,128,128]{2,1,0:T(8,128)(2,1)S(1)} %get-tuple-element.28), channel_id=1, source_target_pairs={{0,4},{1,5},{2,6},{3,7},{4,0},{5,1},{6,2},{7,3},{8,12},{9,13},{10,... | collective-permute-start | bytes 294920 | tf_op jit(solution)/shard_map/ppermute | solution.py:368
  6.6 5.6 %collective-permute-start.2 = (bf16[14,48,128]{2,1,0:T(8,128)(2,1)S(1)}, bf16[14,48,128]{2,1,0:T(8,128)(2,1)S(1)}, u32[]{:S(2)}, u32[]{:S(2)}) collective-permute-start(bf16[14,48,128]{2,1,0:T(8,128)(2,1)S(1)} %get-tuple-element.30), channel_id=1, source_target_pairs={{0,1},{1,0},{2,3},{3,2},{4,5},{5,4},{6,7},{7,6},{8,9},{9,8},{10,11... | collective-permute-start | bytes 516104 | tf_op jit(solution)/shard_map/ppermute | solution.py:400
  8.1 4.2 %collective-permute-start.3 = (bf16[14,48,128]{2,1,0:T(8,128)(2,1)S(1)}, bf16[14,48,128]{2,1,0:T(8,128)(2,1)S(1)}, u32[]{:S(2)}, u32[]{:S(2)}) collective-permute-start(bf16[14,48,128]{2,1,0:T(8,128)(2,1)S(1)} %get-tuple-element.31), channel_id=1, source_target_pairs={{0,4},{1,2},{2,1},{3,7},{4,0},{5,6},{6,5},{7,3},{8,12},{9,10},{10,... | collective-permute-start | bytes 516104 | tf_op jit(solution)/shard_map/ppermute | solution.py:399
  13.6 4.6 %collective-permute-start.4 = (bf16[64,128]{1,0:T(8,128)(2,1)S(1)}, bf16[64,128]{1,0:T(8,128)(2,1)S(1)}, u32[]{:S(2)}, u32[]{:S(2)}) collective-permute-start(bf16[64,128]{1,0:T(8,128)(2,1)S(1)} %shard_map.50.refs_0_), channel_id=1, source_target_pairs={{0,3},{1,2},{2,1},{3,0},{4,7},{5,6},{6,5},{7,4},{8,11},{9,10},{10,... | collective-permute-start | bytes 49160 | tf_op jit(solution)/shard_map/ppermute | solution.py:439
  16.7 3.8 %collective-permute-start.5 = (bf16[64,128]{1,0:T(8,128)(2,1)S(1)}, bf16[64,128]{1,0:T(8,128)(2,1)S(1)}, u32[]{:S(2)}, u32[]{:S(2)}) collective-permute-start(bf16[64,128]{1,0:T(8,128)(2,1)S(1)} %shard_map.50.refs_0_), channel_id=1, source_target_pairs={{0,2},{1,3},{2,0},{3,1},{4,6},{5,7},{6,4},{7,5},{8,10},{9,11},{10,... | collective-permute-start | bytes 49160 | tf_op jit(solution)/shard_map/ppermute | solution.py:439
  16.9 3.5 %collective-permute-start.6 = (bf16[64,128]{1,0:T(8,128)(2,1)S(1)}, bf16[64,128]{1,0:T(8,128)(2,1)S(1)}, u32[]{:S(2)}, u32[]{:S(2)}) collective-permute-start(bf16[64,128]{1,0:T(8,128)(2,1)S(1)} %shard_map.50.refs_0_), channel_id=1, source_target_pairs={{0,1},{1,0},{2,3},{3,2},{4,5},{5,4},{6,7},{7,6},{8,9},{9,8},{10,11... | collective-permute-start | bytes 49160 | tf_op jit(solution)/shard_map/ppermute | solution.py:439
  20.6 6.0 %collective-permute-start.7 = (bf16[80,256]{1,0:T(8,128)(2,1)S(1)}, bf16[80,256]{1,0:T(8,128)(2,1)S(1)}, u32[]{:S(2)}, u32[]{:S(2)}) collective-permute-start(bf16[80,256]{1,0:T(8,128)(2,1)S(1)} %get-tuple-element.38.far), channel_id=1, source_target_pairs={{0,1},{1,0},{2,3},{3,2},{4,8},{5,9},{6,10},{7,11},{8,4},{9,5},{10,... | collective-permute-start | bytes 122888 | tf_op jit(solution)/shard_map/ppermute | solution.py:443
  24.6 1.2 %collective-permute-start.8 = (bf16[64,256]{1,0:T(8,128)(2,1)S(1)}, bf16[64,256]{1,0:T(8,128)(2,1)S(1)}, u32[]{:S(2)}, u32[]{:S(2)}) collective-permute-start(bf16[64,256]{1,0:T(8,128)(2,1)S(1)} %get-tuple-element.39.mate), channel_id=1, source_target_pairs={{0,4},{1,5},{2,6},{3,7},{4,0},{5,1},{6,2},{7,3},{8,12},{9,13},{10,... | collective-permute-start | bytes 98312 | tf_op jit(solution)/shard_map/ppermute | solution.py:444

commit v7 on v6

--- a/solution.py
+++ b/solution.py
@@ -244,18 +244,18 @@
     lower, upper = lower1[: 3 * width], upper1[width:]
     rows = 3 * edge
     below, above = [], []
+    lows = [mat(lower, two_cells(low_taps, j, 0, rows)) for j in range(pairs)]
+    highs = [mat(upper, two_cells(high_taps, j, 0, rows)) for j in range(pairs)]
     for j in range(pairs):
         p = partial1[0, j]
-        a = p[: 3 * width] + mat(lower, two_cells(low_taps, j, 0, rows))
-        below.append(pool_first(jnp.concatenate([a, p[3 * width :]], 0), j, pairs, first, False))
+        below.append(pool_first(jnp.concatenate([p[: 3 * width] + lows[j], p[3 * width :]], 0), j, pairs, first, False))
         p = partial1[1, j]
-        b = p[width:] + mat(upper, two_cells(high_taps, j, 0, rows))
-        above.append(pool_first(jnp.concatenate([p[:width], b], 0), j, pairs, False, last))
+        above.append(pool_first(jnp.concatenate([p[:width], p[width:] + highs[j]], 0), j, pairs, False, last))
     width = outer2.shape[0] // 4
+    sums = [mat(outer2[2 * y * width : 2 * (y + 1) * width], second_taps(p)) for y, p in enumerate((below, above))]
     halves = []
-    for y, pooled in enumerate((below, above)):
-        part = slice(2 * y * width, 2 * (y + 1) * width)
-        r = relu(partial2[part] + mat(outer2[part], second_taps(pooled)))
+    for y in range(2):
+        r = relu(partial2[2 * y * width : 2 * (y + 1) * width] + sums[y])
         t = r[:width] + r[width:]
         t = [t[:, 2 * x * breadth : (2 * x + 1) * breadth] + t[:, (2 * x + 1) * breadth : 2 * (x + 1) * breadth] for x in range(PLANES)]
         halves.append([((u + pltpu.roll(u, breadth - 2, 1)) * 0.125).astype(BF) for u in t])
@@ -331,7 +331,9 @@
 def write_planes(beside_mate, beside_far, out, block, sem):
     even = is_even("gx")
     a, b = relu(beside_mate), relu(beside_far)
-    block[...] = jnp.stack([jnp.where(even, b, a), jnp.where(even, a, b)], 1).astype(BF)
+    rows, cells = a.shape
+    pair = jnp.concatenate([jnp.where(even, b, a), jnp.where(even, a, b)], 1)
+    block[...] = pair.astype(BF).reshape(rows, 2, cells)
     copy = pltpu.make_async_copy(block, out, sem)
     copy.start()
     copy.wait()

time: 27.8 us -> 27.7 us (level)
  no operation moved by 1% of the time
where the time goes in v7:
time: 27.7 us; the launch traced here: 27.5 us
  starting transfers between devices  13.3 us (48%)
  Pallas kernels  6.83 us (25%)
  waiting for transfers between devices  6.37 us (23%)
  local copies, waits for them, and re-layouts  0.95 us (3%)
    pallas_call x9, Pallas kernels, call(): pl.pallas_call(body, out_shape=[jax.ShapeDtypeStruct(s, d) for s, d in ou...  6.83 us
    ppermute x1, starting transfers between devices, per_device(): got_far = lax.ppermute(far, ('gx', 'yz'), away)  4.06 us
    ppermute x3, starting transfers between devices, per_device(): lax.ppermute(tile, 'yz', [(i, i ^ d) for i in range(yz)])  3.61 us
    ppermute x3, waiting for transfers between devices, per_device(): lax.ppermute(tile, 'yz', [(i, i ^ d) for i in range(yz)])  3.23 us
    ppermute x1, starting transfers between devices, per_device(): got_far = lax.ppermute(send_far, ('gx', 'yz'), away)  2.67 us
    ppermute x1, starting transfers between devices, per_device(): got_a = lax.ppermute(send_a, ('gx', 'yz'), yz_pairs(gx, yz, False))  1.44 us
    ppermute x1, waiting for transfers between devices, per_device(): got_far = lax.ppermute(send_far, ('gx', 'yz'), away)  1.09 us
    ppermute x1, starting transfers between devices, per_device(): got_b = lax.ppermute(send_b, ('gx', 'yz'), yz_pairs(gx, yz, True))  1.04 us
  transfers between devices with their start and end apart: 9, of which 6 were waited for; matrix products, arithmetic and copies ran while one was open for 0% of the time, Pallas kernels for 15%

profile of v7, /device:TPU:1, one launch (start us, length us, event | category | flops | bytes accessed | tf_op | source)
XLA Modules:
  0.0 27.5 jit_solution(17182106212693523109)
XLA Ops:
  0.0 0.9 %copy-done = bf16[8,16,8,128]{3,2,1,0:T(8,128)(2,1)S(1)} copy-done((bf16[8,16,8,128]{3,2,1,0:T(8,128)(2,1)S(1)}, bf16[8,16,8,128]{3,2,1,0:T(8,128)(2,1)}, u32[]{:S(2)}) %copy-start) | copy-done | bytes 262168
  1.0 0.2 shard_map.46
  1.2 2.7 %collective-permute-start = (bf16[3,128,128]{2,1,0:T(8,128)(2,1)S(1)}, bf16[3,128,128]{2,1,0:T(8,128)(2,1)S(1)}, u32[]{:S(2)}, u32[]{:S(2)}) collective-permute-start(bf16[3,128,128]{2,1,0:T(8,128)(2,1)S(1)} %get-tuple-element.27), channel_id=1, source_target_pairs={{0,1},{1,0},{2,3},{3,2},{4,8},{5,9},{6,10},{7,11},{8,4},{9,5},{10,... | collective-permute-start | bytes 294920 | tf_op jit(solution)/shard_map/ppermute | solution.py:371
  3.9 0.5 %collective-permute-start.1 = (bf16[3,128,128]{2,1,0:T(8,128)(2,1)S(1)}, bf16[3,128,128]{2,1,0:T(8,128)(2,1)S(1)}, u32[]{:S(2)}, u32[]{:S(2)}) collective-permute-start(bf16[3,128,128]{2,1,0:T(8,128)(2,1)S(1)} %get-tuple-element.28), channel_id=1, source_target_pairs={{0,4},{1,5},{2,6},{3,7},{4,0},{5,1},{6,2},{7,3},{8,12},{9,13},{10,... | collective-permute-start | bytes 294920 | tf_op jit(solution)/shard_map/ppermute | solution.py:370
  4.4 1.1 %shard_map.47 = (bf16[128,432]{1,0:T(8,128)(2,1)S(1)}, bf16[128,432]{1,0:T(8,128)(2,1)S(1)}, bf16[256,576]{1,0:T(8,128)(2,1)S(1)}, bf16[256,576]{1,0:T(8,128)(2,1)S(1)}, bf16[512,128]{1,0:T(8,128)(2,1)S(1)}) custom-call(bf16[32,432]{1,0:T(8,128)(2,1)} %w1_hbm.1, bf16[64,864]{1,0:T(8,128)(2,1)} %w2_hbm.1), custom_call_target="tpu_custom_call" | custom-call | flops 191102976 | bytes 138240 | tf_op jit(solution)/shard_map/pallas_call | solution.py:32
  5.5 1.1 %collective-permute-done.got_far = bf16[3,128,128]{2,1,0:T(8,128)(2,1)S(1)} collective-permute-done((bf16[3,128,128]{2,1,0:T(8,128)(2,1)S(1)}, bf16[3,128,128]{2,1,0:T(8,128)(2,1)S(1)}, u32[]{:S(2)}, u32[]{:S(2)}) %collective-permute-start) | collective-permute-done | bytes 98336 | tf_op jit(solution)/shard_map/ppermute | solution.py:371
  6.6 0.1 shard_map.48
  6.6 1.4 %collective-permute-start.2 = (bf16[14,48,128]{2,1,0:T(8,128)(2,1)S(1)}, bf16[14,48,128]{2,1,0:T(8,128)(2,1)S(1)}, u32[]{:S(2)}, u32[]{:S(2)}) collective-permute-start(bf16[14,48,128]{2,1,0:T(8,128)(2,1)S(1)} %get-tuple-element.30), channel_id=1, source_target_pairs={{0,1},{1,0},{2,3},{3,2},{4,5},{5,4},{6,7},{7,6},{8,9},{9,8},{10,11... | collective-permute-start | bytes 516104 | tf_op jit(solution)/shard_map/ppermute | solution.py:402
  8.1 1.0 %collective-permute-start.3 = (bf16[14,48,128]{2,1,0:T(8,128)(2,1)S(1)}, bf16[14,48,128]{2,1,0:T(8,128)(2,1)S(1)}, u32[]{:S(2)}, u32[]{:S(2)}) collective-permute-start(bf16[14,48,128]{2,1,0:T(8,128)(2,1)S(1)} %get-tuple-element.31), channel_id=1, source_target_pairs={{0,4},{1,2},{2,1},{3,7},{4,0},{5,6},{6,5},{7,3},{8,12},{9,10},{10,... | collective-permute-start | bytes 516104 | tf_op jit(solution)/shard_map/ppermute | solution.py:401
  9.1 2.2 %shard_map.49 = (f32[2,6,128,256]{3,2,1,0:T(8,128)S(1)}, f32[256,512]{1,0:T(8,128)S(1)}, f32[288,192]{1,0:T(8,128)S(1)}) custom-call(bf16[8,128,128]{2,1,0:T(8,128)(2,1)S(1)} %get-tuple-element.26.turned, bf16[3,128,128]{2,1,0:T(8,128)(2,1)S(1)} %collective-permute-done.1.got_mate, bf16[3,128,128]{2,1,0:T(8,128)(2,1)S(1)} %collective-permute-done.got_far, ...), custom_call_target="tpu_custom_call" | custom-call | flops 600000000 | bytes 1417216 | tf_op jit(solution)/shard_map/pallas_call | solution.py:32
  11.3 1.0 %collective-permute-done.2.got_a = bf16[14,48,128]{2,1,0:T(8,128)(2,1)S(1)} collective-permute-done((bf16[14,48,128]{2,1,0:T(8,128)(2,1)S(1)}, bf16[14,48,128]{2,1,0:T(8,128)(2,1)S(1)}, u32[]{:S(2)}, u32[]{:S(2)}) %collective-permute-start.2) | collective-permute-done | bytes 172064 | tf_op jit(solution)/shard_map/ppermute | solution.py:402
  12.3 1.3 %shard_map.50.refs_0_ = bf16[64,128]{1,0:T(8,128)(2,1)S(1)} custom-call(bf16[14,48,128]{2,1,0:T(8,128)(2,1)S(1)} %collective-permute-done.2.got_a, bf16[14,48,128]{2,1,0:T(8,128)(2,1)S(1)} %collective-permute-done.3.got_b, f32[2,6,128,256]{3,2,1,0:T(8,128)S(1)} %get-tuple-element.35.partial1, f32[256,512]{1,0:T(8,128)S(1)} %get-tuple-element.36.partial2, ...), custom_call_target="tpu_custom_call" | custom-call | flops 800000000 | bytes 3088384 | tf_op jit(solution)/shard_map/pallas_call | solution.py:32
  13.6 3.0 %collective-permute-start.4 = (bf16[64,128]{1,0:T(8,128)(2,1)S(1)}, bf16[64,128]{1,0:T(8,128)(2,1)S(1)}, u32[]{:S(2)}, u32[]{:S(2)}) collective-permute-start(bf16[64,128]{1,0:T(8,128)(2,1)S(1)} %shard_map.50.refs_0_), channel_id=1, source_target_pairs={{0,3},{1,2},{2,1},{3,0},{4,7},{5,6},{6,5},{7,4},{8,11},{9,10},{10,... | collective-permute-start | bytes 49160 | tf_op jit(solution)/shard_map/ppermute | solution.py:441
  16.6 0.3 %collective-permute-start.5 = (bf16[64,128]{1,0:T(8,128)(2,1)S(1)}, bf16[64,128]{1,0:T(8,128)(2,1)S(1)}, u32[]{:S(2)}, u32[]{:S(2)}) collective-permute-start(bf16[64,128]{1,0:T(8,128)(2,1)S(1)} %shard_map.50.refs_0_), channel_id=1, source_target_pairs={{0,2},{1,3},{2,0},{3,1},{4,6},{5,7},{6,4},{7,5},{8,10},{9,11},{10,... | collective-permute-start | bytes 49160 | tf_op jit(solution)/shard_map/ppermute | solution.py:441
  16.9 0.3 %collective-permute-start.6 = (bf16[64,128]{1,0:T(8,128)(2,1)S(1)}, bf16[64,128]{1,0:T(8,128)(2,1)S(1)}, u32[]{:S(2)}, u32[]{:S(2)}) collective-permute-start(bf16[64,128]{1,0:T(8,128)(2,1)S(1)} %shard_map.50.refs_0_), channel_id=1, source_target_pairs={{0,1},{1,0},{2,3},{3,2},{4,5},{5,4},{6,7},{7,6},{8,9},{9,8},{10,11... | collective-permute-start | bytes 49160 | tf_op jit(solution)/shard_map/ppermute | solution.py:441
  17.2 0.9 %collective-permute-done.4.refs_1_ = bf16[64,128]{1,0:T(8,128)(2,1)S(1)} collective-permute-done((bf16[64,128]{1,0:T(8,128)(2,1)S(1)}, bf16[64,128]{1,0:T(8,128)(2,1)S(1)}, u32[]{:S(2)}, u32[]{:S(2)}) %collective-permute-start.4) | collective-permute-done | bytes 16416 | tf_op jit(solution)/shard_map/ppermute | solution.py:441
  18.1 2.3 %collective-permute-done.5.refs_2_ = bf16[64,128]{1,0:T(8,128)(2,1)S(1)} collective-permute-done((bf16[64,128]{1,0:T(8,128)(2,1)S(1)}, bf16[64,128]{1,0:T(8,128)(2,1)S(1)}, u32[]{:S(2)}, u32[]{:S(2)}) %collective-permute-start.5) | collective-permute-done | bytes 16416 | tf_op jit(solution)/shard_map/ppermute | solution.py:441
  20.4 0.1 shard_map.51
  20.5 4.1 %collective-permute-start.7 = (bf16[80,256]{1,0:T(8,128)(2,1)S(1)}, bf16[80,256]{1,0:T(8,128)(2,1)S(1)}, u32[]{:S(2)}, u32[]{:S(2)}) collective-permute-start(bf16[80,256]{1,0:T(8,128)(2,1)S(1)} %get-tuple-element.38.far), channel_id=1, source_target_pairs={{0,1},{1,0},{2,3},{3,2},{4,8},{5,9},{6,10},{7,11},{8,4},{9,5},{10,... | collective-permute-start | bytes 122888 | tf_op jit(solution)/shard_map/ppermute | solution.py:445
  24.6 0.6 %shard_map.52 = (f32[32,256]{1,0:T(8,128)S(1)}, f32[32,256]{1,0:T(8,128)S(1)}, bf16[288,64]{1,0:T(8,128)(2,1)S(1)}, bf16[288,64]{1,0:T(8,128)(2,1)S(1)}) custom-call(bf16[64,256]{1,0:T(8,128)(2,1)S(1)} %get-tuple-element.39.mate, bf16[80,256]{1,0:T(8,128)(2,1)S(1)} %get-tuple-element.38.far, f32[288,192]{1,0:T(8,128)S(1)} %get-tuple-element.40.w3), custom_call_target="tpu_custom_call" | custom-call | flops 37748736 | bytes 294912 | tf_op jit(solution)/shard_map/pallas_call | solution.py:32
  25.2 0.6 %collective-permute-done.8.got_mate = bf16[64,256]{1,0:T(8,128)(2,1)S(1)} collective-permute-done((bf16[64,256]{1,0:T(8,128)(2,1)S(1)}, bf16[64,256]{1,0:T(8,128)(2,1)S(1)}, u32[]{:S(2)}, u32[]{:S(2)}) %collective-permute-start.8) | collective-permute-done | bytes 32800 | tf_op jit(solution)/shard_map/ppermute | solution.py:446
  25.8 0.3 %shard_map.53 = (bf16[32,2,256]{2,1,0:T(2,128)(2,1)}, f32[32,256]{1,0:T(8,128)S(1)}) custom-call(f32[32,256]{1,0:T(8,128)S(1)} %get-tuple-element.42.beside_mate, f32[32,256]{1,0:T(8,128)S(1)} %get-tuple-element.43.beside_far, bf16[288,64]{1,0:T(8,128)(2,1)S(1)} %get-tuple-element.44.w_mate, bf16[64,256]{1,0:T(8,128)(2,1)S(1)} %collective-permute-done.8.got_mate), custom_call_target="tpu_custom_call" | custom-call | tf_op jit(solution)/shard_map/pallas_call | solution.py:32
  26.1 0.4 %collective-permute-done.7.got_far = bf16[80,256]{1,0:T(8,128)(2,1)S(1)} collective-permute-done((bf16[80,256]{1,0:T(8,128)(2,1)S(1)}, bf16[80,256]{1,0:T(8,128)(2,1)S(1)}, u32[]{:S(2)}, u32[]{:S(2)}) %collective-permute-start.7) | collective-permute-done | bytes 40992 | tf_op jit(solution)/shard_map/ppermute | solution.py:445
  26.5 1.0 %shard_map.54 = bf16[32,2,256]{2,1,0:T(2,128)(2,1)} custom-call(bf16[80,256]{1,0:T(8,128)(2,1)S(1)} %collective-permute-done.7.got_far, bf16[288,64]{1,0:T(8,128)(2,1)S(1)} %get-tuple-element.41.w_far, f32[32,256]{1,0:T(8,128)S(1)} %get-tuple-element.45.ready, f32[32,256]{1,0:T(8,128)S(1)} %get-tuple-element.43.beside_far, ...), custom_call_target="tpu_custom_call", output_to_operand_aliasing={{}: (4, {})} | custom-call | flops 9437184 | bytes 176128 | tf_op jit(solution)/shard_map/pallas_call | solution.py:32
  (5 shorter events, 0.0 us)
Async XLA Ops:
  0.0 0.9 %copy-start = (bf16[8,16,8,128]{3,2,1,0:T(8,128)(2,1)S(1)}, bf16[8,16,8,128]{3,2,1,0:T(8,128)(2,1)}, u32[]{:S(2)}) copy-start(bf16[8,16,8,128]{3,2,1,0:T(8,128)(2,1)} %vol.1) | copy-start | bytes 786436
  1.2 5.4 %collective-permute-start = (bf16[3,128,128]{2,1,0:T(8,128)(2,1)S(1)}, bf16[3,128,128]{2,1,0:T(8,128)(2,1)S(1)}, u32[]{:S(2)}, u32[]{:S(2)}) collective-permute-start(bf16[3,128,128]{2,1,0:T(8,128)(2,1)S(1)} %get-tuple-element.27), channel_id=1, source_target_pairs={{0,1},{1,0},{2,3},{3,2},{4,8},{5,9},{6,10},{7,11},{8,4},{9,5},{10,... | collective-permute-start | bytes 294920 | tf_op jit(solution)/shard_map/ppermute | solution.py:371
  3.9 2.7 %collective-permute-start.1 = (bf16[3,128,128]{2,1,0:T(8,128)(2,1)S(1)}, bf16[3,128,128]{2,1,0:T(8,128)(2,1)S(1)}, u32[]{:S(2)}, u32[]{:S(2)}) collective-permute-start(bf16[3,128,128]{2,1,0:T(8,128)(2,1)S(1)} %get-tuple-element.28), channel_id=1, source_target_pairs={{0,4},{1,5},{2,6},{3,7},{4,0},{5,1},{6,2},{7,3},{8,12},{9,13},{10,... | collective-permute-start | bytes 294920 | tf_op jit(solution)/shard_map/ppermute | solution.py:370
  6.6 5.6 %collective-permute-start.2 = (bf16[14,48,128]{2,1,0:T(8,128)(2,1)S(1)}, bf16[14,48,128]{2,1,0:T(8,128)(2,1)S(1)}, u32[]{:S(2)}, u32[]{:S(2)}) collective-permute-start(bf16[14,48,128]{2,1,0:T(8,128)(2,1)S(1)} %get-tuple-element.30), channel_id=1, source_target_pairs={{0,1},{1,0},{2,3},{3,2},{4,5},{5,4},{6,7},{7,6},{8,9},{9,8},{10,11... | collective-permute-start | bytes 516104 | tf_op jit(solution)/shard_map/ppermute | solution.py:402
  8.1 4.2 %collective-permute-start.3 = (bf16[14,48,128]{2,1,0:T(8,128)(2,1)S(1)}, bf16[14,48,128]{2,1,0:T(8,128)(2,1)S(1)}, u32[]{:S(2)}, u32[]{:S(2)}) collective-permute-start(bf16[14,48,128]{2,1,0:T(8,128)(2,1)S(1)} %get-tuple-element.31), channel_id=1, source_target_pairs={{0,4},{1,2},{2,1},{3,7},{4,0},{5,6},{6,5},{7,3},{8,12},{9,10},{10,... | collective-permute-start | bytes 516104 | tf_op jit(solution)/shard_map/ppermute | solution.py:401
  13.6 4.6 %collective-permute-start.4 = (bf16[64,128]{1,0:T(8,128)(2,1)S(1)}, bf16[64,128]{1,0:T(8,128)(2,1)S(1)}, u32[]{:S(2)}, u32[]{:S(2)}) collective-permute-start(bf16[64,128]{1,0:T(8,128)(2,1)S(1)} %shard_map.50.refs_0_), channel_id=1, source_target_pairs={{0,3},{1,2},{2,1},{3,0},{4,7},{5,6},{6,5},{7,4},{8,11},{9,10},{10,... | collective-permute-start | bytes 49160 | tf_op jit(solution)/shard_map/ppermute | solution.py:441
  16.6 3.8 %collective-permute-start.5 = (bf16[64,128]{1,0:T(8,128)(2,1)S(1)}, bf16[64,128]{1,0:T(8,128)(2,1)S(1)}, u32[]{:S(2)}, u32[]{:S(2)}) collective-permute-start(bf16[64,128]{1,0:T(8,128)(2,1)S(1)} %shard_map.50.refs_0_), channel_id=1, source_target_pairs={{0,2},{1,3},{2,0},{3,1},{4,6},{5,7},{6,4},{7,5},{8,10},{9,11},{10,... | collective-permute-start | bytes 49160 | tf_op jit(solution)/shard_map/ppermute | solution.py:441
  16.9 3.5 %collective-permute-start.6 = (bf16[64,128]{1,0:T(8,128)(2,1)S(1)}, bf16[64,128]{1,0:T(8,128)(2,1)S(1)}, u32[]{:S(2)}, u32[]{:S(2)}) collective-permute-start(bf16[64,128]{1,0:T(8,128)(2,1)S(1)} %shard_map.50.refs_0_), channel_id=1, source_target_pairs={{0,1},{1,0},{2,3},{3,2},{4,5},{5,4},{6,7},{7,6},{8,9},{9,8},{10,11... | collective-permute-start | bytes 49160 | tf_op jit(solution)/shard_map/ppermute | solution.py:441
  20.5 6.0 %collective-permute-start.7 = (bf16[80,256]{1,0:T(8,128)(2,1)S(1)}, bf16[80,256]{1,0:T(8,128)(2,1)S(1)}, u32[]{:S(2)}, u32[]{:S(2)}) collective-permute-start(bf16[80,256]{1,0:T(8,128)(2,1)S(1)} %get-tuple-element.38.far), channel_id=1, source_target_pairs={{0,1},{1,0},{2,3},{3,2},{4,8},{5,9},{6,10},{7,11},{8,4},{9,5},{10,... | collective-permute-start | bytes 122888 | tf_op jit(solution)/shard_map/ppermute | solution.py:445
  24.6 1.2 %collective-permute-start.8 = (bf16[64,256]{1,0:T(8,128)(2,1)S(1)}, bf16[64,256]{1,0:T(8,128)(2,1)S(1)}, u32[]{:S(2)}, u32[]{:S(2)}) collective-permute-start(bf16[64,256]{1,0:T(8,128)(2,1)S(1)} %get-tuple-element.39.mate), channel_id=1, source_target_pairs={{0,4},{1,5},{2,6},{3,7},{4,0},{5,1},{6,2},{7,3},{8,12},{9,13},{10,... | collective-permute-start | bytes 98312 | tf_op jit(solution)/shard_map/ppermute | solution.py:446

commit v8 on v7

--- a/solution.py
+++ b/solution.py
@@ -41,21 +41,23 @@
     )(*args)
 
 
-def turn_kernel(vol, turned, send_mate, send_far):
-    planes, chans, height, breadth = vol.shape
-    rows = chans * height
-    dest = iota((rows, rows), 0)
-    source = (dest & (chans - 1)) * height + dest // chans
-    swap = (iota((rows, rows), 1) == source).astype(F32).astype(BF)
-    for x in range(planes):
-        turned[x] = mat(swap, vol[x].reshape(rows, breadth)).astype(BF)
+def planes_kernel(volume, send_mate, send_far, sems):
+    planes = volume.shape[0]
     even = is_even("gx")
-    for out, first in (
-        (send_mate, jnp.where(even, planes - HALO, 0)),
-        (send_far, jnp.where(even, 0, planes - HALO)),
+    copies = []
+    for i, (out, first) in enumerate(
+        ((send_far, jnp.where(even, 0, planes - HALO)), (send_mate, jnp.where(even, planes - HALO, 0)))
     ):
-        for x in range(HALO):
-            out[x] = turned[first + x]
+        copies.append(pltpu.make_async_copy(volume.at[pl.ds(first, HALO)], out, sems.at[i]))
+    for copy in copies:
+        copy.start()
+    for copy in copies:
+        copy.wait()
+
+
+def turn(swap, plane):
+    rows, breadth = swap.shape[0], plane.shape[-1]
+    return mat(swap, plane.reshape(rows, breadth)).astype(BF)
 
 
 def yz_pairs(gx, yz, second):
@@ -102,7 +104,10 @@
     return [low for low, _ in sides] + [turned[x] for x in range(turned.shape[0])] + [high for _, high in sides]
 
 
-def edge_kernel(turned, got_far, got_mate, _, send_a, send_b):
+def edge_kernel(raw_far, raw_mate, turned, swap, _, send_a, send_b, got_far, got_mate):
+    for x in range(HALO):
+        got_far[x] = turn(swap[...], raw_far[x])
+        got_mate[x] = turn(swap[...], raw_mate[x])
     edge = send_a.shape[1]
     even = is_even("yz")
     for x, t in enumerate(all_planes(turned, got_mate, got_far)):
@@ -111,8 +116,9 @@
         send_b[x] = jnp.where(even, low, high)
 
 
-def weights_kernel(w1_hbm, w2_hbm, lower1, upper1, middle2, outer2, p_sel, w1, w2, sems):
-    loads = [pltpu.make_async_copy(a, b, sems.at[i]) for i, (a, b) in enumerate(((w1_hbm, w1), (w2_hbm, w2)))]
+def weights_kernel(volume, w1_hbm, w2_hbm, lower1, upper1, middle2, outer2, p_sel, swap, turned, vol, w1, w2, sems):
+    pairs = ((w1_hbm, w1), (w2_hbm, w2), (volume, vol))
+    loads = [pltpu.make_async_copy(a, b, sems.at[i]) for i, (a, b) in enumerate(pairs)]
     for load in loads:
         load.start()
 
@@ -123,8 +129,15 @@
     hit = hit & ((r & (z - 1)) == 4 * (c & (z // 4 - 1)))
     p_sel[...] = jnp.where(hit, 1.0, 0.0).astype(BF)
 
+    planes, chans, height, breadth = vol.shape
+    dest = iota(swap.shape, 0)
+    source = (dest & (chans - 1)) * height + dest // chans
+    swap[...] = (iota(swap.shape, 1) == source).astype(F32).astype(BF)
+
     for load in loads:
         load.wait()
+    for x in range(planes):
+        turned[x] = turn(swap[...], vol[x])
     for w, bands in (
         (w1, ((lower1, lambda y: (0, 1, 2)), (upper1, lambda y: (3, 4, 5)))),
         (w2, ((middle2, lambda y: (2, 3)), (outer2, lambda y: (0, 1) if y < 2 else (4, 5)))),
@@ -266,7 +279,7 @@
     even = is_even("yz")
     half = tiles[0].shape[1] // 2
     lane = iota((1, 2 * half), 1)
-    tiles = [tiles[i] for i in [0, 3, 2, 1]]
+    tiles = [tiles[i] for i in [0, 1, 2, 3]]
     low, high = [], []
     for m in range(len(tiles) // 2):
         a, b = tiles[2 * m][rows].astype(F32), tiles[2 * m + 1][rows].astype(F32)
@@ -361,16 +374,19 @@
     edge = EDGE * chans
     c2, c3 = weight_one.shape[0], weight_two.shape[0]
 
-    turned, send_mate, send_far = call(
-        turn_kernel,
-        [((planes, rows, breadth), BF), ((HALO, rows, breadth), BF), ((HALO, rows, breadth), BF)],
+    planes_shape = ((HALO, chans, height, breadth), BF)
+    send_mate, send_far = call(
+        planes_kernel,
+        [planes_shape, planes_shape],
         volume,
+        scratch=[pltpu.SemaphoreType.DMA((2,))],
+        hbm=(0,),
     )
     near, away = gx_pairs(gx, yz, False), gx_pairs(gx, yz, True)
-    got_mate = lax.ppermute(send_mate, ("gx", "yz"), near)
-    got_far = lax.ppermute(send_far, ("gx", "yz"), away)
+    raw_mate = lax.ppermute(send_mate, ("gx", "yz"), near)
+    raw_far = lax.ppermute(send_far, ("gx", "yz"), away)
     k1, k2 = 27 * chans, 27 * c2
-    lower1, upper1, middle2, outer2, p_sel = call(
+    lower1, upper1, middle2, outer2, p_sel, swap, turned = call(
         weights_kernel,
         [
             ((4 * c2, k1), BF),
@@ -378,24 +394,30 @@
             ((4 * c3, 2 * k2 // 3), BF),
             ((4 * c3, 2 * k2 // 3), BF),
             ((4 * breadth, breadth), BF),
+            ((rows, rows), BF),
+            ((planes, rows, breadth), BF),
         ],
+        volume,
         weight_one,
         weight_two,
         scratch=[
+            pltpu.VMEM(volume.shape, BF),
             pltpu.VMEM(weight_one.shape, BF),
             pltpu.VMEM(weight_two.shape, BF),
-            pltpu.SemaphoreType.DMA((2,)),
+            pltpu.SemaphoreType.DMA((3,)),
         ],
-        hbm=(0, 1),
+        hbm=(0, 1, 2),
         flops=2 * 64 * 864 * 1728,
     )
     wide = planes + 2 * HALO
-    send_a, send_b = call(
+    halo = ((HALO, rows, breadth), BF)
+    send_a, send_b, got_far, got_mate = call(
         edge_kernel,
-        [((wide, edge, breadth), BF), ((wide, edge, breadth), BF)],
+        [((wide, edge, breadth), BF), ((wide, edge, breadth), BF), halo, halo],
+        raw_far,
+        raw_mate,
         turned,
-        got_far,
-        got_mate,
+        swap,
         p_sel,
     )
     got_b = lax.ppermute(send_b, ("gx", "yz"), yz_pairs(gx, yz, True))
@@ -441,7 +463,7 @@
     tiles = [tile] + [lax.ppermute(tile, "yz", [(i, i ^ d) for i in range(yz)]) for d in range(1, yz)]
     cells = yz * (height // 4) * (breadth // 4)
     z = breadth // 4
-    mate, far = call(lay_kernel, [((c3, cells), BF), ((c3 + 16, cells), BF)], tiles[0], *[tiles[d] for d in [3, 2, 1]])
+    mate, far = call(lay_kernel, [((c3, cells), BF), ((c3 + 16, cells), BF)], tiles[0], *[tiles[d] for d in [1, 2, 3]])
     got_far = lax.ppermute(far, ("gx", "yz"), away)
     got_mate = lax.ppermute(mate, ("gx", "yz"), near)
     shape = (out_rows, 2, cells)

time: 27.7 us -> 27.6 us (level)
  Pallas kernels: 6.83 us -> 7.84 us
  local copies, waits for them, and re-layouts: 0.95 us -> 0 us
    pallas_call x9, Pallas kernels: 6.83 us -> 7.84 us  [call(): pl.pallas_call(body, out_shape=[jax.ShapeDtypeStruct(s, d) for s, d in ou...]
    unnamed x2 -> x0, local copies, waits for them, and re-layouts: 0.95 us -> none
  transfers between devices with their start and end apart: 9 -> 9, of which waited for: 6 -> 6; matrix products, arithmetic and copies ran while one was open for 0% -> 0% of each run, Pallas kernels for 15% -> 16%
where the time goes in v8:
time: 27.6 us; the launch traced here: 27.4 us
  starting transfers between devices  13.3 us (48%)
  Pallas kernels  7.84 us (28%)
  waiting for transfers between devices  6.2 us (22%)
    pallas_call x9, Pallas kernels, call(): pl.pallas_call(body, out_shape=[jax.ShapeDtypeStruct(s, d) for s, d in ou...  7.84 us
    ppermute x1, starting transfers between devices, per_device(): got_far = lax.ppermute(far, ('gx', 'yz'), away)  4.05 us
    ppermute x3, starting transfers between devices, per_device(): lax.ppermute(tile, 'yz', [(i, i ^ d) for i in range(yz)])  3.61 us
    ppermute x3, waiting for transfers between devices, per_device(): lax.ppermute(tile, 'yz', [(i, i ^ d) for i in range(yz)])  3.23 us
    ppermute x1, starting transfers between devices, per_device(): raw_far = lax.ppermute(send_far, ('gx', 'yz'), away)  2.67 us
    ppermute x1, starting transfers between devices, per_device(): got_a = lax.ppermute(send_a, ('gx', 'yz'), yz_pairs(gx, yz, False))  1.44 us
    ppermute x1, starting transfers between devices, per_device(): got_b = lax.ppermute(send_b, ('gx', 'yz'), yz_pairs(gx, yz, True))  1.04 us
    ppermute x1, waiting for transfers between devices, per_device(): got_a = lax.ppermute(send_a, ('gx', 'yz'), yz_pairs(gx, yz, False))  0.98 us
  transfers between devices with their start and end apart: 9, of which 6 were waited for; matrix products, arithmetic and copies ran while one was open for 0% of the time, Pallas kernels for 16%

profile of v8, /device:TPU:1, one launch (start us, length us, event | category | flops | bytes accessed | tf_op | source)
XLA Modules:
  0.0 27.4 jit_solution(7365349737290840165)
XLA Ops:
  0.0 1.0 %shard_map.46 = (bf16[3,16,8,128]{3,2,1,0:T(8,128)(2,1)S(1)}, bf16[3,16,8,128]{3,2,1,0:T(8,128)(2,1)S(1)}) custom-call(bf16[8,16,8,128]{3,2,1,0:T(8,128)(2,1)} %volume.3), custom_call_target="tpu_custom_call" | custom-call | bytes 262144 | tf_op jit(solution)/shard_map/pallas_call | solution.py:32
  1.0 2.7 %collective-permute-start = (bf16[3,16,8,128]{3,2,1,0:T(8,128)(2,1)S(1)}, bf16[3,16,8,128]{3,2,1,0:T(8,128)(2,1)S(1)}, u32[]{:S(2)}, u32[]{:S(2)}) collective-permute-start(bf16[3,16,8,128]{3,2,1,0:T(8,128)(2,1)S(1)} %get-tuple-element.29), channel_id=1, source_target_pairs={{0,1},{1,0},{2,3},{3,2},{4,8},{5,9},{6,10},{7,11},{8,4},{9,5},{10,... | collective-permute-start | bytes 294920 | tf_op jit(solution)/shard_map/ppermute | solution.py:387
  3.6 0.5 %collective-permute-start.1 = (bf16[3,16,8,128]{3,2,1,0:T(8,128)(2,1)S(1)}, bf16[3,16,8,128]{3,2,1,0:T(8,128)(2,1)S(1)}, u32[]{:S(2)}, u32[]{:S(2)}) collective-permute-start(bf16[3,16,8,128]{3,2,1,0:T(8,128)(2,1)S(1)} %get-tuple-element.30), channel_id=1, source_target_pairs={{0,4},{1,5},{2,6},{3,7},{4,0},{5,1},{6,2},{7,3},{8,12},{9,13},{10,... | collective-permute-start | bytes 294920 | tf_op jit(solution)/shard_map/ppermute | solution.py:386
  4.1 1.3 %shard_map.47 = (bf16[128,432]{1,0:T(8,128)(2,1)S(1)}, bf16[128,432]{1,0:T(8,128)(2,1)S(1)}, bf16[256,576]{1,0:T(8,128)(2,1)S(1)}, bf16[256,576]{1,0:T(8,128)(2,...) custom-call(bf16[8,16,8,128]{3,2,1,0:T(8,128)(2,1)} %volume.3, ...), custom_call_target="tpu_custom_call" | custom-call | flops 191102976 | bytes 400384 | tf_op jit(solution)/shard_map/pallas_call | solution.py:32
  5.4 0.9 %collective-permute-done.raw_far = bf16[3,16,8,128]{3,2,1,0:T(8,128)(2,1)S(1)} collective-permute-done((bf16[3,16,8,128]{3,2,1,0:T(8,128)(2,1)S(1)}, bf16[3,16,8,128]{3,2,1,0:T(8,128)(2,1)S(1)}, u32[]{:S(2)}, u32[]{:S(2)}) %collective-permute-start) | collective-permute-done | bytes 98336 | tf_op jit(solution)/shard_map/ppermute | solution.py:387
  6.3 0.0 collective-permute-done.1.raw_mate
  6.3 0.2 shard_map.48
  6.5 1.4 %collective-permute-start.2 = (bf16[14,48,128]{2,1,0:T(8,128)(2,1)S(1)}, bf16[14,48,128]{2,1,0:T(8,128)(2,1)S(1)}, u32[]{:S(2)}, u32[]{:S(2)}) collective-permute-start(bf16[14,48,128]{2,1,0:T(8,128)(2,1)S(1)} %get-tuple-element.34), channel_id=1, source_target_pairs={{0,1},{1,0},{2,3},{3,2},{4,5},{5,4},{6,7},{7,6},{8,9},{9,8},{10,11... | collective-permute-start | bytes 516104 | tf_op jit(solution)/shard_map/ppermute | solution.py:424
  8.0 1.0 %collective-permute-start.3 = (bf16[14,48,128]{2,1,0:T(8,128)(2,1)S(1)}, bf16[14,48,128]{2,1,0:T(8,128)(2,1)S(1)}, u32[]{:S(2)}, u32[]{:S(2)}) collective-permute-start(bf16[14,48,128]{2,1,0:T(8,128)(2,1)S(1)} %get-tuple-element.35), channel_id=1, source_target_pairs={{0,4},{1,2},{2,1},{3,7},{4,0},{5,6},{6,5},{7,3},{8,12},{9,10},{10,... | collective-permute-start | bytes 516104 | tf_op jit(solution)/shard_map/ppermute | solution.py:423
  9.0 2.2 %shard_map.49 = (f32[2,6,128,256]{3,2,1,0:T(8,128)S(1)}, f32[256,512]{1,0:T(8,128)S(1)}, f32[288,192]{1,0:T(8,128)S(1)}) custom-call(bf16[8,128,128]{2,1,0:T(8,128)(2,1)S(1)} %get-tuple-element.31.turned, bf16[3,128,128]{2,1,0:T(8,128)(2,1)S(1)} %get-tuple-element.36.got_mate, bf16[3,128,128]{2,1,0:T(8,128)(2,1)S(1)} %get-tuple-element.37.got_far, ...), custom_call_target="tpu_custom_call" | custom-call | flops 600000000 | bytes 1417216 | tf_op jit(solution)/shard_map/pallas_call | solution.py:32
  11.2 1.0 %collective-permute-done.2.got_a = bf16[14,48,128]{2,1,0:T(8,128)(2,1)S(1)} collective-permute-done((bf16[14,48,128]{2,1,0:T(8,128)(2,1)S(1)}, bf16[14,48,128]{2,1,0:T(8,128)(2,1)S(1)}, u32[]{:S(2)}, u32[]{:S(2)}) %collective-permute-start.2) | collective-permute-done | bytes 172064 | tf_op jit(solution)/shard_map/ppermute | solution.py:424
  12.2 1.3 %shard_map.50.refs_0_ = bf16[64,128]{1,0:T(8,128)(2,1)S(1)} custom-call(bf16[14,48,128]{2,1,0:T(8,128)(2,1)S(1)} %collective-permute-done.2.got_a, bf16[14,48,128]{2,1,0:T(8,128)(2,1)S(1)} %collective-permute-done.3.got_b, f32[2,6,128,256]{3,2,1,0:T(8,128)S(1)} %get-tuple-element.41.partial1, f32[256,512]{1,0:T(8,128)S(1)} %get-tuple-element.42.partial2, ...), custom_call_target="tpu_custom_call" | custom-call | flops 800000000 | bytes 3088384 | tf_op jit(solution)/shard_map/pallas_call | solution.py:32
  13.5 3.0 %collective-permute-start.6 = (bf16[64,128]{1,0:T(8,128)(2,1)S(1)}, bf16[64,128]{1,0:T(8,128)(2,1)S(1)}, u32[]{:S(2)}, u32[]{:S(2)}) collective-permute-start(bf16[64,128]{1,0:T(8,128)(2,1)S(1)} %shard_map.50.refs_0_), channel_id=1, source_target_pairs={{0,3},{1,2},{2,1},{3,0},{4,7},{5,6},{6,5},{7,4},{8,11},{9,10},{10,... | collective-permute-start | bytes 49160 | tf_op jit(solution)/shard_map/ppermute | solution.py:463
  16.5 0.3 %collective-permute-start.5 = (bf16[64,128]{1,0:T(8,128)(2,1)S(1)}, bf16[64,128]{1,0:T(8,128)(2,1)S(1)}, u32[]{:S(2)}, u32[]{:S(2)}) collective-permute-start(bf16[64,128]{1,0:T(8,128)(2,1)S(1)} %shard_map.50.refs_0_), channel_id=1, source_target_pairs={{0,2},{1,3},{2,0},{3,1},{4,6},{5,7},{6,4},{7,5},{8,10},{9,11},{10,... | collective-permute-start | bytes 49160 | tf_op jit(solution)/shard_map/ppermute | solution.py:463
  16.8 0.3 %collective-permute-start.4 = (bf16[64,128]{1,0:T(8,128)(2,1)S(1)}, bf16[64,128]{1,0:T(8,128)(2,1)S(1)}, u32[]{:S(2)}, u32[]{:S(2)}) collective-permute-start(bf16[64,128]{1,0:T(8,128)(2,1)S(1)} %shard_map.50.refs_0_), channel_id=1, source_target_pairs={{0,1},{1,0},{2,3},{3,2},{4,5},{5,4},{6,7},{7,6},{8,9},{9,8},{10,11... | collective-permute-start | bytes 49160 | tf_op jit(solution)/shard_map/ppermute | solution.py:463
  17.1 0.9 %collective-permute-done.6.refs_3_ = bf16[64,128]{1,0:T(8,128)(2,1)S(1)} collective-permute-done((bf16[64,128]{1,0:T(8,128)(2,1)S(1)}, bf16[64,128]{1,0:T(8,128)(2,1)S(1)}, u32[]{:S(2)}, u32[]{:S(2)}) %collective-permute-start.6) | collective-permute-done | bytes 16416 | tf_op jit(solution)/shard_map/ppermute | solution.py:463
  18.0 2.3 %collective-permute-done.5.refs_2_ = bf16[64,128]{1,0:T(8,128)(2,1)S(1)} collective-permute-done((bf16[64,128]{1,0:T(8,128)(2,1)S(1)}, bf16[64,128]{1,0:T(8,128)(2,1)S(1)}, u32[]{:S(2)}, u32[]{:S(2)}) %collective-permute-start.5) | collective-permute-done | bytes 16416 | tf_op jit(solution)/shard_map/ppermute | solution.py:463
  20.3 0.1 shard_map.51
  20.4 4.0 %collective-permute-start.7 = (bf16[80,256]{1,0:T(8,128)(2,1)S(1)}, bf16[80,256]{1,0:T(8,128)(2,1)S(1)}, u32[]{:S(2)}, u32[]{:S(2)}) collective-permute-start(bf16[80,256]{1,0:T(8,128)(2,1)S(1)} %get-tuple-element.44.far), channel_id=1, source_target_pairs={{0,1},{1,0},{2,3},{3,2},{4,8},{5,9},{6,10},{7,11},{8,4},{9,5},{10,... | collective-permute-start | bytes 122888 | tf_op jit(solution)/shard_map/ppermute | solution.py:467
  24.5 0.6 %shard_map.52 = (f32[32,256]{1,0:T(8,128)S(1)}, f32[32,256]{1,0:T(8,128)S(1)}, bf16[288,64]{1,0:T(8,128)(2,1)S(1)}, bf16[288,64]{1,0:T(8,128)(2,1)S(1)}) custom-call(bf16[64,256]{1,0:T(8,128)(2,1)S(1)} %get-tuple-element.45.mate, bf16[80,256]{1,0:T(8,128)(2,1)S(1)} %get-tuple-element.44.far, f32[288,192]{1,0:T(8,128)S(1)} %get-tuple-element.46.w3), custom_call_target="tpu_custom_call" | custom-call | flops 37748736 | bytes 294912 | tf_op jit(solution)/shard_map/pallas_call | solution.py:32
  25.0 0.6 %collective-permute-done.8.got_mate = bf16[64,256]{1,0:T(8,128)(2,1)S(1)} collective-permute-done((bf16[64,256]{1,0:T(8,128)(2,1)S(1)}, bf16[64,256]{1,0:T(8,128)(2,1)S(1)}, u32[]{:S(2)}, u32[]{:S(2)}) %collective-permute-start.8) | collective-permute-done | bytes 32800 | tf_op jit(solution)/shard_map/ppermute | solution.py:468
  25.7 0.3 %shard_map.53 = (bf16[32,2,256]{2,1,0:T(2,128)(2,1)}, f32[32,256]{1,0:T(8,128)S(1)}) custom-call(f32[32,256]{1,0:T(8,128)S(1)} %get-tuple-element.48.beside_mate, f32[32,256]{1,0:T(8,128)S(1)} %get-tuple-element.49.beside_far, bf16[288,64]{1,0:T(8,128)(2,1)S(1)} %get-tuple-element.50.w_mate, bf16[64,256]{1,0:T(8,128)(2,1)S(1)} %collective-permute-done.8.got_mate), custom_call_target="tpu_custom_call" | custom-call | tf_op jit(solution)/shard_map/pallas_call | solution.py:32
  26.0 0.4 %collective-permute-done.7.got_far = bf16[80,256]{1,0:T(8,128)(2,1)S(1)} collective-permute-done((bf16[80,256]{1,0:T(8,128)(2,1)S(1)}, bf16[80,256]{1,0:T(8,128)(2,1)S(1)}, u32[]{:S(2)}, u32[]{:S(2)}) %collective-permute-start.7) | collective-permute-done | bytes 40992 | tf_op jit(solution)/shard_map/ppermute | solution.py:467
  26.4 1.0 %shard_map.54 = bf16[32,2,256]{2,1,0:T(2,128)(2,1)} custom-call(bf16[80,256]{1,0:T(8,128)(2,1)S(1)} %collective-permute-done.7.got_far, bf16[288,64]{1,0:T(8,128)(2,1)S(1)} %get-tuple-element.47.w_far, f32[32,256]{1,0:T(8,128)S(1)} %get-tuple-element.51.ready, f32[32,256]{1,0:T(8,128)S(1)} %get-tuple-element.49.beside_far, ...), custom_call_target="tpu_custom_call", output_to_operand_aliasing={{}: (4, {})} | custom-call | flops 9437184 | bytes 176128 | tf_op jit(solution)/shard_map/pallas_call | solution.py:32
  (3 shorter events, 0.0 us)
Async XLA Ops:
  1.0 5.3 %collective-permute-start = (bf16[3,16,8,128]{3,2,1,0:T(8,128)(2,1)S(1)}, bf16[3,16,8,128]{3,2,1,0:T(8,128)(2,1)S(1)}, u32[]{:S(2)}, u32[]{:S(2)}) collective-permute-start(bf16[3,16,8,128]{3,2,1,0:T(8,128)(2,1)S(1)} %get-tuple-element.29), channel_id=1, source_target_pairs={{0,1},{1,0},{2,3},{3,2},{4,8},{5,9},{6,10},{7,11},{8,4},{9,5},{10,... | collective-permute-start | bytes 294920 | tf_op jit(solution)/shard_map/ppermute | solution.py:387
  3.6 2.7 %collective-permute-start.1 = (bf16[3,16,8,128]{3,2,1,0:T(8,128)(2,1)S(1)}, bf16[3,16,8,128]{3,2,1,0:T(8,128)(2,1)S(1)}, u32[]{:S(2)}, u32[]{:S(2)}) collective-permute-start(bf16[3,16,8,128]{3,2,1,0:T(8,128)(2,1)S(1)} %get-tuple-element.30), channel_id=1, source_target_pairs={{0,4},{1,5},{2,6},{3,7},{4,0},{5,1},{6,2},{7,3},{8,12},{9,13},{10,... | collective-permute-start | bytes 294920 | tf_op jit(solution)/shard_map/ppermute | solution.py:386
  6.5 5.6 %collective-permute-start.2 = (bf16[14,48,128]{2,1,0:T(8,128)(2,1)S(1)}, bf16[14,48,128]{2,1,0:T(8,128)(2,1)S(1)}, u32[]{:S(2)}, u32[]{:S(2)}) collective-permute-start(bf16[14,48,128]{2,1,0:T(8,128)(2,1)S(1)} %get-tuple-element.34), channel_id=1, source_target_pairs={{0,1},{1,0},{2,3},{3,2},{4,5},{5,4},{6,7},{7,6},{8,9},{9,8},{10,11... | collective-permute-start | bytes 516104 | tf_op jit(solution)/shard_map/ppermute | solution.py:424
  8.0 4.2 %collective-permute-start.3 = (bf16[14,48,128]{2,1,0:T(8,128)(2,1)S(1)}, bf16[14,48,128]{2,1,0:T(8,128)(2,1)S(1)}, u32[]{:S(2)}, u32[]{:S(2)}) collective-permute-start(bf16[14,48,128]{2,1,0:T(8,128)(2,1)S(1)} %get-tuple-element.35), channel_id=1, source_target_pairs={{0,4},{1,2},{2,1},{3,7},{4,0},{5,6},{6,5},{7,3},{8,12},{9,10},{10,... | collective-permute-start | bytes 516104 | tf_op jit(solution)/shard_map/ppermute | solution.py:423
  13.5 4.6 %collective-permute-start.6 = (bf16[64,128]{1,0:T(8,128)(2,1)S(1)}, bf16[64,128]{1,0:T(8,128)(2,1)S(1)}, u32[]{:S(2)}, u32[]{:S(2)}) collective-permute-start(bf16[64,128]{1,0:T(8,128)(2,1)S(1)} %shard_map.50.refs_0_), channel_id=1, source_target_pairs={{0,3},{1,2},{2,1},{3,0},{4,7},{5,6},{6,5},{7,4},{8,11},{9,10},{10,... | collective-permute-start | bytes 49160 | tf_op jit(solution)/shard_map/ppermute | solution.py:463
  16.5 3.8 %collective-permute-start.5 = (bf16[64,128]{1,0:T(8,128)(2,1)S(1)}, bf16[64,128]{1,0:T(8,128)(2,1)S(1)}, u32[]{:S(2)}, u32[]{:S(2)}) collective-permute-start(bf16[64,128]{1,0:T(8,128)(2,1)S(1)} %shard_map.50.refs_0_), channel_id=1, source_target_pairs={{0,2},{1,3},{2,0},{3,1},{4,6},{5,7},{6,4},{7,5},{8,10},{9,11},{10,... | collective-permute-start | bytes 49160 | tf_op jit(solution)/shard_map/ppermute | solution.py:463
  16.8 3.5 %collective-permute-start.4 = (bf16[64,128]{1,0:T(8,128)(2,1)S(1)}, bf16[64,128]{1,0:T(8,128)(2,1)S(1)}, u32[]{:S(2)}, u32[]{:S(2)}) collective-permute-start(bf16[64,128]{1,0:T(8,128)(2,1)S(1)} %shard_map.50.refs_0_), channel_id=1, source_target_pairs={{0,1},{1,0},{2,3},{3,2},{4,5},{5,4},{6,7},{7,6},{8,9},{9,8},{10,11... | collective-permute-start | bytes 49160 | tf_op jit(solution)/shard_map/ppermute | solution.py:463
  20.4 6.0 %collective-permute-start.7 = (bf16[80,256]{1,0:T(8,128)(2,1)S(1)}, bf16[80,256]{1,0:T(8,128)(2,1)S(1)}, u32[]{:S(2)}, u32[]{:S(2)}) collective-permute-start(bf16[80,256]{1,0:T(8,128)(2,1)S(1)} %get-tuple-element.44.far), channel_id=1, source_target_pairs={{0,1},{1,0},{2,3},{3,2},{4,8},{5,9},{6,10},{7,11},{8,4},{9,5},{10,... | collective-permute-start | bytes 122888 | tf_op jit(solution)/shard_map/ppermute | solution.py:467
  24.4 1.2 %collective-permute-start.8 = (bf16[64,256]{1,0:T(8,128)(2,1)S(1)}, bf16[64,256]{1,0:T(8,128)(2,1)S(1)}, u32[]{:S(2)}, u32[]{:S(2)}) collective-permute-start(bf16[64,256]{1,0:T(8,128)(2,1)S(1)} %get-tuple-element.45.mate), channel_id=1, source_target_pairs={{0,4},{1,5},{2,6},{3,7},{4,0},{5,1},{6,2},{7,3},{8,12},{9,13},{10,... | collective-permute-start | bytes 98312 | tf_op jit(solution)/shard_map/ppermute | solution.py:468

commit v9 on v8

--- a/solution.py
+++ b/solution.py
@@ -220,12 +220,9 @@
     lower, upper = lower1[: 3 * width], upper1[width:]
     step = 3 * chans
     pooled = []
-    zero = jnp.zeros((width, partial1.shape[3]), F32)
     for j in range(pairs):
-        partial1[0, j, :width] = zero
-        partial1[0, j, width:] = mat(upper, two_cells(taps, j, 0, 3 * step))
-        partial1[1, j, : 3 * width] = mat(lower, two_cells(taps, j, 5 * step, 3 * step))
-        partial1[1, j, 3 * width :] = zero
+        partial1[0, j] = mat(upper, two_cells(taps, j, 0, 3 * step))
+        partial1[1, j] = mat(lower, two_cells(taps, j, 5 * step, 3 * step))
         a = mat(lower, two_cells(taps, j, step, 3 * step))
         b = mat(upper, two_cells(taps, j, 4 * step, 3 * step))
         acc = jnp.concatenate([a[:width], a[width:] + b[: 2 * width], b[2 * width :]], 0)
@@ -261,9 +258,13 @@
     highs = [mat(upper, two_cells(high_taps, j, 0, rows)) for j in range(pairs)]
     for j in range(pairs):
         p = partial1[0, j]
-        below.append(pool_first(jnp.concatenate([p[: 3 * width] + lows[j], p[3 * width :]], 0), j, pairs, first, False))
+        a = lows[j]
+        a = jnp.concatenate([a[:width], p[: 2 * width] + a[width:], p[2 * width :]], 0)
+        below.append(pool_first(a, j, pairs, first, False))
         p = partial1[1, j]
-        above.append(pool_first(jnp.concatenate([p[:width], p[width:] + highs[j]], 0), j, pairs, False, last))
+        b = highs[j]
+        b = jnp.concatenate([p[:width], p[width:] + b[: 2 * width], b[2 * width :]], 0)
+        above.append(pool_first(b, j, pairs, False, last))
     width = outer2.shape[0] // 4
     sums = [mat(outer2[2 * y * width : 2 * (y + 1) * width], second_taps(p)) for y, p in enumerate((below, above))]
     halves = []
@@ -427,7 +428,7 @@
     partial1, partial2, picked = call(
         inner_kernel,
         [
-            ((2, pairs, 4 * c2, 2 * breadth), F32),
+            ((2, pairs, 3 * c2, 2 * breadth), F32),
             ((4 * c3, 2 * PLANES * breadth), F32),
             ((9 * out_rows, 3 * c3), F32),
         ],

time: 27.6 us -> 27.6 us (level)
  no operation moved by 1% of the time
where the time goes in v9:
time: 27.6 us; the launch traced here: 27.4 us
  starting transfers between devices  13.3 us (48%)
  Pallas kernels  7.84 us (28%)
  waiting for transfers between devices  6.19 us (22%)
    pallas_call x9, Pallas kernels, call(): pl.pallas_call(body, out_shape=[jax.ShapeDtypeStruct(s, d) for s, d in ou...  7.84 us
    ppermute x1, starting transfers between devices, per_device(): got_far = lax.ppermute(far, ('gx', 'yz'), away)  4.05 us
    ppermute x3, starting transfers between devices, per_device(): lax.ppermute(tile, 'yz', [(i, i ^ d) for i in range(yz)])  3.61 us
    ppermute x3, waiting for transfers between devices, per_device(): lax.ppermute(tile, 'yz', [(i, i ^ d) for i in range(yz)])  3.23 us
    ppermute x1, starting transfers between devices, per_device(): raw_far = lax.ppermute(send_far, ('gx', 'yz'), away)  2.67 us
    ppermute x1, starting transfers between devices, per_device(): got_a = lax.ppermute(send_a, ('gx', 'yz'), yz_pairs(gx, yz, False))  1.44 us
    ppermute x1, starting transfers between devices, per_device(): got_b = lax.ppermute(send_b, ('gx', 'yz'), yz_pairs(gx, yz, True))  1.04 us
    ppermute x1, waiting for transfers between devices, per_device(): got_a = lax.ppermute(send_a, ('gx', 'yz'), yz_pairs(gx, yz, False))  0.98 us
  transfers between devices with their start and end apart: 9, of which 6 were waited for; matrix products, arithmetic and copies ran while one was open for 0% of the time, Pallas kernels for 16%

profile of v9, /device:TPU:1, one launch (start us, length us, event | category | flops | bytes accessed | tf_op | source)
XLA Modules:
  0.0 27.4 jit_solution(10151542716801145461)
XLA Ops:
  0.0 1.0 %shard_map.46 = (bf16[3,16,8,128]{3,2,1,0:T(8,128)(2,1)S(1)}, bf16[3,16,8,128]{3,2,1,0:T(8,128)(2,1)S(1)}) custom-call(bf16[8,16,8,128]{3,2,1,0:T(8,128)(2,1)} %volume.3), custom_call_target="tpu_custom_call" | custom-call | bytes 262144 | tf_op jit(solution)/shard_map/pallas_call | solution.py:32
  1.0 2.7 %collective-permute-start = (bf16[3,16,8,128]{3,2,1,0:T(8,128)(2,1)S(1)}, bf16[3,16,8,128]{3,2,1,0:T(8,128)(2,1)S(1)}, u32[]{:S(2)}, u32[]{:S(2)}) collective-permute-start(bf16[3,16,8,128]{3,2,1,0:T(8,128)(2,1)S(1)} %get-tuple-element.29), channel_id=1, source_target_pairs={{0,1},{1,0},{2,3},{3,2},{4,8},{5,9},{6,10},{7,11},{8,4},{9,5},{10,... | collective-permute-start | bytes 294920 | tf_op jit(solution)/shard_map/ppermute | solution.py:388
  3.6 0.5 %collective-permute-start.1 = (bf16[3,16,8,128]{3,2,1,0:T(8,128)(2,1)S(1)}, bf16[3,16,8,128]{3,2,1,0:T(8,128)(2,1)S(1)}, u32[]{:S(2)}, u32[]{:S(2)}) collective-permute-start(bf16[3,16,8,128]{3,2,1,0:T(8,128)(2,1)S(1)} %get-tuple-element.30), channel_id=1, source_target_pairs={{0,4},{1,5},{2,6},{3,7},{4,0},{5,1},{6,2},{7,3},{8,12},{9,13},{10,... | collective-permute-start | bytes 294920 | tf_op jit(solution)/shard_map/ppermute | solution.py:387
  4.1 1.3 %shard_map.47 = (bf16[128,432]{1,0:T(8,128)(2,1)S(1)}, bf16[128,432]{1,0:T(8,128)(2,1)S(1)}, bf16[256,576]{1,0:T(8,128)(2,1)S(1)}, bf16[256,576]{1,0:T(8,128)(2,...) custom-call(bf16[8,16,8,128]{3,2,1,0:T(8,128)(2,1)} %volume.3, ...), custom_call_target="tpu_custom_call" | custom-call | flops 191102976 | bytes 400384 | tf_op jit(solution)/shard_map/pallas_call | solution.py:32
  5.4 0.9 %collective-permute-done.raw_far = bf16[3,16,8,128]{3,2,1,0:T(8,128)(2,1)S(1)} collective-permute-done((bf16[3,16,8,128]{3,2,1,0:T(8,128)(2,1)S(1)}, bf16[3,16,8,128]{3,2,1,0:T(8,128)(2,1)S(1)}, u32[]{:S(2)}, u32[]{:S(2)}) %collective-permute-start) | collective-permute-done | bytes 98336 | tf_op jit(solution)/shard_map/ppermute | solution.py:388
  6.3 0.0 collective-permute-done.1.raw_mate
  6.3 0.2 shard_map.48
  6.5 1.4 %collective-permute-start.2 = (bf16[14,48,128]{2,1,0:T(8,128)(2,1)S(1)}, bf16[14,48,128]{2,1,0:T(8,128)(2,1)S(1)}, u32[]{:S(2)}, u32[]{:S(2)}) collective-permute-start(bf16[14,48,128]{2,1,0:T(8,128)(2,1)S(1)} %get-tuple-element.34), channel_id=1, source_target_pairs={{0,1},{1,0},{2,3},{3,2},{4,5},{5,4},{6,7},{7,6},{8,9},{9,8},{10,11... | collective-permute-start | bytes 516104 | tf_op jit(solution)/shard_map/ppermute | solution.py:425
  8.0 1.0 %collective-permute-start.3 = (bf16[14,48,128]{2,1,0:T(8,128)(2,1)S(1)}, bf16[14,48,128]{2,1,0:T(8,128)(2,1)S(1)}, u32[]{:S(2)}, u32[]{:S(2)}) collective-permute-start(bf16[14,48,128]{2,1,0:T(8,128)(2,1)S(1)} %get-tuple-element.35), channel_id=1, source_target_pairs={{0,4},{1,2},{2,1},{3,7},{4,0},{5,6},{6,5},{7,3},{8,12},{9,10},{10,... | collective-permute-start | bytes 516104 | tf_op jit(solution)/shard_map/ppermute | solution.py:424
  9.0 2.2 %shard_map.49 = (f32[2,6,96,256]{3,2,1,0:T(8,128)S(1)}, f32[256,512]{1,0:T(8,128)S(1)}, f32[288,192]{1,0:T(8,128)S(1)}) custom-call(bf16[8,128,128]{2,1,0:T(8,128)(2,1)S(1)} %get-tuple-element.31.turned, bf16[3,128,128]{2,1,0:T(8,128)(2,1)S(1)} %get-tuple-element.36.got_mate, bf16[3,128,128]{2,1,0:T(8,128)(2,1)S(1)} %get-tuple-element.37.got_far, ...), custom_call_target="tpu_custom_call" | custom-call | flops 600000000 | bytes 1417216 | tf_op jit(solution)/shard_map/pallas_call | solution.py:32
  11.2 1.0 %collective-permute-done.2.got_a = bf16[14,48,128]{2,1,0:T(8,128)(2,1)S(1)} collective-permute-done((bf16[14,48,128]{2,1,0:T(8,128)(2,1)S(1)}, bf16[14,48,128]{2,1,0:T(8,128)(2,1)S(1)}, u32[]{:S(2)}, u32[]{:S(2)}) %collective-permute-start.2) | collective-permute-done | bytes 172064 | tf_op jit(solution)/shard_map/ppermute | solution.py:425
  12.2 1.3 %shard_map.50.refs_0_ = bf16[64,128]{1,0:T(8,128)(2,1)S(1)} custom-call(bf16[14,48,128]{2,1,0:T(8,128)(2,1)S(1)} %collective-permute-done.2.got_a, bf16[14,48,128]{2,1,0:T(8,128)(2,1)S(1)} %collective-permute-done.3.got_b, f32[2,6,96,256]{3,2,1,0:T(8,128)S(1)} %get-tuple-element.41.partial1, f32[256,512]{1,0:T(8,128)S(1)} %get-tuple-element.42.partial2, ...), custom_call_target="tpu_custom_call" | custom-call | flops 800000000 | bytes 2695168 | tf_op jit(solution)/shard_map/pallas_call | solution.py:32
  13.4 3.0 %collective-permute-start.6 = (bf16[64,128]{1,0:T(8,128)(2,1)S(1)}, bf16[64,128]{1,0:T(8,128)(2,1)S(1)}, u32[]{:S(2)}, u32[]{:S(2)}) collective-permute-start(bf16[64,128]{1,0:T(8,128)(2,1)S(1)} %shard_map.50.refs_0_), channel_id=1, source_target_pairs={{0,3},{1,2},{2,1},{3,0},{4,7},{5,6},{6,5},{7,4},{8,11},{9,10},{10,... | collective-permute-start | bytes 49160 | tf_op jit(solution)/shard_map/ppermute | solution.py:464
  16.5 0.3 %collective-permute-start.5 = (bf16[64,128]{1,0:T(8,128)(2,1)S(1)}, bf16[64,128]{1,0:T(8,128)(2,1)S(1)}, u32[]{:S(2)}, u32[]{:S(2)}) collective-permute-start(bf16[64,128]{1,0:T(8,128)(2,1)S(1)} %shard_map.50.refs_0_), channel_id=1, source_target_pairs={{0,2},{1,3},{2,0},{3,1},{4,6},{5,7},{6,4},{7,5},{8,10},{9,11},{10,... | collective-permute-start | bytes 49160 | tf_op jit(solution)/shard_map/ppermute | solution.py:464
  16.8 0.3 %collective-permute-start.4 = (bf16[64,128]{1,0:T(8,128)(2,1)S(1)}, bf16[64,128]{1,0:T(8,128)(2,1)S(1)}, u32[]{:S(2)}, u32[]{:S(2)}) collective-permute-start(bf16[64,128]{1,0:T(8,128)(2,1)S(1)} %shard_map.50.refs_0_), channel_id=1, source_target_pairs={{0,1},{1,0},{2,3},{3,2},{4,5},{5,4},{6,7},{7,6},{8,9},{9,8},{10,11... | collective-permute-start | bytes 49160 | tf_op jit(solution)/shard_map/ppermute | solution.py:464
  17.1 0.9 %collective-permute-done.6.refs_3_ = bf16[64,128]{1,0:T(8,128)(2,1)S(1)} collective-permute-done((bf16[64,128]{1,0:T(8,128)(2,1)S(1)}, bf16[64,128]{1,0:T(8,128)(2,1)S(1)}, u32[]{:S(2)}, u32[]{:S(2)}) %collective-permute-start.6) | collective-permute-done | bytes 16416 | tf_op jit(solution)/shard_map/ppermute | solution.py:464
  18.0 2.3 %collective-permute-done.5.refs_2_ = bf16[64,128]{1,0:T(8,128)(2,1)S(1)} collective-permute-done((bf16[64,128]{1,0:T(8,128)(2,1)S(1)}, bf16[64,128]{1,0:T(8,128)(2,1)S(1)}, u32[]{:S(2)}, u32[]{:S(2)}) %collective-permute-start.5) | collective-permute-done | bytes 16416 | tf_op jit(solution)/shard_map/ppermute | solution.py:464
  20.3 0.1 shard_map.51
  20.4 4.1 %collective-permute-start.7 = (bf16[80,256]{1,0:T(8,128)(2,1)S(1)}, bf16[80,256]{1,0:T(8,128)(2,1)S(1)}, u32[]{:S(2)}, u32[]{:S(2)}) collective-permute-start(bf16[80,256]{1,0:T(8,128)(2,1)S(1)} %get-tuple-element.44.far), channel_id=1, source_target_pairs={{0,1},{1,0},{2,3},{3,2},{4,8},{5,9},{6,10},{7,11},{8,4},{9,5},{10,... | collective-permute-start | bytes 122888 | tf_op jit(solution)/shard_map/ppermute | solution.py:468
  24.5 0.6 %shard_map.52 = (f32[32,256]{1,0:T(8,128)S(1)}, f32[32,256]{1,0:T(8,128)S(1)}, bf16[288,64]{1,0:T(8,128)(2,1)S(1)}, bf16[288,64]{1,0:T(8,128)(2,1)S(1)}) custom-call(bf16[64,256]{1,0:T(8,128)(2,1)S(1)} %get-tuple-element.45.mate, bf16[80,256]{1,0:T(8,128)(2,1)S(1)} %get-tuple-element.44.far, f32[288,192]{1,0:T(8,128)S(1)} %get-tuple-element.46.w3), custom_call_target="tpu_custom_call" | custom-call | flops 37748736 | bytes 294912 | tf_op jit(solution)/shard_map/pallas_call | solution.py:32
  25.0 0.6 %collective-permute-done.8.got_mate = bf16[64,256]{1,0:T(8,128)(2,1)S(1)} collective-permute-done((bf16[64,256]{1,0:T(8,128)(2,1)S(1)}, bf16[64,256]{1,0:T(8,128)(2,1)S(1)}, u32[]{:S(2)}, u32[]{:S(2)}) %collective-permute-start.8) | collective-permute-done | bytes 32800 | tf_op jit(solution)/shard_map/ppermute | solution.py:469
  25.7 0.3 %shard_map.53 = (bf16[32,2,256]{2,1,0:T(2,128)(2,1)}, f32[32,256]{1,0:T(8,128)S(1)}) custom-call(f32[32,256]{1,0:T(8,128)S(1)} %get-tuple-element.48.beside_mate, f32[32,256]{1,0:T(8,128)S(1)} %get-tuple-element.49.beside_far, bf16[288,64]{1,0:T(8,128)(2,1)S(1)} %get-tuple-element.50.w_mate, bf16[64,256]{1,0:T(8,128)(2,1)S(1)} %collective-permute-done.8.got_mate), custom_call_target="tpu_custom_call" | custom-call | tf_op jit(solution)/shard_map/pallas_call | solution.py:32
  26.0 0.4 %collective-permute-done.7.got_far = bf16[80,256]{1,0:T(8,128)(2,1)S(1)} collective-permute-done((bf16[80,256]{1,0:T(8,128)(2,1)S(1)}, bf16[80,256]{1,0:T(8,128)(2,1)S(1)}, u32[]{:S(2)}, u32[]{:S(2)}) %collective-permute-start.7) | collective-permute-done | bytes 40992 | tf_op jit(solution)/shard_map/ppermute | solution.py:468
  26.4 1.0 %shard_map.54 = bf16[32,2,256]{2,1,0:T(2,128)(2,1)} custom-call(bf16[80,256]{1,0:T(8,128)(2,1)S(1)} %collective-permute-done.7.got_far, bf16[288,64]{1,0:T(8,128)(2,1)S(1)} %get-tuple-element.47.w_far, f32[32,256]{1,0:T(8,128)S(1)} %get-tuple-element.51.ready, f32[32,256]{1,0:T(8,128)S(1)} %get-tuple-element.49.beside_far, ...), custom_call_target="tpu_custom_call", output_to_operand_aliasing={{}: (4, {})} | custom-call | flops 9437184 | bytes 176128 | tf_op jit(solution)/shard_map/pallas_call | solution.py:32
  (3 shorter events, 0.0 us)
Async XLA Ops:
  1.0 5.3 %collective-permute-start = (bf16[3,16,8,128]{3,2,1,0:T(8,128)(2,1)S(1)}, bf16[3,16,8,128]{3,2,1,0:T(8,128)(2,1)S(1)}, u32[]{:S(2)}, u32[]{:S(2)}) collective-permute-start(bf16[3,16,8,128]{3,2,1,0:T(8,128)(2,1)S(1)} %get-tuple-element.29), channel_id=1, source_target_pairs={{0,1},{1,0},{2,3},{3,2},{4,8},{5,9},{6,10},{7,11},{8,4},{9,5},{10,... | collective-permute-start | bytes 294920 | tf_op jit(solution)/shard_map/ppermute | solution.py:388
  3.6 2.7 %collective-permute-start.1 = (bf16[3,16,8,128]{3,2,1,0:T(8,128)(2,1)S(1)}, bf16[3,16,8,128]{3,2,1,0:T(8,128)(2,1)S(1)}, u32[]{:S(2)}, u32[]{:S(2)}) collective-permute-start(bf16[3,16,8,128]{3,2,1,0:T(8,128)(2,1)S(1)} %get-tuple-element.30), channel_id=1, source_target_pairs={{0,4},{1,5},{2,6},{3,7},{4,0},{5,1},{6,2},{7,3},{8,12},{9,13},{10,... | collective-permute-start | bytes 294920 | tf_op jit(solution)/shard_map/ppermute | solution.py:387
  6.5 5.6 %collective-permute-start.2 = (bf16[14,48,128]{2,1,0:T(8,128)(2,1)S(1)}, bf16[14,48,128]{2,1,0:T(8,128)(2,1)S(1)}, u32[]{:S(2)}, u32[]{:S(2)}) collective-permute-start(bf16[14,48,128]{2,1,0:T(8,128)(2,1)S(1)} %get-tuple-element.34), channel_id=1, source_target_pairs={{0,1},{1,0},{2,3},{3,2},{4,5},{5,4},{6,7},{7,6},{8,9},{9,8},{10,11... | collective-permute-start | bytes 516104 | tf_op jit(solution)/shard_map/ppermute | solution.py:425
  8.0 4.2 %collective-permute-start.3 = (bf16[14,48,128]{2,1,0:T(8,128)(2,1)S(1)}, bf16[14,48,128]{2,1,0:T(8,128)(2,1)S(1)}, u32[]{:S(2)}, u32[]{:S(2)}) collective-permute-start(bf16[14,48,128]{2,1,0:T(8,128)(2,1)S(1)} %get-tuple-element.35), channel_id=1, source_target_pairs={{0,4},{1,2},{2,1},{3,7},{4,0},{5,6},{6,5},{7,3},{8,12},{9,10},{10,... | collective-permute-start | bytes 516104 | tf_op jit(solution)/shard_map/ppermute | solution.py:424
  13.4 4.6 %collective-permute-start.6 = (bf16[64,128]{1,0:T(8,128)(2,1)S(1)}, bf16[64,128]{1,0:T(8,128)(2,1)S(1)}, u32[]{:S(2)}, u32[]{:S(2)}) collective-permute-start(bf16[64,128]{1,0:T(8,128)(2,1)S(1)} %shard_map.50.refs_0_), channel_id=1, source_target_pairs={{0,3},{1,2},{2,1},{3,0},{4,7},{5,6},{6,5},{7,4},{8,11},{9,10},{10,... | collective-permute-start | bytes 49160 | tf_op jit(solution)/shard_map/ppermute | solution.py:464
  16.5 3.8 %collective-permute-start.5 = (bf16[64,128]{1,0:T(8,128)(2,1)S(1)}, bf16[64,128]{1,0:T(8,128)(2,1)S(1)}, u32[]{:S(2)}, u32[]{:S(2)}) collective-permute-start(bf16[64,128]{1,0:T(8,128)(2,1)S(1)} %shard_map.50.refs_0_), channel_id=1, source_target_pairs={{0,2},{1,3},{2,0},{3,1},{4,6},{5,7},{6,4},{7,5},{8,10},{9,11},{10,... | collective-permute-start | bytes 49160 | tf_op jit(solution)/shard_map/ppermute | solution.py:464
  16.8 3.5 %collective-permute-start.4 = (bf16[64,128]{1,0:T(8,128)(2,1)S(1)}, bf16[64,128]{1,0:T(8,128)(2,1)S(1)}, u32[]{:S(2)}, u32[]{:S(2)}) collective-permute-start(bf16[64,128]{1,0:T(8,128)(2,1)S(1)} %shard_map.50.refs_0_), channel_id=1, source_target_pairs={{0,1},{1,0},{2,3},{3,2},{4,5},{5,4},{6,7},{7,6},{8,9},{9,8},{10,11... | collective-permute-start | bytes 49160 | tf_op jit(solution)/shard_map/ppermute | solution.py:464
  20.4 6.0 %collective-permute-start.7 = (bf16[80,256]{1,0:T(8,128)(2,1)S(1)}, bf16[80,256]{1,0:T(8,128)(2,1)S(1)}, u32[]{:S(2)}, u32[]{:S(2)}) collective-permute-start(bf16[80,256]{1,0:T(8,128)(2,1)S(1)} %get-tuple-element.44.far), channel_id=1, source_target_pairs={{0,1},{1,0},{2,3},{3,2},{4,8},{5,9},{6,10},{7,11},{8,4},{9,5},{10,... | collective-permute-start | bytes 122888 | tf_op jit(solution)/shard_map/ppermute | solution.py:468
  24.4 1.2 %collective-permute-start.8 = (bf16[64,256]{1,0:T(8,128)(2,1)S(1)}, bf16[64,256]{1,0:T(8,128)(2,1)S(1)}, u32[]{:S(2)}, u32[]{:S(2)}) collective-permute-start(bf16[64,256]{1,0:T(8,128)(2,1)S(1)} %get-tuple-element.45.mate), channel_id=1, source_target_pairs={{0,4},{1,5},{2,6},{3,7},{4,0},{5,1},{6,2},{7,3},{8,12},{9,13},{10,... | collective-permute-start | bytes 98312 | tf_op jit(solution)/shard_map/ppermute | solution.py:469

commit v10 on v8

--- a/solution.py
+++ b/solution.py
@@ -105,9 +105,12 @@
 
 
 def edge_kernel(raw_far, raw_mate, turned, swap, _, send_a, send_b, got_far, got_mate):
+    rows, breadth = got_far.shape[1:]
+    beside = [raw[x].reshape(rows, breadth) for raw in (raw_far, raw_mate) for x in range(HALO)]
+    beside = mat(swap[...], jnp.concatenate(beside, 1)).astype(BF)
     for x in range(HALO):
-        got_far[x] = turn(swap[...], raw_far[x])
-        got_mate[x] = turn(swap[...], raw_mate[x])
+        got_far[x] = beside[:, x * breadth : (x + 1) * breadth]
+        got_mate[x] = beside[:, (HALO + x) * breadth : (HALO + x + 1) * breadth]
     edge = send_a.shape[1]
     even = is_even("yz")
     for x, t in enumerate(all_planes(turned, got_mate, got_far)):

time: 27.6 us -> 27.6 us (level)
  no operation moved by 1% of the time
where the time goes in v10:
time: 27.6 us; the launch traced here: 27.4 us
  starting transfers between devices  13.3 us (48%)
  Pallas kernels  7.85 us (28%)
  waiting for transfers between devices  6.2 us (22%)
    pallas_call x9, Pallas kernels, call(): pl.pallas_call(body, out_shape=[jax.ShapeDtypeStruct(s, d) for s, d in ou...  7.85 us
    ppermute x1, starting transfers between devices, per_device(): got_far = lax.ppermute(far, ('gx', 'yz'), away)  4.05 us
    ppermute x3, starting transfers between devices, per_device(): lax.ppermute(tile, 'yz', [(i, i ^ d) for i in range(yz)])  3.61 us
    ppermute x3, waiting for transfers between devices, per_device(): lax.ppermute(tile, 'yz', [(i, i ^ d) for i in range(yz)])  3.24 us
    ppermute x1, starting transfers between devices, per_device(): raw_far = lax.ppermute(send_far, ('gx', 'yz'), away)  2.67 us
    ppermute x1, starting transfers between devices, per_device(): got_a = lax.ppermute(send_a, ('gx', 'yz'), yz_pairs(gx, yz, False))  1.44 us
    ppermute x1, starting transfers between devices, per_device(): got_b = lax.ppermute(send_b, ('gx', 'yz'), yz_pairs(gx, yz, True))  1.05 us
    ppermute x1, waiting for transfers between devices, per_device(): got_a = lax.ppermute(send_a, ('gx', 'yz'), yz_pairs(gx, yz, False))  0.98 us
  transfers between devices with their start and end apart: 9, of which 6 were waited for; matrix products, arithmetic and copies ran while one was open for 0% of the time, Pallas kernels for 16%

profile of v10, /device:TPU:1, one launch (start us, length us, event | category | flops | bytes accessed | tf_op | source)
XLA Modules:
  0.0 27.4 jit_solution(17856004265667460473)
XLA Ops:
  0.0 1.0 %shard_map.46 = (bf16[3,16,8,128]{3,2,1,0:T(8,128)(2,1)S(1)}, bf16[3,16,8,128]{3,2,1,0:T(8,128)(2,1)S(1)}) custom-call(bf16[8,16,8,128]{3,2,1,0:T(8,128)(2,1)} %volume.3), custom_call_target="tpu_custom_call" | custom-call | bytes 262144 | tf_op jit(solution)/shard_map/pallas_call | solution.py:32
  1.0 2.7 %collective-permute-start = (bf16[3,16,8,128]{3,2,1,0:T(8,128)(2,1)S(1)}, bf16[3,16,8,128]{3,2,1,0:T(8,128)(2,1)S(1)}, u32[]{:S(2)}, u32[]{:S(2)}) collective-permute-start(bf16[3,16,8,128]{3,2,1,0:T(8,128)(2,1)S(1)} %get-tuple-element.29), channel_id=1, source_target_pairs={{0,1},{1,0},{2,3},{3,2},{4,8},{5,9},{6,10},{7,11},{8,4},{9,5},{10,... | collective-permute-start | bytes 294920 | tf_op jit(solution)/shard_map/ppermute | solution.py:390
  3.6 0.5 %collective-permute-start.1 = (bf16[3,16,8,128]{3,2,1,0:T(8,128)(2,1)S(1)}, bf16[3,16,8,128]{3,2,1,0:T(8,128)(2,1)S(1)}, u32[]{:S(2)}, u32[]{:S(2)}) collective-permute-start(bf16[3,16,8,128]{3,2,1,0:T(8,128)(2,1)S(1)} %get-tuple-element.30), channel_id=1, source_target_pairs={{0,4},{1,5},{2,6},{3,7},{4,0},{5,1},{6,2},{7,3},{8,12},{9,13},{10,... | collective-permute-start | bytes 294920 | tf_op jit(solution)/shard_map/ppermute | solution.py:389
  4.1 1.3 %shard_map.47 = (bf16[128,432]{1,0:T(8,128)(2,1)S(1)}, bf16[128,432]{1,0:T(8,128)(2,1)S(1)}, bf16[256,576]{1,0:T(8,128)(2,1)S(1)}, bf16[256,576]{1,0:T(8,128)(2,...) custom-call(bf16[8,16,8,128]{3,2,1,0:T(8,128)(2,1)} %volume.3, ...), custom_call_target="tpu_custom_call" | custom-call | flops 191102976 | bytes 400384 | tf_op jit(solution)/shard_map/pallas_call | solution.py:32
  5.4 0.9 %collective-permute-done.raw_far = bf16[3,16,8,128]{3,2,1,0:T(8,128)(2,1)S(1)} collective-permute-done((bf16[3,16,8,128]{3,2,1,0:T(8,128)(2,1)S(1)}, bf16[3,16,8,128]{3,2,1,0:T(8,128)(2,1)S(1)}, u32[]{:S(2)}, u32[]{:S(2)}) %collective-permute-start) | collective-permute-done | bytes 98336 | tf_op jit(solution)/shard_map/ppermute | solution.py:390
  6.3 0.2 shard_map.48
  6.5 1.4 %collective-permute-start.2 = (bf16[14,48,128]{2,1,0:T(8,128)(2,1)S(1)}, bf16[14,48,128]{2,1,0:T(8,128)(2,1)S(1)}, u32[]{:S(2)}, u32[]{:S(2)}) collective-permute-start(bf16[14,48,128]{2,1,0:T(8,128)(2,1)S(1)} %get-tuple-element.34), channel_id=1, source_target_pairs={{0,1},{1,0},{2,3},{3,2},{4,5},{5,4},{6,7},{7,6},{8,9},{9,8},{10,11... | collective-permute-start | bytes 516104 | tf_op jit(solution)/shard_map/ppermute | solution.py:427
  8.0 1.0 %collective-permute-start.3 = (bf16[14,48,128]{2,1,0:T(8,128)(2,1)S(1)}, bf16[14,48,128]{2,1,0:T(8,128)(2,1)S(1)}, u32[]{:S(2)}, u32[]{:S(2)}) collective-permute-start(bf16[14,48,128]{2,1,0:T(8,128)(2,1)S(1)} %get-tuple-element.35), channel_id=1, source_target_pairs={{0,4},{1,2},{2,1},{3,7},{4,0},{5,6},{6,5},{7,3},{8,12},{9,10},{10,... | collective-permute-start | bytes 516104 | tf_op jit(solution)/shard_map/ppermute | solution.py:426
  9.0 2.2 %shard_map.49 = (f32[2,6,128,256]{3,2,1,0:T(8,128)S(1)}, f32[256,512]{1,0:T(8,128)S(1)}, f32[288,192]{1,0:T(8,128)S(1)}) custom-call(bf16[8,128,128]{2,1,0:T(8,128)(2,1)S(1)} %get-tuple-element.31.turned, bf16[3,128,128]{2,1,0:T(8,128)(2,1)S(1)} %get-tuple-element.36.got_mate, bf16[3,128,128]{2,1,0:T(8,128)(2,1)S(1)} %get-tuple-element.37.got_far, ...), custom_call_target="tpu_custom_call" | custom-call | flops 600000000 | bytes 1417216 | tf_op jit(solution)/shard_map/pallas_call | solution.py:32
  11.2 1.0 %collective-permute-done.2.got_a = bf16[14,48,128]{2,1,0:T(8,128)(2,1)S(1)} collective-permute-done((bf16[14,48,128]{2,1,0:T(8,128)(2,1)S(1)}, bf16[14,48,128]{2,1,0:T(8,128)(2,1)S(1)}, u32[]{:S(2)}, u32[]{:S(2)}) %collective-permute-start.2) | collective-permute-done | bytes 172064 | tf_op jit(solution)/shard_map/ppermute | solution.py:427
  12.2 0.0 collective-permute-done.3.got_b
  12.2 1.3 %shard_map.50.refs_0_ = bf16[64,128]{1,0:T(8,128)(2,1)S(1)} custom-call(bf16[14,48,128]{2,1,0:T(8,128)(2,1)S(1)} %collective-permute-done.2.got_a, bf16[14,48,128]{2,1,0:T(8,128)(2,1)S(1)} %collective-permute-done.3.got_b, f32[2,6,128,256]{3,2,1,0:T(8,128)S(1)} %get-tuple-element.41.partial1, f32[256,512]{1,0:T(8,128)S(1)} %get-tuple-element.42.partial2, ...), custom_call_target="tpu_custom_call" | custom-call | flops 800000000 | bytes 3088384 | tf_op jit(solution)/shard_map/pallas_call | solution.py:32
  13.5 3.1 %collective-permute-start.6 = (bf16[64,128]{1,0:T(8,128)(2,1)S(1)}, bf16[64,128]{1,0:T(8,128)(2,1)S(1)}, u32[]{:S(2)}, u32[]{:S(2)}) collective-permute-start(bf16[64,128]{1,0:T(8,128)(2,1)S(1)} %shard_map.50.refs_0_), channel_id=1, source_target_pairs={{0,3},{1,2},{2,1},{3,0},{4,7},{5,6},{6,5},{7,4},{8,11},{9,10},{10,... | collective-permute-start | bytes 49160 | tf_op jit(solution)/shard_map/ppermute | solution.py:466
  16.5 0.3 %collective-permute-start.5 = (bf16[64,128]{1,0:T(8,128)(2,1)S(1)}, bf16[64,128]{1,0:T(8,128)(2,1)S(1)}, u32[]{:S(2)}, u32[]{:S(2)}) collective-permute-start(bf16[64,128]{1,0:T(8,128)(2,1)S(1)} %shard_map.50.refs_0_), channel_id=1, source_target_pairs={{0,2},{1,3},{2,0},{3,1},{4,6},{5,7},{6,4},{7,5},{8,10},{9,11},{10,... | collective-permute-start | bytes 49160 | tf_op jit(solution)/shard_map/ppermute | solution.py:466
  16.8 0.3 %collective-permute-start.4 = (bf16[64,128]{1,0:T(8,128)(2,1)S(1)}, bf16[64,128]{1,0:T(8,128)(2,1)S(1)}, u32[]{:S(2)}, u32[]{:S(2)}) collective-permute-start(bf16[64,128]{1,0:T(8,128)(2,1)S(1)} %shard_map.50.refs_0_), channel_id=1, source_target_pairs={{0,1},{1,0},{2,3},{3,2},{4,5},{5,4},{6,7},{7,6},{8,9},{9,8},{10,11... | collective-permute-start | bytes 49160 | tf_op jit(solution)/shard_map/ppermute | solution.py:466
  17.1 0.9 %collective-permute-done.6.refs_3_ = bf16[64,128]{1,0:T(8,128)(2,1)S(1)} collective-permute-done((bf16[64,128]{1,0:T(8,128)(2,1)S(1)}, bf16[64,128]{1,0:T(8,128)(2,1)S(1)}, u32[]{:S(2)}, u32[]{:S(2)}) %collective-permute-start.6) | collective-permute-done | bytes 16416 | tf_op jit(solution)/shard_map/ppermute | solution.py:466
  17.9 2.4 %collective-permute-done.5.refs_2_ = bf16[64,128]{1,0:T(8,128)(2,1)S(1)} collective-permute-done((bf16[64,128]{1,0:T(8,128)(2,1)S(1)}, bf16[64,128]{1,0:T(8,128)(2,1)S(1)}, u32[]{:S(2)}, u32[]{:S(2)}) %collective-permute-start.5) | collective-permute-done | bytes 16416 | tf_op jit(solution)/shard_map/ppermute | solution.py:466
  20.3 0.1 shard_map.51
  20.4 4.0 %collective-permute-start.7 = (bf16[80,256]{1,0:T(8,128)(2,1)S(1)}, bf16[80,256]{1,0:T(8,128)(2,1)S(1)}, u32[]{:S(2)}, u32[]{:S(2)}) collective-permute-start(bf16[80,256]{1,0:T(8,128)(2,1)S(1)} %get-tuple-element.44.far), channel_id=1, source_target_pairs={{0,1},{1,0},{2,3},{3,2},{4,8},{5,9},{6,10},{7,11},{8,4},{9,5},{10,... | collective-permute-start | bytes 122888 | tf_op jit(solution)/shard_map/ppermute | solution.py:470
  24.5 0.6 %shard_map.52 = (f32[32,256]{1,0:T(8,128)S(1)}, f32[32,256]{1,0:T(8,128)S(1)}, bf16[288,64]{1,0:T(8,128)(2,1)S(1)}, bf16[288,64]{1,0:T(8,128)(2,1)S(1)}) custom-call(bf16[64,256]{1,0:T(8,128)(2,1)S(1)} %get-tuple-element.45.mate, bf16[80,256]{1,0:T(8,128)(2,1)S(1)} %get-tuple-element.44.far, f32[288,192]{1,0:T(8,128)S(1)} %get-tuple-element.46.w3), custom_call_target="tpu_custom_call" | custom-call | flops 37748736 | bytes 294912 | tf_op jit(solution)/shard_map/pallas_call | solution.py:32
  25.0 0.6 %collective-permute-done.8.got_mate = bf16[64,256]{1,0:T(8,128)(2,1)S(1)} collective-permute-done((bf16[64,256]{1,0:T(8,128)(2,1)S(1)}, bf16[64,256]{1,0:T(8,128)(2,1)S(1)}, u32[]{:S(2)}, u32[]{:S(2)}) %collective-permute-start.8) | collective-permute-done | bytes 32800 | tf_op jit(solution)/shard_map/ppermute | solution.py:471
  25.7 0.3 %shard_map.53 = (bf16[32,2,256]{2,1,0:T(2,128)(2,1)}, f32[32,256]{1,0:T(8,128)S(1)}) custom-call(f32[32,256]{1,0:T(8,128)S(1)} %get-tuple-element.48.beside_mate, f32[32,256]{1,0:T(8,128)S(1)} %get-tuple-element.49.beside_far, bf16[288,64]{1,0:T(8,128)(2,1)S(1)} %get-tuple-element.50.w_mate, bf16[64,256]{1,0:T(8,128)(2,1)S(1)} %collective-permute-done.8.got_mate), custom_call_target="tpu_custom_call" | custom-call | tf_op jit(solution)/shard_map/pallas_call | solution.py:32
  26.0 0.4 %collective-permute-done.7.got_far = bf16[80,256]{1,0:T(8,128)(2,1)S(1)} collective-permute-done((bf16[80,256]{1,0:T(8,128)(2,1)S(1)}, bf16[80,256]{1,0:T(8,128)(2,1)S(1)}, u32[]{:S(2)}, u32[]{:S(2)}) %collective-permute-start.7) | collective-permute-done | bytes 40992 | tf_op jit(solution)/shard_map/ppermute | solution.py:470
  26.4 1.0 %shard_map.54 = bf16[32,2,256]{2,1,0:T(2,128)(2,1)} custom-call(bf16[80,256]{1,0:T(8,128)(2,1)S(1)} %collective-permute-done.7.got_far, bf16[288,64]{1,0:T(8,128)(2,1)S(1)} %get-tuple-element.47.w_far, f32[32,256]{1,0:T(8,128)S(1)} %get-tuple-element.51.ready, f32[32,256]{1,0:T(8,128)S(1)} %get-tuple-element.49.beside_far, ...), custom_call_target="tpu_custom_call", output_to_operand_aliasing={{}: (4, {})} | custom-call | flops 9437184 | bytes 176128 | tf_op jit(solution)/shard_map/pallas_call | solution.py:32
  (3 shorter events, 0.0 us)
Async XLA Ops:
  1.0 5.3 %collective-permute-start = (bf16[3,16,8,128]{3,2,1,0:T(8,128)(2,1)S(1)}, bf16[3,16,8,128]{3,2,1,0:T(8,128)(2,1)S(1)}, u32[]{:S(2)}, u32[]{:S(2)}) collective-permute-start(bf16[3,16,8,128]{3,2,1,0:T(8,128)(2,1)S(1)} %get-tuple-element.29), channel_id=1, source_target_pairs={{0,1},{1,0},{2,3},{3,2},{4,8},{5,9},{6,10},{7,11},{8,4},{9,5},{10,... | collective-permute-start | bytes 294920 | tf_op jit(solution)/shard_map/ppermute | solution.py:390
  3.6 2.7 %collective-permute-start.1 = (bf16[3,16,8,128]{3,2,1,0:T(8,128)(2,1)S(1)}, bf16[3,16,8,128]{3,2,1,0:T(8,128)(2,1)S(1)}, u32[]{:S(2)}, u32[]{:S(2)}) collective-permute-start(bf16[3,16,8,128]{3,2,1,0:T(8,128)(2,1)S(1)} %get-tuple-element.30), channel_id=1, source_target_pairs={{0,4},{1,5},{2,6},{3,7},{4,0},{5,1},{6,2},{7,3},{8,12},{9,13},{10,... | collective-permute-start | bytes 294920 | tf_op jit(solution)/shard_map/ppermute | solution.py:389
  6.5 5.6 %collective-permute-start.2 = (bf16[14,48,128]{2,1,0:T(8,128)(2,1)S(1)}, bf16[14,48,128]{2,1,0:T(8,128)(2,1)S(1)}, u32[]{:S(2)}, u32[]{:S(2)}) collective-permute-start(bf16[14,48,128]{2,1,0:T(8,128)(2,1)S(1)} %get-tuple-element.34), channel_id=1, source_target_pairs={{0,1},{1,0},{2,3},{3,2},{4,5},{5,4},{6,7},{7,6},{8,9},{9,8},{10,11... | collective-permute-start | bytes 516104 | tf_op jit(solution)/shard_map/ppermute | solution.py:427
  8.0 4.2 %collective-permute-start.3 = (bf16[14,48,128]{2,1,0:T(8,128)(2,1)S(1)}, bf16[14,48,128]{2,1,0:T(8,128)(2,1)S(1)}, u32[]{:S(2)}, u32[]{:S(2)}) collective-permute-start(bf16[14,48,128]{2,1,0:T(8,128)(2,1)S(1)} %get-tuple-element.35), channel_id=1, source_target_pairs={{0,4},{1,2},{2,1},{3,7},{4,0},{5,6},{6,5},{7,3},{8,12},{9,10},{10,... | collective-permute-start | bytes 516104 | tf_op jit(solution)/shard_map/ppermute | solution.py:426
  13.5 4.5 %collective-permute-start.6 = (bf16[64,128]{1,0:T(8,128)(2,1)S(1)}, bf16[64,128]{1,0:T(8,128)(2,1)S(1)}, u32[]{:S(2)}, u32[]{:S(2)}) collective-permute-start(bf16[64,128]{1,0:T(8,128)(2,1)S(1)} %shard_map.50.refs_0_), channel_id=1, source_target_pairs={{0,3},{1,2},{2,1},{3,0},{4,7},{5,6},{6,5},{7,4},{8,11},{9,10},{10,... | collective-permute-start | bytes 49160 | tf_op jit(solution)/shard_map/ppermute | solution.py:466
  16.5 3.8 %collective-permute-start.5 = (bf16[64,128]{1,0:T(8,128)(2,1)S(1)}, bf16[64,128]{1,0:T(8,128)(2,1)S(1)}, u32[]{:S(2)}, u32[]{:S(2)}) collective-permute-start(bf16[64,128]{1,0:T(8,128)(2,1)S(1)} %shard_map.50.refs_0_), channel_id=1, source_target_pairs={{0,2},{1,3},{2,0},{3,1},{4,6},{5,7},{6,4},{7,5},{8,10},{9,11},{10,... | collective-permute-start | bytes 49160 | tf_op jit(solution)/shard_map/ppermute | solution.py:466
  16.8 3.5 %collective-permute-start.4 = (bf16[64,128]{1,0:T(8,128)(2,1)S(1)}, bf16[64,128]{1,0:T(8,128)(2,1)S(1)}, u32[]{:S(2)}, u32[]{:S(2)}) collective-permute-start(bf16[64,128]{1,0:T(8,128)(2,1)S(1)} %shard_map.50.refs_0_), channel_id=1, source_target_pairs={{0,1},{1,0},{2,3},{3,2},{4,5},{5,4},{6,7},{7,6},{8,9},{9,8},{10,11... | collective-permute-start | bytes 49160 | tf_op jit(solution)/shard_map/ppermute | solution.py:466
  20.4 6.0 %collective-permute-start.7 = (bf16[80,256]{1,0:T(8,128)(2,1)S(1)}, bf16[80,256]{1,0:T(8,128)(2,1)S(1)}, u32[]{:S(2)}, u32[]{:S(2)}) collective-permute-start(bf16[80,256]{1,0:T(8,128)(2,1)S(1)} %get-tuple-element.44.far), channel_id=1, source_target_pairs={{0,1},{1,0},{2,3},{3,2},{4,8},{5,9},{6,10},{7,11},{8,4},{9,5},{10,... | collective-permute-start | bytes 122888 | tf_op jit(solution)/shard_map/ppermute | solution.py:470
  24.5 1.2 %collective-permute-start.8 = (bf16[64,256]{1,0:T(8,128)(2,1)S(1)}, bf16[64,256]{1,0:T(8,128)(2,1)S(1)}, u32[]{:S(2)}, u32[]{:S(2)}) collective-permute-start(bf16[64,256]{1,0:T(8,128)(2,1)S(1)} %get-tuple-element.45.mate), channel_id=1, source_target_pairs={{0,4},{1,5},{2,6},{3,7},{4,0},{5,1},{6,2},{7,3},{8,12},{9,13},{10,... | collective-permute-start | bytes 98312 | tf_op jit(solution)/shard_map/ppermute | solution.py:471

commit v11 on v9

--- a/solution.py
+++ b/solution.py
@@ -105,9 +105,12 @@
 
 
 def edge_kernel(raw_far, raw_mate, turned, swap, _, send_a, send_b, got_far, got_mate):
+    rows, breadth = got_far.shape[1:]
+    beside = [raw[x].reshape(rows, breadth) for raw in (raw_far, raw_mate) for x in range(HALO)]
+    beside = mat(swap[...], jnp.concatenate(beside, 1)).astype(BF)
     for x in range(HALO):
-        got_far[x] = turn(swap[...], raw_far[x])
-        got_mate[x] = turn(swap[...], raw_mate[x])
+        got_far[x] = beside[:, x * breadth : (x + 1) * breadth]
+        got_mate[x] = beside[:, (HALO + x) * breadth : (HALO + x + 1) * breadth]
     edge = send_a.shape[1]
     even = is_even("yz")
     for x, t in enumerate(all_planes(turned, got_mate, got_far)):

time: 27.6 us -> 27.6 us (level)
  no operation moved by 1% of the time
where the time goes in v11:
time: 27.6 us; the launch traced here: 27.4 us
  starting transfers between devices  13.3 us (48%)
  Pallas kernels  7.85 us (28%)
  waiting for transfers between devices  6.21 us (22%)
    pallas_call x9, Pallas kernels, call(): pl.pallas_call(body, out_shape=[jax.ShapeDtypeStruct(s, d) for s, d in ou...  7.85 us
    ppermute x1, starting transfers between devices, per_device(): got_far = lax.ppermute(far, ('gx', 'yz'), away)  4.05 us
    ppermute x3, starting transfers between devices, per_device(): lax.ppermute(tile, 'yz', [(i, i ^ d) for i in range(yz)])  3.61 us
    ppermute x3, waiting for transfers between devices, per_device(): lax.ppermute(tile, 'yz', [(i, i ^ d) for i in range(yz)])  3.25 us
    ppermute x1, starting transfers between devices, per_device(): raw_far = lax.ppermute(send_far, ('gx', 'yz'), away)  2.67 us
    ppermute x1, starting transfers between devices, per_device(): got_a = lax.ppermute(send_a, ('gx', 'yz'), yz_pairs(gx, yz, False))  1.44 us
    ppermute x1, starting transfers between devices, per_device(): got_b = lax.ppermute(send_b, ('gx', 'yz'), yz_pairs(gx, yz, True))  1.05 us
    ppermute x1, waiting for transfers between devices, per_device(): got_a = lax.ppermute(send_a, ('gx', 'yz'), yz_pairs(gx, yz, False))  0.98 us
  transfers between devices with their start and end apart: 9, of which 6 were waited for; matrix products, arithmetic and copies ran while one was open for 0% of the time, Pallas kernels for 16%

profile of v11, /device:TPU:1, one launch (start us, length us, event | category | flops | bytes accessed | tf_op | source)
XLA Modules:
  0.0 27.4 jit_solution(14102030986062820702)
XLA Ops:
  0.0 1.0 %shard_map.46 = (bf16[3,16,8,128]{3,2,1,0:T(8,128)(2,1)S(1)}, bf16[3,16,8,128]{3,2,1,0:T(8,128)(2,1)S(1)}) custom-call(bf16[8,16,8,128]{3,2,1,0:T(8,128)(2,1)} %volume.3), custom_call_target="tpu_custom_call" | custom-call | bytes 262144 | tf_op jit(solution)/shard_map/pallas_call | solution.py:32
  1.0 2.7 %collective-permute-start = (bf16[3,16,8,128]{3,2,1,0:T(8,128)(2,1)S(1)}, bf16[3,16,8,128]{3,2,1,0:T(8,128)(2,1)S(1)}, u32[]{:S(2)}, u32[]{:S(2)}) collective-permute-start(bf16[3,16,8,128]{3,2,1,0:T(8,128)(2,1)S(1)} %get-tuple-element.29), channel_id=1, source_target_pairs={{0,1},{1,0},{2,3},{3,2},{4,8},{5,9},{6,10},{7,11},{8,4},{9,5},{10,... | collective-permute-start | bytes 294920 | tf_op jit(solution)/shard_map/ppermute | solution.py:391
  3.6 0.5 %collective-permute-start.1 = (bf16[3,16,8,128]{3,2,1,0:T(8,128)(2,1)S(1)}, bf16[3,16,8,128]{3,2,1,0:T(8,128)(2,1)S(1)}, u32[]{:S(2)}, u32[]{:S(2)}) collective-permute-start(bf16[3,16,8,128]{3,2,1,0:T(8,128)(2,1)S(1)} %get-tuple-element.30), channel_id=1, source_target_pairs={{0,4},{1,5},{2,6},{3,7},{4,0},{5,1},{6,2},{7,3},{8,12},{9,13},{10,... | collective-permute-start | bytes 294920 | tf_op jit(solution)/shard_map/ppermute | solution.py:390
  4.1 1.3 %shard_map.47 = (bf16[128,432]{1,0:T(8,128)(2,1)S(1)}, bf16[128,432]{1,0:T(8,128)(2,1)S(1)}, bf16[256,576]{1,0:T(8,128)(2,1)S(1)}, bf16[256,576]{1,0:T(8,128)(2,...) custom-call(bf16[8,16,8,128]{3,2,1,0:T(8,128)(2,1)} %volume.3, ...), custom_call_target="tpu_custom_call" | custom-call | flops 191102976 | bytes 400384 | tf_op jit(solution)/shard_map/pallas_call | solution.py:32
  5.4 0.9 %collective-permute-done.raw_far = bf16[3,16,8,128]{3,2,1,0:T(8,128)(2,1)S(1)} collective-permute-done((bf16[3,16,8,128]{3,2,1,0:T(8,128)(2,1)S(1)}, bf16[3,16,8,128]{3,2,1,0:T(8,128)(2,1)S(1)}, u32[]{:S(2)}, u32[]{:S(2)}) %collective-permute-start) | collective-permute-done | bytes 98336 | tf_op jit(solution)/shard_map/ppermute | solution.py:391
  6.3 0.2 shard_map.48
  6.5 1.4 %collective-permute-start.2 = (bf16[14,48,128]{2,1,0:T(8,128)(2,1)S(1)}, bf16[14,48,128]{2,1,0:T(8,128)(2,1)S(1)}, u32[]{:S(2)}, u32[]{:S(2)}) collective-permute-start(bf16[14,48,128]{2,1,0:T(8,128)(2,1)S(1)} %get-tuple-element.34), channel_id=1, source_target_pairs={{0,1},{1,0},{2,3},{3,2},{4,5},{5,4},{6,7},{7,6},{8,9},{9,8},{10,11... | collective-permute-start | bytes 516104 | tf_op jit(solution)/shard_map/ppermute | solution.py:428
  8.0 1.0 %collective-permute-start.3 = (bf16[14,48,128]{2,1,0:T(8,128)(2,1)S(1)}, bf16[14,48,128]{2,1,0:T(8,128)(2,1)S(1)}, u32[]{:S(2)}, u32[]{:S(2)}) collective-permute-start(bf16[14,48,128]{2,1,0:T(8,128)(2,1)S(1)} %get-tuple-element.35), channel_id=1, source_target_pairs={{0,4},{1,2},{2,1},{3,7},{4,0},{5,6},{6,5},{7,3},{8,12},{9,10},{10,... | collective-permute-start | bytes 516104 | tf_op jit(solution)/shard_map/ppermute | solution.py:427
  9.0 2.2 %shard_map.49 = (f32[2,6,96,256]{3,2,1,0:T(8,128)S(1)}, f32[256,512]{1,0:T(8,128)S(1)}, f32[288,192]{1,0:T(8,128)S(1)}) custom-call(bf16[8,128,128]{2,1,0:T(8,128)(2,1)S(1)} %get-tuple-element.31.turned, bf16[3,128,128]{2,1,0:T(8,128)(2,1)S(1)} %get-tuple-element.36.got_mate, bf16[3,128,128]{2,1,0:T(8,128)(2,1)S(1)} %get-tuple-element.37.got_far, ...), custom_call_target="tpu_custom_call" | custom-call | flops 600000000 | bytes 1417216 | tf_op jit(solution)/shard_map/pallas_call | solution.py:32
  11.2 1.0 %collective-permute-done.2.got_a = bf16[14,48,128]{2,1,0:T(8,128)(2,1)S(1)} collective-permute-done((bf16[14,48,128]{2,1,0:T(8,128)(2,1)S(1)}, bf16[14,48,128]{2,1,0:T(8,128)(2,1)S(1)}, u32[]{:S(2)}, u32[]{:S(2)}) %collective-permute-start.2) | collective-permute-done | bytes 172064 | tf_op jit(solution)/shard_map/ppermute | solution.py:428
  12.2 0.0 collective-permute-done.3.got_b
  12.2 1.3 %shard_map.50.refs_0_ = bf16[64,128]{1,0:T(8,128)(2,1)S(1)} custom-call(bf16[14,48,128]{2,1,0:T(8,128)(2,1)S(1)} %collective-permute-done.2.got_a, bf16[14,48,128]{2,1,0:T(8,128)(2,1)S(1)} %collective-permute-done.3.got_b, f32[2,6,96,256]{3,2,1,0:T(8,128)S(1)} %get-tuple-element.41.partial1, f32[256,512]{1,0:T(8,128)S(1)} %get-tuple-element.42.partial2, ...), custom_call_target="tpu_custom_call" | custom-call | flops 800000000 | bytes 2695168 | tf_op jit(solution)/shard_map/pallas_call | solution.py:32
  13.4 3.1 %collective-permute-start.6 = (bf16[64,128]{1,0:T(8,128)(2,1)S(1)}, bf16[64,128]{1,0:T(8,128)(2,1)S(1)}, u32[]{:S(2)}, u32[]{:S(2)}) collective-permute-start(bf16[64,128]{1,0:T(8,128)(2,1)S(1)} %shard_map.50.refs_0_), channel_id=1, source_target_pairs={{0,3},{1,2},{2,1},{3,0},{4,7},{5,6},{6,5},{7,4},{8,11},{9,10},{10,... | collective-permute-start | bytes 49160 | tf_op jit(solution)/shard_map/ppermute | solution.py:467
  16.5 0.3 %collective-permute-start.5 = (bf16[64,128]{1,0:T(8,128)(2,1)S(1)}, bf16[64,128]{1,0:T(8,128)(2,1)S(1)}, u32[]{:S(2)}, u32[]{:S(2)}) collective-permute-start(bf16[64,128]{1,0:T(8,128)(2,1)S(1)} %shard_map.50.refs_0_), channel_id=1, source_target_pairs={{0,2},{1,3},{2,0},{3,1},{4,6},{5,7},{6,4},{7,5},{8,10},{9,11},{10,... | collective-permute-start | bytes 49160 | tf_op jit(solution)/shard_map/ppermute | solution.py:467
  16.8 0.3 %collective-permute-start.4 = (bf16[64,128]{1,0:T(8,128)(2,1)S(1)}, bf16[64,128]{1,0:T(8,128)(2,1)S(1)}, u32[]{:S(2)}, u32[]{:S(2)}) collective-permute-start(bf16[64,128]{1,0:T(8,128)(2,1)S(1)} %shard_map.50.refs_0_), channel_id=1, source_target_pairs={{0,1},{1,0},{2,3},{3,2},{4,5},{5,4},{6,7},{7,6},{8,9},{9,8},{10,11... | collective-permute-start | bytes 49160 | tf_op jit(solution)/shard_map/ppermute | solution.py:467
  17.1 0.9 %collective-permute-done.6.refs_3_ = bf16[64,128]{1,0:T(8,128)(2,1)S(1)} collective-permute-done((bf16[64,128]{1,0:T(8,128)(2,1)S(1)}, bf16[64,128]{1,0:T(8,128)(2,1)S(1)}, u32[]{:S(2)}, u32[]{:S(2)}) %collective-permute-start.6) | collective-permute-done | bytes 16416 | tf_op jit(solution)/shard_map/ppermute | solution.py:467
  17.9 2.4 %collective-permute-done.5.refs_2_ = bf16[64,128]{1,0:T(8,128)(2,1)S(1)} collective-permute-done((bf16[64,128]{1,0:T(8,128)(2,1)S(1)}, bf16[64,128]{1,0:T(8,128)(2,1)S(1)}, u32[]{:S(2)}, u32[]{:S(2)}) %collective-permute-start.5) | collective-permute-done | bytes 16416 | tf_op jit(solution)/shard_map/ppermute | solution.py:467
  20.3 0.1 shard_map.51
  20.4 4.0 %collective-permute-start.7 = (bf16[80,256]{1,0:T(8,128)(2,1)S(1)}, bf16[80,256]{1,0:T(8,128)(2,1)S(1)}, u32[]{:S(2)}, u32[]{:S(2)}) collective-permute-start(bf16[80,256]{1,0:T(8,128)(2,1)S(1)} %get-tuple-element.44.far), channel_id=1, source_target_pairs={{0,1},{1,0},{2,3},{3,2},{4,8},{5,9},{6,10},{7,11},{8,4},{9,5},{10,... | collective-permute-start | bytes 122888 | tf_op jit(solution)/shard_map/ppermute | solution.py:471
  24.5 0.6 %shard_map.52 = (f32[32,256]{1,0:T(8,128)S(1)}, f32[32,256]{1,0:T(8,128)S(1)}, bf16[288,64]{1,0:T(8,128)(2,1)S(1)}, bf16[288,64]{1,0:T(8,128)(2,1)S(1)}) custom-call(bf16[64,256]{1,0:T(8,128)(2,1)S(1)} %get-tuple-element.45.mate, bf16[80,256]{1,0:T(8,128)(2,1)S(1)} %get-tuple-element.44.far, f32[288,192]{1,0:T(8,128)S(1)} %get-tuple-element.46.w3), custom_call_target="tpu_custom_call" | custom-call | flops 37748736 | bytes 294912 | tf_op jit(solution)/shard_map/pallas_call | solution.py:32
  25.0 0.6 %collective-permute-done.8.got_mate = bf16[64,256]{1,0:T(8,128)(2,1)S(1)} collective-permute-done((bf16[64,256]{1,0:T(8,128)(2,1)S(1)}, bf16[64,256]{1,0:T(8,128)(2,1)S(1)}, u32[]{:S(2)}, u32[]{:S(2)}) %collective-permute-start.8) | collective-permute-done | bytes 32800 | tf_op jit(solution)/shard_map/ppermute | solution.py:472
  25.7 0.3 %shard_map.53 = (bf16[32,2,256]{2,1,0:T(2,128)(2,1)}, f32[32,256]{1,0:T(8,128)S(1)}) custom-call(f32[32,256]{1,0:T(8,128)S(1)} %get-tuple-element.48.beside_mate, f32[32,256]{1,0:T(8,128)S(1)} %get-tuple-element.49.beside_far, bf16[288,64]{1,0:T(8,128)(2,1)S(1)} %get-tuple-element.50.w_mate, bf16[64,256]{1,0:T(8,128)(2,1)S(1)} %collective-permute-done.8.got_mate), custom_call_target="tpu_custom_call" | custom-call | tf_op jit(solution)/shard_map/pallas_call | solution.py:32
  26.0 0.4 %collective-permute-done.7.got_far = bf16[80,256]{1,0:T(8,128)(2,1)S(1)} collective-permute-done((bf16[80,256]{1,0:T(8,128)(2,1)S(1)}, bf16[80,256]{1,0:T(8,128)(2,1)S(1)}, u32[]{:S(2)}, u32[]{:S(2)}) %collective-permute-start.7) | collective-permute-done | bytes 40992 | tf_op jit(solution)/shard_map/ppermute | solution.py:471
  26.4 1.0 %shard_map.54 = bf16[32,2,256]{2,1,0:T(2,128)(2,1)} custom-call(bf16[80,256]{1,0:T(8,128)(2,1)S(1)} %collective-permute-done.7.got_far, bf16[288,64]{1,0:T(8,128)(2,1)S(1)} %get-tuple-element.47.w_far, f32[32,256]{1,0:T(8,128)S(1)} %get-tuple-element.51.ready, f32[32,256]{1,0:T(8,128)S(1)} %get-tuple-element.49.beside_far, ...), custom_call_target="tpu_custom_call", output_to_operand_aliasing={{}: (4, {})} | custom-call | flops 9437184 | bytes 176128 | tf_op jit(solution)/shard_map/pallas_call | solution.py:32
  (3 shorter events, 0.0 us)
Async XLA Ops:
  1.0 5.3 %collective-permute-start = (bf16[3,16,8,128]{3,2,1,0:T(8,128)(2,1)S(1)}, bf16[3,16,8,128]{3,2,1,0:T(8,128)(2,1)S(1)}, u32[]{:S(2)}, u32[]{:S(2)}) collective-permute-start(bf16[3,16,8,128]{3,2,1,0:T(8,128)(2,1)S(1)} %get-tuple-element.29), channel_id=1, source_target_pairs={{0,1},{1,0},{2,3},{3,2},{4,8},{5,9},{6,10},{7,11},{8,4},{9,5},{10,... | collective-permute-start | bytes 294920 | tf_op jit(solution)/shard_map/ppermute | solution.py:391
  3.6 2.7 %collective-permute-start.1 = (bf16[3,16,8,128]{3,2,1,0:T(8,128)(2,1)S(1)}, bf16[3,16,8,128]{3,2,1,0:T(8,128)(2,1)S(1)}, u32[]{:S(2)}, u32[]{:S(2)}) collective-permute-start(bf16[3,16,8,128]{3,2,1,0:T(8,128)(2,1)S(1)} %get-tuple-element.30), channel_id=1, source_target_pairs={{0,4},{1,5},{2,6},{3,7},{4,0},{5,1},{6,2},{7,3},{8,12},{9,13},{10,... | collective-permute-start | bytes 294920 | tf_op jit(solution)/shard_map/ppermute | solution.py:390
  6.5 5.6 %collective-permute-start.2 = (bf16[14,48,128]{2,1,0:T(8,128)(2,1)S(1)}, bf16[14,48,128]{2,1,0:T(8,128)(2,1)S(1)}, u32[]{:S(2)}, u32[]{:S(2)}) collective-permute-start(bf16[14,48,128]{2,1,0:T(8,128)(2,1)S(1)} %get-tuple-element.34), channel_id=1, source_target_pairs={{0,1},{1,0},{2,3},{3,2},{4,5},{5,4},{6,7},{7,6},{8,9},{9,8},{10,11... | collective-permute-start | bytes 516104 | tf_op jit(solution)/shard_map/ppermute | solution.py:428
  8.0 4.2 %collective-permute-start.3 = (bf16[14,48,128]{2,1,0:T(8,128)(2,1)S(1)}, bf16[14,48,128]{2,1,0:T(8,128)(2,1)S(1)}, u32[]{:S(2)}, u32[]{:S(2)}) collective-permute-start(bf16[14,48,128]{2,1,0:T(8,128)(2,1)S(1)} %get-tuple-element.35), channel_id=1, source_target_pairs={{0,4},{1,2},{2,1},{3,7},{4,0},{5,6},{6,5},{7,3},{8,12},{9,10},{10,... | collective-permute-start | bytes 516104 | tf_op jit(solution)/shard_map/ppermute | solution.py:427
  13.4 4.5 %collective-permute-start.6 = (bf16[64,128]{1,0:T(8,128)(2,1)S(1)}, bf16[64,128]{1,0:T(8,128)(2,1)S(1)}, u32[]{:S(2)}, u32[]{:S(2)}) collective-permute-start(bf16[64,128]{1,0:T(8,128)(2,1)S(1)} %shard_map.50.refs_0_), channel_id=1, source_target_pairs={{0,3},{1,2},{2,1},{3,0},{4,7},{5,6},{6,5},{7,4},{8,11},{9,10},{10,... | collective-permute-start | bytes 49160 | tf_op jit(solution)/shard_map/ppermute | solution.py:467
  16.5 3.8 %collective-permute-start.5 = (bf16[64,128]{1,0:T(8,128)(2,1)S(1)}, bf16[64,128]{1,0:T(8,128)(2,1)S(1)}, u32[]{:S(2)}, u32[]{:S(2)}) collective-permute-start(bf16[64,128]{1,0:T(8,128)(2,1)S(1)} %shard_map.50.refs_0_), channel_id=1, source_target_pairs={{0,2},{1,3},{2,0},{3,1},{4,6},{5,7},{6,4},{7,5},{8,10},{9,11},{10,... | collective-permute-start | bytes 49160 | tf_op jit(solution)/shard_map/ppermute | solution.py:467
  16.8 3.5 %collective-permute-start.4 = (bf16[64,128]{1,0:T(8,128)(2,1)S(1)}, bf16[64,128]{1,0:T(8,128)(2,1)S(1)}, u32[]{:S(2)}, u32[]{:S(2)}) collective-permute-start(bf16[64,128]{1,0:T(8,128)(2,1)S(1)} %shard_map.50.refs_0_), channel_id=1, source_target_pairs={{0,1},{1,0},{2,3},{3,2},{4,5},{5,4},{6,7},{7,6},{8,9},{9,8},{10,11... | collective-permute-start | bytes 49160 | tf_op jit(solution)/shard_map/ppermute | solution.py:467
  20.4 6.0 %collective-permute-start.7 = (bf16[80,256]{1,0:T(8,128)(2,1)S(1)}, bf16[80,256]{1,0:T(8,128)(2,1)S(1)}, u32[]{:S(2)}, u32[]{:S(2)}) collective-permute-start(bf16[80,256]{1,0:T(8,128)(2,1)S(1)} %get-tuple-element.44.far), channel_id=1, source_target_pairs={{0,1},{1,0},{2,3},{3,2},{4,8},{5,9},{6,10},{7,11},{8,4},{9,5},{10,... | collective-permute-start | bytes 122888 | tf_op jit(solution)/shard_map/ppermute | solution.py:471
  24.5 1.2 %collective-permute-start.8 = (bf16[64,256]{1,0:T(8,128)(2,1)S(1)}, bf16[64,256]{1,0:T(8,128)(2,1)S(1)}, u32[]{:S(2)}, u32[]{:S(2)}) collective-permute-start(bf16[64,256]{1,0:T(8,128)(2,1)S(1)} %get-tuple-element.45.mate), channel_id=1, source_target_pairs={{0,4},{1,5},{2,6},{3,7},{4,0},{5,1},{6,2},{7,3},{8,12},{9,13},{10,... | collective-permute-start | bytes 98312 | tf_op jit(solution)/shard_map/ppermute | solution.py:472
